TPU v7x, 32 devices: a whole 2x2x4 slice. The times are simulated.
32 devices in a mesh: docs: 8 (over z, core), protos: 4 (over y, x).
Axes of the slice: x: 2, y: 2, z: 4, core: 2. Of those that a mesh axis runs over, the one named last changes fastest.
Arguments:
- embeddings: bfloat16 [8192, 512], P('docs'), may hold values from -12.5 to 12.5
- prototypes: bfloat16 [65536, 512], P('protos'), may hold values from -4 to 4
Outputs:
- new_prototypes: bfloat16 [65536, 512], P(('protos', 'docs'))
- column_potential: float32 [65536], P('protos')
- row_potential: float32 [8192], P('docs')
All inputs are finite; a program needn't handle non-finite values.
Results may differ from a plain program's by a relative error of at most 0.0035.
Values may be sent and summed in bfloat16 or wider, within the bound.
No kernel may reach another device: no remote copies, remote signals or barrier semaphores. Data moves between devices by JAX's collectives and lax.ppermute only.
A program may use at most 256 MiB of HBM per device.

v0:
```python
import math

import jax
import jax.numpy as jnp
from jax import lax
from jax.sharding import PartitionSpec as P

SWEEPS = 2


def on_device(embeddings, prototypes):
    local_docs = embeddings.shape[0]
    local_protos = prototypes.shape[0]
    total_docs = local_docs * lax.axis_size("docs")
    total_protos = local_protos * lax.axis_size("protos")
    logit_gain = 4.0 / math.sqrt(embeddings.shape[1])
    scores = (
        lax.dot_general(
            embeddings, prototypes, (((1,), (1,)), ((), ())), preferred_element_type=jnp.float32
        )
        * logit_gain
    )
    row_peak = lax.pmax(jnp.max(scores, axis=1), "protos")
    numerators = jnp.exp(scores - row_peak[:, None])
    row_total = lax.psum(jnp.sum(numerators, axis=1), "protos")
    rescale = 1.0
    row_scale = 1.0 / row_total
    row_weight = rescale * row_scale
    col_scale = jnp.zeros((local_protos,), jnp.float32)
    for sweep_index in range(SWEEPS):
        col_local = jnp.dot(
            row_weight,
            numerators,
            precision=lax.Precision.HIGHEST,
            preferred_element_type=jnp.float32,
        )
        col_total = lax.psum(col_local, "docs")
        col_scale = 1.0 / (total_protos * col_total)
        row_local = rescale * jnp.dot(
            numerators,
            col_scale,
            precision=lax.Precision.HIGHEST,
            preferred_element_type=jnp.float32,
        )
        row_sum = lax.psum(row_local, "protos")
        row_scale = 1.0 / (total_docs * row_sum)
        row_weight = rescale * row_scale
    column_potential = jnp.log(total_docs * col_scale)
    row_potential = jnp.log(row_scale * row_total)
    assignment = (numerators * (total_docs * row_weight)[:, None] * col_scale[None, :]).astype(
        jnp.bfloat16
    )
    summed = lax.psum_scatter(
        lax.dot_general(
            assignment, embeddings, (((0,), (0,)), ((), ())), preferred_element_type=jnp.float32
        ),
        "docs",
        scatter_dimension=0,
        tiled=True,
    )
    new_prototypes = (
        summed * lax.rsqrt(jnp.mean(summed * summed, axis=1, keepdims=True) + 1e-06)
    ).astype(jnp.bfloat16)
    return (new_prototypes, column_potential, row_potential)


def solution(mesh):
    placed = (P("docs", None), P("protos", None))
    return jax.shard_map(
        on_device,
        mesh=mesh,
        in_specs=placed,
        out_specs=(P(("protos", "docs"), None), P("protos"), P("docs")),
        check_vma=False,
    )
```

profile of v0, /device:TPU:0, one launch (start us, length us, event | category | flops | bytes accessed | tf_op | source)
XLA Modules:
  0.0 816.1 jit_solution(17064669797004932549)
XLA Ops:
  7.2 0.0 copy-start
  7.2 0.0 all-reduce.3.cloned.1.call-start
  7.2 1.2 copy-done
  8.4 31.5 %multiply_reduce_fusion = (f32[1024]{0:T(1024)S(1)}, f32[1024,16384]{1,0:T(8,128)}) fusion(bf16[1024,512]{1,0:T(8,128)(2,1)S(1)} %copy-done, bf16[16384,512]{1,0:T(8,128)(2,1)} %param.3), kind=kOutput, calls=%fused_computation.2 | convolution fusion | flops 17213423616 | bytes 84938752 | tf_op jit(solution)/shard_map/dot_general | solution.py:18
  39.9 11.3 %pmax.7 = f32[1024]{0:T(1024)S(1)} all-reduce(f32[1024]{0:T(1024)S(1)} %get-tuple-element.7), channel_id=1, replica_groups=mesh['docs'=8,'protos'=4] {'protos'}, use_global_device_ids=true, to_apply=%region_1.0 | all-reduce | flops 1024 | bytes 8192 | tf_op jit(solution)/shard_map/pmax | solution.py:23
  51.2 21.2 %fusion.7 = f32[1024]{0:T(1024)S(1)} fusion(f32[1024]{0:T(1024)S(1)} %pmax.7, f32[1024,16384]{1,0:T(8,128)} %get-tuple-element.8), kind=kLoop, calls=%fused_computation.21 | loop fusion | flops 50330624 | bytes 67117056 | tf_op jit(solution)/shard_map/reduce_sum | solution.py:25
  72.4 8.1 psum.35
  80.6 46.4 %fusion.6 = f32[1,16384]{1,0:T(1,128)} fusion(f32[1024,1]{0,1:T(1,128)S(1)} %bitcast.20, f32[1024,16384]{1,0:T(8,128)} %get-tuple-element.8, f32[1024]{0:T(1024)S(1)} %pmax.7), kind=kOutput, calls=%fused_computation.20 | convolution fusion | flops 234881024 | bytes 67182592 | tf_op jit(solution)/shard_map/dot_general | solution.py:31
  127.0 0.0 all-reduce.3.cloned.1.call-update
  127.0 0.3 all-reduce.5.cloned.1.call-start
  127.3 53.8 %all-reduce.3.cloned.1.call-done = f32[16384]{0:T(1024)} async-done(((f32[16384]{0:T(1024)}), f32[16384]{0:T(1024)}) %all-reduce.3.cloned.1.call-update) | async-done | bytes 65552 | tf_op jit(solution)/shard_map/psum | solution.py:37
  181.1 0.9 multiply_divide_fusion.1
  181.9 69.4 %fusion.5 = f32[1,1024]{1,0:T(1,128)S(1)} fusion(f32[16384,1]{0,1:T(1,128)S(1)} %bitcast.16, f32[1024,16384]{1,0:T(8,128)} %get-tuple-element.8, f32[1024]{0:T(1024)S(1)} %pmax.7), kind=kOutput, calls=%fused_computation.19 | convolution fusion | flops 234881024 | bytes 67182592 | tf_op jit(solution)/shard_map/dot_general | solution.py:39
  251.3 10.1 %psum.37 = f32[1024]{0:T(1024)S(1)} all-reduce(f32[1024]{0:T(1024)S(1)} %bitcast.21), channel_id=1, replica_groups=mesh['docs'=8,'protos'=4] {'protos'}, use_global_device_ids=true, to_apply=%region_5.0 | all-reduce | flops 1024 | bytes 8192 | tf_op jit(solution)/shard_map/psum | solution.py:45
  261.4 46.4 %fusion.4 = f32[1,16384]{1,0:T(1,128)} fusion(f32[1024,1]{0,1:T(1,128)S(1)} %bitcast.19, f32[1024,16384]{1,0:T(8,128)} %get-tuple-element.8, f32[1024]{0:T(1024)S(1)} %pmax.7), kind=kOutput, calls=%fused_computation.18 | convolution fusion | flops 234881024 | bytes 67182592 | tf_op jit(solution)/shard_map/dot_general | solution.py:31
  307.8 0.0 all-reduce.5.cloned.1.call-update
  307.8 0.5 reduce-scatter.2.cloned.1.call-start
  308.3 50.4 %all-reduce.5.cloned.1.call-done = f32[16384]{0:T(1024)} async-done(((f32[16384]{0:T(1024)}), f32[16384]{0:T(1024)}) %all-reduce.5.cloned.1.call-update) | async-done | bytes 65552 | tf_op jit(solution)/shard_map/psum | solution.py:37
  358.8 1.5 multiply_log_fusion
  360.3 69.4 %fusion.3 = f32[1,1024]{1,0:T(1,128)S(1)} fusion(f32[16384,1]{0,1:T(1,128)S(1)} %bitcast.15, f32[1024,16384]{1,0:T(8,128)} %get-tuple-element.8, f32[1024]{0:T(1024)S(1)} %pmax.7), kind=kOutput, calls=%fused_computation.17 | convolution fusion | flops 234881024 | bytes 67182592 | tf_op jit(solution)/shard_map/dot_general | solution.py:39
  429.6 10.0 %psum.39 = f32[1024]{0:T(1024)S(1)} all-reduce(f32[1024]{0:T(1024)S(1)} %bitcast.22), channel_id=1, replica_groups=mesh['docs'=8,'protos'=4] {'protos'}, use_global_device_ids=true, to_apply=%region_7.0 | all-reduce | flops 1024 | bytes 8192 | tf_op jit(solution)/shard_map/psum | solution.py:45
  439.6 0.6 multiply_log_fusion.1
  440.2 39.8 %fusion = f32[16384,512]{1,0:T(8,128)} fusion(bf16[1024,512]{1,0:T(8,128)(2,1)S(1)} %copy-done, f32[16384]{0:T(1024)S(1)} %get-tuple-element.4, f32[1024]{0:T(1024)S(1)} %get-tuple-element.6, f32[1024,16384]{1,0:T(8,128)} %get-tuple-element.8, f32[1024]{0:T(1024)S(1)} %pmax.7), kind=kOutput, calls=%fused_computation.3 | convolution fusion | flops 17263755264 | bytes 101785600 | tf_op jit(solution)/shard_map/dot_general | solution.py:54
  480.0 0.0 reduce-scatter.2.cloned.1.call-update
  480.1 322.9 %reduce-scatter.2.cloned.1.call-done = f32[2048,512]{1,0:T(8,128)} async-done(((f32[16384,512]{1,0:T(8,128)}), f32[2048,512]{1,0:T(8,128)}) %reduce-scatter.2.cloned.1.call-update) | async-done | bytes 4194320 | tf_op jit(solution)/shard_map/reduce_scatter | solution.py:53
  803.0 2.5 multiply_reduce_fusion.1
  805.5 3.8 multiply_convert_fusion.2
  (3 shorter events, 0.0 us)
Async XLA Ops:
  7.2 1.2 copy-start
  7.2 173.9 %all-reduce.3.cloned.1.call-start = ((), (), s32[]{:S(2)}) async-start(), calls=%async_computation.1 | async-start | bytes 131072 | tf_op jit(solution)/shard_map/psum | solution.py:37
  127.0 231.8 %all-reduce.5.cloned.1.call-start = ((), (), s32[]{:S(2)}) async-start(), calls=%async_computation.2 | async-start | bytes 131072 | tf_op jit(solution)/shard_map/psum | solution.py:37
  307.8 495.2 %reduce-scatter.2.cloned.1.call-start = ((), (), s32[]{:S(2)}) async-start(), calls=%async_computation.3 | async-start | bytes 37748736 | tf_op jit(solution)/shard_map/reduce_scatter | solution.py:53
Sparse Core Ops, SparseCore 0:
  127.1 53.9 all-reduce.2
  307.9 50.7 all-reduce.4
  480.2 322.7 reduce-scatter.1
where the time goes:
time: 820 us; the launch traced here: 816 us
  waiting for transfers between devices  427 us (52%)
  matrix products  303 us (37%)
  blocking collectives  39.5 us (5%)
  other arithmetic  30.6 us (4%)
  between operations  14 us (2%)
    reduce_scatter x1, waiting for transfers between devices, on_device(): lax.psum_scatter(lax.dot_general(assignment, embeddings, (((0,), (0,)), (...  323 us
    dot_general x2, matrix products, on_device(): jnp.dot(numerators, col_scale, precision=lax.Precision.HIGHEST, preferred...  139 us
    psum x2, waiting for transfers between devices, on_device(): col_total = lax.psum(col_local, 'docs')  104 us
    dot_general x2, matrix products, on_device(): jnp.dot(row_weight, numerators, precision=lax.Precision.HIGHEST, preferre...  92.8 us
    dot_general x1, matrix products, on_device(): lax.dot_general(assignment, embeddings, (((0,), (0,)), ((), ())), preferr...  39.8 us
    dot_general x1, matrix products, on_device(): lax.dot_general(embeddings, prototypes, (((1,), (1,)), ((), ())), preferr...  31.5 us
    reduce_sum x1, other arithmetic, on_device(): row_total = lax.psum(jnp.sum(numerators, axis=1), 'protos')  21.2 us
    psum x2, blocking collectives, on_device(): row_sum = lax.psum(row_local, 'protos')  20.1 us
  transfers between devices with their start and end apart: 3, of which 3 were waited for; matrix products, arithmetic and copies ran while one was open for 0% of the time, Pallas kernels for 0%

commit v1 on v0

v1 whole, which is shorter than its diff:
```python
import functools
import math

import jax
import jax.numpy as jnp
from jax import lax
from jax.experimental import pallas as pl
from jax.experimental.pallas import tpu as pltpu
from jax.sharding import PartitionSpec as P

SWEEPS = 2
VMEM_LIMIT = 26 << 20
SUB = 512
F32 = jnp.float32
BF16 = jnp.bfloat16


def params():
    return pltpu.CompilerParams(vmem_limit_bytes=VMEM_LIMIT)


def whole():
    return pl.BlockSpec(memory_space=pltpu.VMEM)


def transposed_dot(a, b):
    return lax.dot_general(a, b, (((1,), (1,)), ((), ())), preferred_element_type=F32)


def rows_of(index, size):
    return pl.ds(pl.multiple_of(index * size, size), size)


def stats_kernel(gain, e_ref, p_ref, num_ref, peak_ref, lse_ref, s0, s1, total):
    step = pl.program_id(0)
    steps = pl.num_programs(0) - 1

    def finish(scores_ref, block):
        scores = scores_ref[...]
        peak = jnp.max(scores, axis=0, keepdims=True)
        num = jnp.exp2((scores - peak) * gain)
        num_ref[rows_of(block, SUB), :] = num.astype(BF16)
        peak_ref[pl.ds(block, 1), :] = peak * gain
        total[pl.ds(block, 1), :] = jnp.sum(num, axis=0, keepdims=True)

    @pl.when(step < steps)
    def _():
        s0[...] = transposed_dot(p_ref[:SUB, :], e_ref[...])
        finish(s1, jnp.maximum(2 * step - 1, 0))
        s1[...] = transposed_dot(p_ref[SUB:, :], e_ref[...])
        finish(s0, 2 * step)

    @pl.when(step == steps)
    def _():
        finish(s1, 2 * step - 1)
        peaks = peak_ref[...]
        top = jnp.max(peaks, axis=0, keepdims=True)
        parts = total[...] * jnp.exp2(peaks - top)
        lse_ref[...] = top + jnp.log2(jnp.sum(parts, axis=0, keepdims=True))


def stats(e, p, gain):
    docs, width = e.shape
    protos = p.shape[0]
    steps = protos // (2 * SUB)
    blocks = protos // SUB
    return pl.pallas_call(
        functools.partial(stats_kernel, gain),
        grid=(steps + 1,),
        in_specs=[
            pl.BlockSpec((docs, width), lambda i: (0, 0)),
            pl.BlockSpec((2 * SUB, width), lambda i: (jnp.minimum(i, steps - 1), 0)),
        ],
        out_specs=[whole(), whole(), whole()],
        out_shape=[
            pltpu.VMEM((protos, docs), BF16),
            jax.ShapeDtypeStruct((blocks, docs), F32),
            jax.ShapeDtypeStruct((1, docs), F32),
        ],
        scratch_shapes=[
            pltpu.VMEM((SUB, docs), F32),
            pltpu.VMEM((SUB, docs), F32),
            pltpu.VMEM((blocks, docs), F32),
        ],
        compiler_params=params(),
    )(e, p)


def split_rows(row):
    high = row.astype(BF16)
    rest = row - high.astype(F32)
    mid = rest.astype(BF16)
    low = (rest - mid.astype(F32)).astype(BF16)
    pad = jnp.zeros((5, row.shape[1]), BF16)
    return jnp.concatenate([high, mid, low, pad], axis=0)


def columns_kernel(num_ref, peak_ref, lse_ref, r_ref, out_ref):
    blocks = peak_ref.shape[0]

    def body(b, carry):
        weight = jnp.exp2(peak_ref[pl.ds(b, 1), :] - lse_ref[...]) * r_ref[...]
        part = transposed_dot(split_rows(weight), num_ref[rows_of(b, SUB), :])
        out_ref[:, rows_of(b, SUB)] = jnp.sum(part, axis=0, keepdims=True)
        return carry

    lax.fori_loop(0, blocks, body, 0, unroll=2)


def columns(num, peaks, lse, r):
    return pl.pallas_call(
        columns_kernel,
        in_specs=[whole()] * 4,
        out_specs=whole(),
        out_shape=jax.ShapeDtypeStruct((1, num.shape[0]), F32),
        compiler_params=params(),
    )(num, peaks, lse, r)


def rows_kernel(num_ref, peak_ref, lse_ref, cs_ref, out_ref):
    blocks = peak_ref.shape[0]

    def body(b, total):
        weight = jnp.exp2(peak_ref[pl.ds(b, 1), :] - lse_ref[...])
        part = jnp.dot(
            split_rows(cs_ref[:, rows_of(b, SUB)]),
            num_ref[rows_of(b, SUB), :],
            preferred_element_type=F32,
        )
        return total + weight * part

    total = lax.fori_loop(
        0, blocks, body, jnp.zeros((8, num_ref.shape[1]), F32), unroll=2
    )
    out_ref[...] = jnp.sum(total, axis=0, keepdims=True)


def row_sums(num, peaks, lse, cs):
    return pl.pallas_call(
        rows_kernel,
        in_specs=[whole()] * 4,
        out_specs=whole(),
        out_shape=jax.ShapeDtypeStruct((1, num.shape[1]), F32),
        compiler_params=params(),
    )(num, peaks, lse, cs)


UPDATE_DOCS = 512
UPDATE_SUB = 256


def update_kernel(gain, place_ref, p_ref, e_ref, v_ref, cs_ref, out_ref, scores, acc):
    del place_ref
    step = pl.program_id(0)
    own = p_ref.shape[0]
    parts = own // UPDATE_SUB

    @pl.when(step == 0)
    def _():
        acc[...] = jnp.zeros_like(acc)

    def score(k):
        scores[k % 2] = transposed_dot(
            p_ref[k * UPDATE_SUB : (k + 1) * UPDATE_SUB, :], e_ref[...]
        )

    score(0)
    for k in range(parts):
        if k + 1 < parts:
            score(k + 1)
        share = jnp.exp2(scores[k % 2] * gain + v_ref[...]).astype(BF16)
        place = slice(k * UPDATE_SUB, (k + 1) * UPDATE_SUB)
        acc[place, :] += jnp.dot(share, e_ref[...], preferred_element_type=F32)

    @pl.when(step == pl.num_programs(0) - 1)
    def _():
        summed = acc[...] * cs_ref[...]
        square = jnp.mean(summed * summed, axis=1, keepdims=True)
        out_ref[...] = (summed * lax.rsqrt(square + 1e-06)).astype(BF16)


def update(place, p, e_all, v_all, cs_own, gain):
    own = cs_own.shape[0]
    docs, width = e_all.shape
    return pl.pallas_call(
        functools.partial(update_kernel, gain),
        grid_spec=pltpu.PrefetchScalarGridSpec(
            num_scalar_prefetch=1,
            grid=(docs // UPDATE_DOCS,),
            in_specs=[
                pl.BlockSpec((own, width), lambda i, place: (place[0], 0)),
                pl.BlockSpec((UPDATE_DOCS, width), lambda i, place: (i, 0)),
                pl.BlockSpec((1, UPDATE_DOCS), lambda i, place: (0, i)),
                pl.BlockSpec((own, 1), lambda i, place: (0, 0)),
            ],
            out_specs=pl.BlockSpec((own, width), lambda i, place: (0, 0)),
            scratch_shapes=[
                pltpu.VMEM((2, UPDATE_SUB, UPDATE_DOCS), F32),
                pltpu.VMEM((own, width), F32),
            ],
        ),
        out_shape=jax.ShapeDtypeStruct((own, width), BF16),
        compiler_params=params(),
    )(place, p, e_all, v_all, cs_own)


def swap(x, axis, bit):
    size = lax.axis_size(axis)
    return lax.ppermute(x, axis, [(i, i ^ bit) for i in range(size)])


def bits(axis):
    bit = 1
    while bit < lax.axis_size(axis):
        yield bit
        bit *= 2


def reduce_over(x, axis, combine):
    for bit in bits(axis):
        x = combine(x, swap(x, axis, bit))
    return x


def gather_over(x, axis):
    for bit in bits(axis):
        other = swap(x, axis, bit)
        upper = (lax.axis_index(axis) & bit) != 0
        x = jnp.where(
            upper,
            jnp.concatenate([other, x], axis=1),
            jnp.concatenate([x, other], axis=1),
        )
    return x


def log_add(a, b):
    top = jnp.maximum(a, b)
    return top + jnp.log2(jnp.exp2(a - top) + jnp.exp2(b - top))


def on_device(embeddings, prototypes):
    docs, width = embeddings.shape
    protos = prototypes.shape[0]
    doc_ranks = lax.axis_size("docs")
    total_docs = docs * doc_ranks
    total_protos = protos * lax.axis_size("protos")
    own = protos // doc_ranks
    gain = 4.0 / math.sqrt(width) / math.log(2.0)
    place = lax.axis_index("docs")

    e_all = lax.all_gather(embeddings, "docs", tiled=True)
    num, peaks, lse = stats(embeddings, prototypes, gain)
    num = pltpu.with_memory_space_constraint(num, pltpu.VMEM)
    lse = reduce_over(lse, "protos", log_add)
    r = jnp.ones((1, docs), F32)
    for sweep_index in range(SWEEPS):
        col_total = reduce_over(columns(num, peaks, lse, r), "docs", jnp.add)
        cs = 1.0 / (total_protos * col_total)
        row_sum = reduce_over(row_sums(num, peaks, lse, cs), "protos", jnp.add)
        r = 1.0 / (total_docs * row_sum)
    column_potential = jnp.log(total_docs * cs)
    row_potential = jnp.log(r)
    v_all = gather_over(jnp.log2(r * total_docs) - lse, "docs")
    cs_own = lax.dynamic_slice(cs, (0, place * own), (1, own)).reshape(own, 1)
    new_prototypes = update(
        place.reshape(1).astype(jnp.int32),
        pltpu.with_memory_space_constraint(prototypes, pltpu.HBM),
        pltpu.with_memory_space_constraint(e_all, pltpu.HBM),
        v_all,
        cs_own,
        gain,
    )
    return (new_prototypes, column_potential.reshape(-1), row_potential.reshape(-1))


def solution(mesh):
    placed = (P("docs", None), P("protos", None))
    return jax.shard_map(
        on_device,
        mesh=mesh,
        in_specs=placed,
        out_specs=(P(("protos", "docs"), None), P("protos"), P("docs")),
        check_vma=False,
    )
```

time: 820 us -> 204 us (0.25)
  waiting for transfers between devices: 427 us -> 40.4 us
  matrix products: 303 us -> 0 us
  Pallas kernels: 0 us -> 115 us
  blocking collectives: 39.5 us -> 0 us
  starting transfers between devices: 0.8 us -> 25.4 us
  other arithmetic: 30.6 us -> 7.49 us
    reduce_scatter x1 -> x0, waiting for transfers between devices: 323 us -> none  [on_device(): lax.psum_scatter(lax.dot_general(assignment, embeddings, (((0,), (0,)), (...]
    dot_general x6 -> x0, matrix products: 303 us -> none  [the longest x2 139 us: on_device(): jnp.dot(numerators, col_scale, precision=lax.Precision.HIGHEST, preferred...]
    pallas_call x0 -> x6, Pallas kernels: none -> 115 us  [the longest x1 42.8 us: update(): pl.pallas_call(functools.partial(update_kernel, gain), grid_spec=pltpu.Pr...]
    psum x2 -> x0, waiting for transfers between devices: 104 us -> none  [on_device(): col_total = lax.psum(col_local, 'docs')]
    ppermute x0 -> x15, waiting for transfers between devices: none -> 39.7 us  [swap(): return lax.ppermute(x, axis, [(i, i ^ bit) for i in range(size)])]
    psum x3 -> x0, blocking collectives: 28.2 us -> none  [the longest x2 20.1 us: on_device(): row_sum = lax.psum(row_local, 'protos')]
    ppermute x0 -> x15, starting transfers between devices: none -> 25.4 us  [swap(): return lax.ppermute(x, axis, [(i, i ^ bit) for i in range(size)])]
    reduce_sum x2 -> x0, other arithmetic: 23.8 us -> none  [the longest x1 21.2 us: on_device(): row_total = lax.psum(jnp.sum(numerators, axis=1), 'protos')]
  transfers between devices with their start and end apart: 3 -> 16, of which waited for: 3 -> 15; matrix products, arithmetic and copies ran while one was open for 0% -> 4% of each run, Pallas kernels for 0% -> 35%
where the time goes in v1:
time: 204 us
  Pallas kernels  115 us (56%)
  waiting for transfers between devices  40.4 us (20%)
  starting transfers between devices  25.4 us (12%)
  between operations  14.1 us (7%)
  other arithmetic  7.49 us (4%)
    pallas_call x1, Pallas kernels, update(): pl.pallas_call(functools.partial(update_kernel, gain), grid_spec=pltpu.Pr...  42.8 us
    ppermute x15, waiting for transfers between devices, swap(): return lax.ppermute(x, axis, [(i, i ^ bit) for i in range(size)])  39.7 us
    pallas_call x1, Pallas kernels, stats(): pl.pallas_call(functools.partial(stats_kernel, gain), grid=(steps + 1,),...  32.1 us
    ppermute x15, starting transfers between devices, swap(): return lax.ppermute(x, axis, [(i, i ^ bit) for i in range(size)])  25.4 us
    pallas_call x2, Pallas kernels, columns(): pl.pallas_call(columns_kernel, in_specs=[whole()] * 4, out_specs=whole(),...  24.5 us
    pallas_call x2, Pallas kernels, row_sums(): pl.pallas_call(rows_kernel, in_specs=[whole()] * 4, out_specs=whole(), ou...  15.6 us
  transfers between devices with their start and end apart: 16, of which 15 were waited for; matrix products, arithmetic and copies ran while one was open for 4% of the time, Pallas kernels for 35%

profile of v1, /device:TPU:0, one launch (start us, length us, event | category | flops | bytes accessed | tf_op | source)
XLA Modules:
  0.0 204.0 jit_solution(4898556312660760176)
XLA Ops:
  7.2 0.0 all-gather.2.cloned.1.call-start
  7.2 0.7 all-gather.2.cloned.1.call-update
  7.9 32.1 %shard_map.49 = (bf16[16384,1024]{1,0:T(8,128)(2,1)S(1)}, f32[32,1024]{1,0:T(8,128)}, f32[1,1024]{1,0:T(1,128)}) custom-call(bf16[1024,512]{1,0:T(8,128)(2,1)} %e_ref.1, bf16[16384,512]{1,0:T(8,128)(2,1)} %p_ref.3), custom_call_target="tpu_custom_call" | custom-call | tf_op jit(solution)/shard_map/pallas_call | solution.py:67
  40.0 2.9 %collective-permute-start = (f32[1,1024]{1,0:T(1,128)}, f32[1,1024]{1,0:T(1,128)S(1)}, u32[]{:S(2)}, u32[]{:S(2)}) collective-permute-start(f32[1,1024]{1,0:T(1,128)} %get-tuple-element.8), channel_id=1, source_target_pairs={{0,1},{1,0},{2,3},{3,2},{4,5},{5,4},{6,7},{7,6},{8,9},{9,8},{10,11... | collective-permute-start | bytes 12296 | tf_op jit(solution)/shard_map/ppermute | solution.py:209
  42.9 1.8 collective-permute-done
  44.7 0.7 multiply_add_fusion.1
  45.4 2.1 %collective-permute-start.1 = (f32[1,1024]{1,0:T(1,128)S(1)}, f32[1,1024]{1,0:T(1,128)S(1)}, u32[]{:S(2)}, u32[]{:S(2)}) collective-permute-start(f32[1,1024]{1,0:T(1,128)S(1)} %multiply_add_fusion.1), channel_id=1, source_target_pairs={{0,2},{1,3},{2,0},{3,1},{4,6},{5,7},{6,4},{7,5},{8,10},{9,11},{10,... | collective-permute-start | bytes 12296 | tf_op jit(solution)/shard_map/ppermute | solution.py:209
  47.5 1.6 collective-permute-done.1
  49.1 0.6 multiply_add_fusion.lse_ref
  49.7 0.6 broadcast_9_r_ref.2.r_ref
  50.3 12.3 %shard_map.50 = f32[1,16384]{1,0:T(1,128)} custom-call(bf16[16384,1024]{1,0:T(8,128)(2,1)S(1)} %get-tuple-element.6.num_ref, f32[32,1024]{1,0:T(8,128)} %get-tuple-element.7.peak_ref, f32[1,1024]{1,0:T(1,128)} %multiply_add_fusion.lse_ref, f32[1,1024]{1,0:T(1,128)} %broadcast_9_r_ref.2.r_ref), custom_call_target="tpu_custom_call" | custom-call | tf_op jit(solution)/shard_map/pallas_call | solution.py:111
  62.6 0.0 collective-permute-start.2
  62.6 1.5 collective-permute-done.2
  64.1 0.9 add.49
  65.0 2.2 %collective-permute-start.3 = (f32[1,16384]{1,0:T(1,128)S(1)}, f32[1,16384]{1,0:T(1,128)S(1)}, u32[]{:S(2)}, u32[]{:S(2)}) collective-permute-start(f32[1,16384]{1,0:T(1,128)S(1)} %add.49), channel_id=1, source_target_pairs={{0,8},{4,12},{8,0},{12,4},{16,24},{20,28},{24,16},{28,20},{1,9},{5... | collective-permute-start | bytes 196616 | tf_op jit(solution)/shard_map/ppermute | solution.py:209
  67.1 7.8 %collective-permute-done.3 = f32[1,16384]{1,0:T(1,128)S(1)} collective-permute-done((f32[1,16384]{1,0:T(1,128)S(1)}, f32[1,16384]{1,0:T(1,128)S(1)}, u32[]{:S(2)}, u32[]{:S(2)}) %collective-permute-start.3) | collective-permute-done | bytes 65568 | tf_op jit(solution)/shard_map/ppermute | solution.py:209
  74.9 0.1 add.50
  75.0 2.5 %collective-permute-start.4 = (f32[1,16384]{1,0:T(1,128)S(1)}, f32[1,16384]{1,0:T(1,128)S(1)}, u32[]{:S(2)}, u32[]{:S(2)}) collective-permute-start(f32[1,16384]{1,0:T(1,128)S(1)} %add.50), channel_id=1, source_target_pairs={{0,16},{4,20},{8,24},{12,28},{16,0},{20,4},{24,8},{28,12},{1,17},{... | collective-permute-start | bytes 196616 | tf_op jit(solution)/shard_map/ppermute | solution.py:209
  77.4 7.3 %collective-permute-done.4 = f32[1,16384]{1,0:T(1,128)S(1)} collective-permute-done((f32[1,16384]{1,0:T(1,128)S(1)}, f32[1,16384]{1,0:T(1,128)S(1)}, u32[]{:S(2)}, u32[]{:S(2)}) %collective-permute-start.4) | collective-permute-done | bytes 65568 | tf_op jit(solution)/shard_map/ppermute | solution.py:209
  84.8 0.7 multiply_divide_fusion.1.cs_ref
  85.5 7.8 %shard_map.51 = f32[1,1024]{1,0:T(1,128)} custom-call(bf16[16384,1024]{1,0:T(8,128)(2,1)S(1)} %get-tuple-element.6.num_ref, f32[32,1024]{1,0:T(8,128)} %get-tuple-element.7.peak_ref, f32[1,1024]{1,0:T(1,128)} %multiply_add_fusion.lse_ref, f32[1,16384]{1,0:T(1,128)} %multiply_divide_fusion.1.cs_ref), custom_call_target="tpu_custom_call" | custom-call | tf_op jit(solution)/shard_map/pallas_call | solution.py:139
  93.3 1.5 collective-permute-start.5
  94.8 2.3 %collective-permute-done.5 = f32[1,1024]{1,0:T(1,128)S(1)} collective-permute-done((f32[1,1024]{1,0:T(1,128)}, f32[1,1024]{1,0:T(1,128)S(1)}, u32[]{:S(2)}, u32[]{:S(2)}) %collective-permute-start.5) | collective-permute-done | bytes 4128 | tf_op jit(solution)/shard_map/ppermute | solution.py:209
  97.1 0.7 add.52
  97.8 1.5 collective-permute-start.6
  99.3 2.1 %collective-permute-done.6 = f32[1,1024]{1,0:T(1,128)S(1)} collective-permute-done((f32[1,1024]{1,0:T(1,128)S(1)}, f32[1,1024]{1,0:T(1,128)S(1)}, u32[]{:S(2)}, u32[]{:S(2)}) %collective-permute-start.6) | collective-permute-done | bytes 4128 | tf_op jit(solution)/shard_map/ppermute | solution.py:209
  101.4 0.6 multiply_divide_fusion.3.r_ref
  102.0 12.3 %shard_map.52 = f32[1,16384]{1,0:T(1,128)} custom-call(bf16[16384,1024]{1,0:T(8,128)(2,1)S(1)} %get-tuple-element.6.num_ref, f32[32,1024]{1,0:T(8,128)} %get-tuple-element.7.peak_ref, f32[1,1024]{1,0:T(1,128)} %multiply_add_fusion.lse_ref, f32[1,1024]{1,0:T(1,128)} %multiply_divide_fusion.3.r_ref), custom_call_target="tpu_custom_call" | custom-call | tf_op jit(solution)/shard_map/pallas_call | solution.py:111
  114.3 0.0 collective-permute-start.7
  114.3 1.5 collective-permute-done.7
  115.8 0.9 add.54
  116.7 2.0 collective-permute-start.8
  118.7 2.4 %collective-permute-done.8 = f32[1,16384]{1,0:T(1,128)S(1)} collective-permute-done((f32[1,16384]{1,0:T(1,128)S(1)}, f32[1,16384]{1,0:T(1,128)S(1)}, u32[]{:S(2)}, u32[]{:S(2)}) %collective-permute-start.8) | collective-permute-done | bytes 65568 | tf_op jit(solution)/shard_map/ppermute | solution.py:209
  121.1 0.1 add.55
  121.2 3.5 %collective-permute-start.9 = (f32[1,16384]{1,0:T(1,128)S(1)}, f32[1,16384]{1,0:T(1,128)S(1)}, u32[]{:S(2)}, u32[]{:S(2)}) collective-permute-start(f32[1,16384]{1,0:T(1,128)S(1)} %add.55), channel_id=1, source_target_pairs={{0,16},{4,20},{8,24},{12,28},{16,0},{20,4},{24,8},{28,12},{1,17},{... | collective-permute-start | bytes 196616 | tf_op jit(solution)/shard_map/ppermute | solution.py:209
  124.7 2.6 %collective-permute-done.9 = f32[1,16384]{1,0:T(1,128)S(1)} collective-permute-done((f32[1,16384]{1,0:T(1,128)S(1)}, f32[1,16384]{1,0:T(1,128)S(1)}, u32[]{:S(2)}, u32[]{:S(2)}) %collective-permute-start.9) | collective-permute-done | bytes 65568 | tf_op jit(solution)/shard_map/ppermute | solution.py:209
  127.3 0.8 multiply_log_fusion
  128.1 0.0 copy-start
  128.1 7.8 %shard_map.53 = f32[1,1024]{1,0:T(1,128)} custom-call(bf16[16384,1024]{1,0:T(8,128)(2,1)S(1)} %get-tuple-element.6.num_ref, f32[32,1024]{1,0:T(8,128)} %get-tuple-element.7.peak_ref, f32[1,1024]{1,0:T(1,128)} %multiply_add_fusion.lse_ref, f32[1,16384]{1,0:T(1,128)} %get-tuple-element.12.cs_ref), custom_call_target="tpu_custom_call" | custom-call | tf_op jit(solution)/shard_map/pallas_call | solution.py:139
  135.9 1.4 collective-permute-start.10
  137.3 2.4 %collective-permute-done.10 = f32[1,1024]{1,0:T(1,128)S(1)} collective-permute-done((f32[1,1024]{1,0:T(1,128)}, f32[1,1024]{1,0:T(1,128)S(1)}, u32[]{:S(2)}, u32[]{:S(2)}) %collective-permute-start.10) | collective-permute-done | bytes 4128 | tf_op jit(solution)/shard_map/ppermute | solution.py:209
  139.7 0.7 add.57
  140.4 1.4 collective-permute-start.11
  141.8 2.2 %collective-permute-done.11 = f32[1,1024]{1,0:T(1,128)S(1)} collective-permute-done((f32[1,1024]{1,0:T(1,128)S(1)}, f32[1,1024]{1,0:T(1,128)S(1)}, u32[]{:S(2)}, u32[]{:S(2)}) %collective-permute-start.11) | collective-permute-done | bytes 4128 | tf_op jit(solution)/shard_map/ppermute | solution.py:209
  144.0 0.6 fusion.2
  144.6 0.0 copy-done
  144.6 0.1 collective-permute-start.12
  144.7 0.7 dynamic-slice_bitcast_fusion
  145.4 0.4 copy.5.cs_ref
  145.8 0.1 collective-permute-done.12
  145.9 1.6 collective-permute-start.13
  147.4 2.2 %collective-permute-done.13 = f32[1,2048]{1,0:T(1,128)S(1)} collective-permute-done((f32[1,2048]{1,0:T(1,128)S(1)}, f32[1,2048]{1,0:T(1,128)S(1)}, u32[]{:S(2)}, u32[]{:S(2)}) %collective-permute-start.13) | collective-permute-done | bytes 8224 | tf_op jit(solution)/shard_map/ppermute | solution.py:209
  149.6 2.8 %collective-permute-start.14 = (f32[1,4096]{1,0:T(1,128)S(1)}, f32[1,4096]{1,0:T(1,128)S(1)}, u32[]{:S(2)}, u32[]{:S(2)}) collective-permute-start(f32[1,4096]{1,0:T(1,128)S(1)} %broadcast_select_fusion.1), channel_id=1, source_target_pairs={{0,16},{4,20},{8,24},{12,28},{16,0},{20,4},{24,8},{28,12},{1,17},{... | collective-permute-start | bytes 49160 | tf_op jit(solution)/shard_map/ppermute | solution.py:209
  152.4 2.0 collective-permute-done.14
  154.4 0.0 all-gather.2.cloned.1.call-done.e_ref
  154.4 42.8 %shard_map.54 = bf16[2048,512]{1,0:T(8,128)(2,1)} custom-call(s32[1]{0:T(128)} %bitcast.place_ref, bf16[16384,512]{1,0:T(8,128)(2,1)} %p_ref.3, bf16[8192,512]{1,0:T(8,128)(2,1)} %all-gather.2.cloned.1.call-done.e_ref, f32[1,8192]{1,0:T(1,128)S(1)} %broadcast_select_fusion.v_ref, f32[2048,1]{1,0:T(8,128)S(1)} %copy.5.cs_ref), custom_call_target="tpu_custom_call" | custom-call | tf_op jit(solution)/shard_map/pallas_call | solution.py:185
  (6 shorter events, 0.1 us)
Async XLA Ops:
  7.2 147.2 %all-gather.2.cloned.1.call-start = ((), (), s32[]{:S(2)}) async-start(), calls=%async_computation | async-start | bytes 9437184 | tf_op jit(solution)/shard_map/all_gather | solution.py:252
  40.0 4.7 %collective-permute-start = (f32[1,1024]{1,0:T(1,128)}, f32[1,1024]{1,0:T(1,128)S(1)}, u32[]{:S(2)}, u32[]{:S(2)}) collective-permute-start(f32[1,1024]{1,0:T(1,128)} %get-tuple-element.8), channel_id=1, source_target_pairs={{0,1},{1,0},{2,3},{3,2},{4,5},{5,4},{6,7},{7,6},{8,9},{9,8},{10,11... | collective-permute-start | bytes 12296 | tf_op jit(solution)/shard_map/ppermute | solution.py:209
  45.4 3.7 %collective-permute-start.1 = (f32[1,1024]{1,0:T(1,128)S(1)}, f32[1,1024]{1,0:T(1,128)S(1)}, u32[]{:S(2)}, u32[]{:S(2)}) collective-permute-start(f32[1,1024]{1,0:T(1,128)S(1)} %multiply_add_fusion.1), channel_id=1, source_target_pairs={{0,2},{1,3},{2,0},{3,1},{4,6},{5,7},{6,4},{7,5},{8,10},{9,11},{10,... | collective-permute-start | bytes 12296 | tf_op jit(solution)/shard_map/ppermute | solution.py:209
  62.6 1.5 collective-permute-start.2
  65.0 9.9 %collective-permute-start.3 = (f32[1,16384]{1,0:T(1,128)S(1)}, f32[1,16384]{1,0:T(1,128)S(1)}, u32[]{:S(2)}, u32[]{:S(2)}) collective-permute-start(f32[1,16384]{1,0:T(1,128)S(1)} %add.49), channel_id=1, source_target_pairs={{0,8},{4,12},{8,0},{12,4},{16,24},{20,28},{24,16},{28,20},{1,9},{5... | collective-permute-start | bytes 196616 | tf_op jit(solution)/shard_map/ppermute | solution.py:209
  75.0 9.8 %collective-permute-start.4 = (f32[1,16384]{1,0:T(1,128)S(1)}, f32[1,16384]{1,0:T(1,128)S(1)}, u32[]{:S(2)}, u32[]{:S(2)}) collective-permute-start(f32[1,16384]{1,0:T(1,128)S(1)} %add.50), channel_id=1, source_target_pairs={{0,16},{4,20},{8,24},{12,28},{16,0},{20,4},{24,8},{28,12},{1,17},{... | collective-permute-start | bytes 196616 | tf_op jit(solution)/shard_map/ppermute | solution.py:209
  93.3 3.8 %collective-permute-start.5 = (f32[1,1024]{1,0:T(1,128)}, f32[1,1024]{1,0:T(1,128)S(1)}, u32[]{:S(2)}, u32[]{:S(2)}) collective-permute-start(f32[1,1024]{1,0:T(1,128)} %shard_map.51), channel_id=1, source_target_pairs={{0,1},{1,0},{2,3},{3,2},{4,5},{5,4},{6,7},{7,6},{8,9},{9,8},{10,11... | collective-permute-start | bytes 12296 | tf_op jit(solution)/shard_map/ppermute | solution.py:209
  97.8 3.6 %collective-permute-start.6 = (f32[1,1024]{1,0:T(1,128)S(1)}, f32[1,1024]{1,0:T(1,128)S(1)}, u32[]{:S(2)}, u32[]{:S(2)}) collective-permute-start(f32[1,1024]{1,0:T(1,128)S(1)} %add.52), channel_id=1, source_target_pairs={{0,2},{1,3},{2,0},{3,1},{4,6},{5,7},{6,4},{7,5},{8,10},{9,11},{10,... | collective-permute-start | bytes 12296 | tf_op jit(solution)/shard_map/ppermute | solution.py:209
  114.3 1.5 collective-permute-start.7
  116.7 4.4 %collective-permute-start.8 = (f32[1,16384]{1,0:T(1,128)S(1)}, f32[1,16384]{1,0:T(1,128)S(1)}, u32[]{:S(2)}, u32[]{:S(2)}) collective-permute-start(f32[1,16384]{1,0:T(1,128)S(1)} %add.54), channel_id=1, source_target_pairs={{0,8},{4,12},{8,0},{12,4},{16,24},{20,28},{24,16},{28,20},{1,9},{5... | collective-permute-start | bytes 196616 | tf_op jit(solution)/shard_map/ppermute | solution.py:209
  121.2 6.1 %collective-permute-start.9 = (f32[1,16384]{1,0:T(1,128)S(1)}, f32[1,16384]{1,0:T(1,128)S(1)}, u32[]{:S(2)}, u32[]{:S(2)}) collective-permute-start(f32[1,16384]{1,0:T(1,128)S(1)} %add.55), channel_id=1, source_target_pairs={{0,16},{4,20},{8,24},{12,28},{16,0},{20,4},{24,8},{28,12},{1,17},{... | collective-permute-start | bytes 196616 | tf_op jit(solution)/shard_map/ppermute | solution.py:209
  128.1 16.5 %copy-start = (f32[1,1024]{1,0:T(1,128)S(1)}, f32[1,1024]{1,0:T(1,128)}, u32[]{:S(2)}) copy-start(f32[1,1024]{1,0:T(1,128)} %multiply_add_fusion.lse_ref) | copy-start | bytes 12292
  135.9 3.8 %collective-permute-start.10 = (f32[1,1024]{1,0:T(1,128)}, f32[1,1024]{1,0:T(1,128)S(1)}, u32[]{:S(2)}, u32[]{:S(2)}) collective-permute-start(f32[1,1024]{1,0:T(1,128)} %shard_map.53), channel_id=1, source_target_pairs={{0,1},{1,0},{2,3},{3,2},{4,5},{5,4},{6,7},{7,6},{8,9},{9,8},{10,11... | collective-permute-start | bytes 12296 | tf_op jit(solution)/shard_map/ppermute | solution.py:209
  140.4 3.6 %collective-permute-start.11 = (f32[1,1024]{1,0:T(1,128)S(1)}, f32[1,1024]{1,0:T(1,128)S(1)}, u32[]{:S(2)}, u32[]{:S(2)}) collective-permute-start(f32[1,1024]{1,0:T(1,128)S(1)} %add.57), channel_id=1, source_target_pairs={{0,2},{1,3},{2,0},{3,1},{4,6},{5,7},{6,4},{7,5},{8,10},{9,11},{10,... | collective-permute-start | bytes 12296 | tf_op jit(solution)/shard_map/ppermute | solution.py:209
  144.6 1.2 collective-permute-start.12
  145.9 3.7 %collective-permute-start.13 = (f32[1,2048]{1,0:T(1,128)S(1)}, f32[1,2048]{1,0:T(1,128)S(1)}, u32[]{:S(2)}, u32[]{:S(2)}) collective-permute-start(f32[1,2048]{1,0:T(1,128)S(1)} %broadcast_select_fusion.2), channel_id=1, source_target_pairs={{0,8},{4,12},{8,0},{12,4},{16,24},{20,28},{24,16},{28,20},{1,9},{5... | collective-permute-start | bytes 24584 | tf_op jit(solution)/shard_map/ppermute | solution.py:209
  149.6 4.7 %collective-permute-start.14 = (f32[1,4096]{1,0:T(1,128)S(1)}, f32[1,4096]{1,0:T(1,128)S(1)}, u32[]{:S(2)}, u32[]{:S(2)}) collective-permute-start(f32[1,4096]{1,0:T(1,128)S(1)} %broadcast_select_fusion.1), channel_id=1, source_target_pairs={{0,16},{4,20},{8,24},{12,28},{16,0},{20,4},{24,8},{28,12},{1,17},{... | collective-permute-start | bytes 49160 | tf_op jit(solution)/shard_map/ppermute | solution.py:209
Sparse Core Ops, SparseCore 0:
  9.6 87.5 all-gather.1

commit v2 on v1

v2 whole, which is shorter than its diff:
```python
import functools
import math

import jax
import jax.numpy as jnp
from jax import lax
from jax.experimental import pallas as pl
from jax.experimental.pallas import tpu as pltpu
from jax.sharding import PartitionSpec as P

SWEEPS = 2
VMEM_LIMIT = 26 << 20
BLOCK = 1024
FIRST = 256
DOC_TILE = 256
LARGE = 2.0**60
CHUNK = 128
COLUMN_GROUP = 32
ROW_GROUP = 16
ROW_TAKEN = 10
F32 = jnp.float32
BF16 = jnp.bfloat16


def params():
    return pltpu.CompilerParams(vmem_limit_bytes=VMEM_LIMIT)


def whole():
    return pl.BlockSpec(memory_space=pltpu.VMEM)


def in_vmem(x):
    return pltpu.with_memory_space_constraint(x, pltpu.VMEM)


def in_hbm(x):
    return pltpu.with_memory_space_constraint(x, pltpu.HBM)


def transposed_dot(a, b):
    return lax.dot_general(a, b, (((1,), (1,)), ((), ())), preferred_element_type=F32)


def rows_of(index, size):
    return pl.ds(pl.multiple_of(index * size, size), size)


def stats_kernel(gain, e_ref, p_ref, p_any, num_ref, shift_ref, lse_ref, total, p_buf):
    step = pl.program_id(0)
    docs = e_ref.shape[0]
    tiles = [slice(d, d + DOC_TILE) for d in range(0, docs, DOC_TILE)]

    @pl.when(step == 0)
    def _():
        first = transposed_dot(p_ref[:FIRST, :], e_ref[...])
        shift_ref[...] = jnp.max(first, axis=0, keepdims=True)

    def fill(block_ref, block):
        sums = []
        for tile in tiles:
            scores = transposed_dot(block_ref[...], e_ref[tile, :])
            num = jnp.exp2((scores - shift_ref[:, tile]) * gain)
            num_ref[rows_of(block, BLOCK), tile] = num.astype(BF16)
            sums.append(jnp.sum(num, axis=0, keepdims=True))
        total[pl.ds(block, 1), :] = jnp.concatenate(sums, axis=1)

    fill(p_ref, step)

    @pl.when(step == pl.num_programs(0) - 1)
    def _():
        found = jnp.sum(total[...], axis=0, keepdims=True)
        fits = jnp.min(jnp.where(found < LARGE, 1.0, 0.0))

        @pl.when(fits < 0.5)
        def _():
            def peak(block, carry):
                pltpu.sync_copy(p_any.at[rows_of(block, BLOCK)], p_buf)
                for tile in tiles:
                    scores = transposed_dot(p_buf[...], e_ref[tile, :])
                    top = jnp.max(scores, axis=0, keepdims=True)
                    shift_ref[:, tile] = jnp.maximum(shift_ref[:, tile], top)
                return carry

            def again(block, carry):
                pltpu.sync_copy(p_any.at[rows_of(block, BLOCK)], p_buf)
                fill(p_buf, block)
                return carry

            blocks = total.shape[0]
            lax.fori_loop(0, blocks, peak, 0)
            lax.fori_loop(0, blocks, again, 0)

        found = jnp.sum(total[...], axis=0, keepdims=True)
        shift = shift_ref[...] * gain
        shift_ref[...] = shift
        lse_ref[...] = shift + jnp.log2(found)


def stats(e, p, gain):
    docs, width = e.shape
    protos = p.shape[0]
    blocks = protos // BLOCK
    return pl.pallas_call(
        functools.partial(stats_kernel, gain),
        grid=(blocks,),
        in_specs=[
            pl.BlockSpec((docs, width), lambda i: (0, 0)),
            pl.BlockSpec((BLOCK, width), lambda i: (i, 0)),
            pl.BlockSpec(memory_space=pl.ANY),
        ],
        out_specs=[whole(), whole(), whole()],
        out_shape=[
            pltpu.VMEM((protos, docs), BF16),
            pltpu.VMEM((1, docs), F32),
            pltpu.VMEM((1, docs), F32),
        ],
        scratch_shapes=[
            pltpu.VMEM((blocks, docs), F32),
            pltpu.VMEM((BLOCK, width), BF16),
        ],
        compiler_params=params(),
    )(e, p, p)


def split(x):
    high = x.astype(BF16)
    rest = x - high.astype(F32)
    mid = rest.astype(BF16)
    low = (rest - mid.astype(F32)).astype(BF16)
    return [part.astype(F32) for part in (high, mid, low)]


def columns_kernel(num_ref, w_ref, out_ref, turned):
    docs = num_ref.shape[1]
    taken = turned.shape[0]
    w = w_ref[...]
    rows = split(w[:, :taken]) + [jnp.zeros((CHUNK - 3, taken), F32)]
    turned[...] = jnp.concatenate(rows, axis=0).T.astype(BF16)
    lane = lax.broadcasted_iota(jnp.int32, out_ref.shape, 1)

    def body(group, found):
        base = pl.multiple_of(group * COLUMN_GROUP * CHUNK, CHUNK)
        part = jnp.dot(
            num_ref[pl.ds(base, COLUMN_GROUP * CHUNK), :taken],
            turned[...],
            preferred_element_type=F32,
        )
        for k in range(COLUMN_GROUP):
            here = part[k * CHUNK : (k + 1) * CHUNK]
            place = pl.ds(pl.multiple_of(base + k * CHUNK, CHUNK), CHUNK)
            for d in range(taken, docs, CHUNK):
                here += num_ref[place, d : d + CHUNK].astype(F32) * w[:, d : d + CHUNK]
            column = jnp.sum(here, axis=1, keepdims=True)
            found = jnp.where(lane == group * COLUMN_GROUP + k, column, found)
        return found

    groups = num_ref.shape[0] // (COLUMN_GROUP * CHUNK)
    out_ref[...] = lax.fori_loop(0, groups, body, jnp.ones(out_ref.shape, F32))


def chunk_lanes(protos):
    return -(-protos // (CHUNK * CHUNK)) * CHUNK


def columns(num, w):
    protos, docs = num.shape
    return pl.pallas_call(
        columns_kernel,
        in_specs=[whole()] * 2,
        out_specs=whole(),
        out_shape=pltpu.VMEM((CHUNK, chunk_lanes(protos)), F32),
        scratch_shapes=[pltpu.VMEM((docs // 2, CHUNK), BF16)],
        compiler_params=params(),
    )(num, in_vmem(w))


def rows_kernel(num_ref, w_ref, cs_ref, out_ref, parts):
    docs = num_ref.shape[1]
    turned = cs_ref[...]
    for j, part in enumerate(split(turned.T)):
        parts[j] = part
    lane = lax.broadcasted_iota(jnp.int32, turned.shape, 1)

    def body(group, carry):
        added, product = carry
        base = pl.multiple_of(group * ROW_GROUP * CHUNK, CHUNK)
        rows = [
            jnp.concatenate(
                [parts[j, pl.ds(group * ROW_GROUP + k, 1), :] for k in range(ROW_TAKEN)], axis=1
            )
            for j in range(3)
        ]
        rows.append(jnp.zeros((5, ROW_TAKEN * CHUNK), F32))
        product = product + jnp.dot(
            jnp.concatenate(rows, axis=0).astype(BF16),
            num_ref[pl.ds(base, ROW_TAKEN * CHUNK), :],
            preferred_element_type=F32,
        )
        for k in range(ROW_TAKEN, ROW_GROUP):
            here = jnp.where(lane == group * ROW_GROUP + k, turned, 0.0)
            column = jnp.sum(here, axis=1, keepdims=True)
            place = pl.ds(pl.multiple_of(base + k * CHUNK, CHUNK), CHUNK)
            scaled = num_ref[place, :].astype(F32) * column
            added = added + jnp.sum(scaled.reshape(CHUNK // 8, 8, docs), axis=0)
        return added, product

    groups = num_ref.shape[0] // (ROW_GROUP * CHUNK)
    zero = jnp.zeros((8, docs), F32)
    added, product = lax.fori_loop(0, groups, body, (zero, zero))
    out_ref[...] = w_ref[...] * jnp.sum(added + product, axis=0, keepdims=True)


def row_sums(num, w, cs):
    docs = num.shape[1]
    return pl.pallas_call(
        rows_kernel,
        in_specs=[whole()] * 3,
        out_specs=whole(),
        out_shape=pltpu.VMEM((1, docs), F32),
        scratch_shapes=[pltpu.VMEM((3, cs.shape[1], CHUNK), F32)],
        compiler_params=params(),
    )(num, in_vmem(w), in_vmem(cs))


UPDATE_DOCS = 512
UPDATE_SUB = 256


def update_kernel(gain, place_ref, p_ref, e_ref, v_ref, cs_ref, out_ref, scores, acc):
    step = pl.program_id(0)
    own = p_ref.shape[0]
    parts = own // UPDATE_SUB

    @pl.when(step == 0)
    def _():
        acc[...] = jnp.zeros_like(acc)

    def score(k):
        scores[k % 2] = transposed_dot(
            p_ref[k * UPDATE_SUB : (k + 1) * UPDATE_SUB, :], e_ref[...]
        )

    score(0)
    for k in range(parts):
        if k + 1 < parts:
            score(k + 1)
        share = jnp.exp2(scores[k % 2] * gain + v_ref[...]).astype(BF16)
        place = slice(k * UPDATE_SUB, (k + 1) * UPDATE_SUB)
        acc[place, :] += jnp.dot(share, e_ref[...], preferred_element_type=F32)

    @pl.when(step == pl.num_programs(0) - 1)
    def _():
        lane = lax.broadcasted_iota(jnp.int32, cs_ref.shape, 1)
        chunks = own // CHUNK
        for k in range(chunks):
            here = jnp.where(lane == place_ref[0] * chunks + k, cs_ref[...], 0.0)
            place = slice(k * CHUNK, (k + 1) * CHUNK)
            summed = acc[place, :] * jnp.sum(here, axis=1, keepdims=True)
            square = jnp.mean(summed * summed, axis=1, keepdims=True)
            out_ref[place, :] = (summed * lax.rsqrt(square + 1e-06)).astype(BF16)


def update(place, p, e_all, v_all, cs, own, gain):
    docs, width = e_all.shape
    return pl.pallas_call(
        functools.partial(update_kernel, gain),
        grid_spec=pltpu.PrefetchScalarGridSpec(
            num_scalar_prefetch=1,
            grid=(docs // UPDATE_DOCS,),
            in_specs=[
                pl.BlockSpec((own, width), lambda i, place: (place[0], 0)),
                pl.BlockSpec((UPDATE_DOCS, width), lambda i, place: (i, 0)),
                pl.BlockSpec((1, UPDATE_DOCS), lambda i, place: (0, i)),
                pl.BlockSpec(cs.shape, lambda i, place: (0, 0)),
            ],
            out_specs=pl.BlockSpec((own, width), lambda i, place: (0, 0)),
            scratch_shapes=[
                pltpu.VMEM((2, UPDATE_SUB, UPDATE_DOCS), F32),
                pltpu.VMEM((own, width), F32),
            ],
        ),
        out_shape=jax.ShapeDtypeStruct((own, width), BF16),
        compiler_params=params(),
    )(place, in_hbm(p), in_hbm(e_all), v_all, cs)


def swap(x, axis, bit):
    size = lax.axis_size(axis)
    return lax.ppermute(x, axis, [(i, i ^ bit) for i in range(size)])


def bits(axis):
    bit = 1
    while bit < lax.axis_size(axis):
        yield bit
        bit *= 2


def reduce_over(x, axis, combine):
    for bit in bits(axis):
        x = combine(x, swap(x, axis, bit))
    return x


def gather_over(x, axis):
    for bit in bits(axis):
        other = swap(x, axis, bit)
        upper = (lax.axis_index(axis) & bit) != 0
        x = jnp.where(
            upper,
            jnp.concatenate([other, x], axis=1),
            jnp.concatenate([x, other], axis=1),
        )
    return x


def log_add(a, b):
    top = jnp.maximum(a, b)
    return top + jnp.log2(jnp.exp2(a - top) + jnp.exp2(b - top))


def on_device(embeddings, prototypes):
    docs, width = embeddings.shape
    protos = prototypes.shape[0]
    doc_ranks = lax.axis_size("docs")
    total_docs = docs * doc_ranks
    total_protos = protos * lax.axis_size("protos")
    own = protos // doc_ranks
    gain = 4.0 / math.sqrt(width) / math.log(2.0)

    e_all = lax.all_gather(embeddings, "docs", tiled=True)
    num, shift, lse = stats(embeddings, in_hbm(prototypes), gain)
    num = in_vmem(num)
    lse = reduce_over(lse, "protos", log_add)
    w = jnp.exp2(shift - lse)
    weight = w
    for sweep_index in range(SWEEPS):
        col_total = reduce_over(columns(num, weight), "docs", jnp.add)
        cs = 1.0 / (total_protos * col_total)
        row_sum = reduce_over(row_sums(num, w, cs), "protos", jnp.add)
        r = 1.0 / (total_docs * row_sum)
        weight = w * r
    v_all = gather_over(jnp.log2(r * total_docs) - lse, "docs")
    place = lax.axis_index("docs").reshape(1).astype(jnp.int32)
    new_prototypes = update(place, prototypes, e_all, v_all, cs, own, gain)
    column_potential = jnp.log(total_docs * cs.T.reshape(-1)[:protos])
    row_potential = jnp.log(r).reshape(-1)
    return (new_prototypes, column_potential, row_potential)


def solution(mesh):
    placed = (P("docs", None), P("protos", None))
    return jax.shard_map(
        on_device,
        mesh=mesh,
        in_specs=placed,
        out_specs=(P(("protos", "docs"), None), P("protos"), P("docs")),
        check_vma=False,
    )
```

time: 204 us -> 242 us (1.19)
  Pallas kernels: 115 us -> 170 us
  waiting for transfers between devices: 40.4 us -> 29.2 us
  other arithmetic: 7.49 us -> 0.87 us
    pallas_call x5, Pallas kernels: 72.2 us -> 126 us  [the longest x1 105 us: stats(): pl.pallas_call(functools.partial(stats_kernel, gain), grid=(blocks,), in_...]
    ppermute x15, waiting for transfers between devices: 39.7 us -> 28.5 us  [swap(): return lax.ppermute(x, axis, [(i, i ^ bit) for i in range(size)])]
    add x6, other arithmetic: 3.34 us -> 0.05 us  [reduce_over(): x = combine(x, swap(x, axis, bit))]
  transfers between devices with their start and end apart: 16 -> 16, of which waited for: 15 -> 15; matrix products, arithmetic and copies ran while one was open for 4% -> 1% of each run, Pallas kernels for 35% -> 53%
where the time goes in v2:
time: 242 us; the launch traced here: 241 us
  Pallas kernels  170 us (70%)
  waiting for transfers between devices  29.2 us (12%)
  starting transfers between devices  25.6 us (11%)
  between operations  14.2 us (6%)
    pallas_call x1, Pallas kernels, stats(): pl.pallas_call(functools.partial(stats_kernel, gain), grid=(blocks,), in_...  105 us
    pallas_call x1, Pallas kernels, update(): pl.pallas_call(functools.partial(update_kernel, gain), grid_spec=pltpu.Pr...  43.6 us
    ppermute x15, waiting for transfers between devices, swap(): return lax.ppermute(x, axis, [(i, i ^ bit) for i in range(size)])  28.5 us
    ppermute x15, starting transfers between devices, swap(): return lax.ppermute(x, axis, [(i, i ^ bit) for i in range(size)])  25.6 us
    pallas_call x2, Pallas kernels, columns(): pl.pallas_call(columns_kernel, in_specs=[whole()] * 2, out_specs=whole(),...  11.2 us
    pallas_call x2, Pallas kernels, row_sums(): pl.pallas_call(rows_kernel, in_specs=[whole()] * 3, out_specs=whole(), ou...  9.92 us
  transfers between devices with their start and end apart: 16, of which 15 were waited for; matrix products, arithmetic and copies ran while one was open for 1% of the time, Pallas kernels for 53%

profile of v2, /device:TPU:0, one launch (start us, length us, event | category | flops | bytes accessed | tf_op | source)
XLA Modules:
  0.0 240.7 jit_solution(6642478412919411455)
XLA Ops:
  7.2 0.0 all-gather.2.cloned.1.call-start
  7.2 0.7 all-gather.2.cloned.1.call-update
  7.9 105.4 %shard_map.49 = (bf16[16384,1024]{1,0:T(8,128)(2,1)S(1)}, f32[1,1024]{1,0:T(1,128)S(1)}, f32[1,1024]{1,0:T(1,128)S(1)}) custom-call(bf16[1024,512]{1,0:T(8,128)(2,1)} %e_ref.1, bf16[16384,512]{1,0:T(8,128)(2,1)} %p_ref.3, bf16[16384,512]{1,0:T(8,128)(2,1)} %p_ref.3), custom_call_target="tpu_custom_call" | custom-call | tf_op jit(solution)/shard_map/pallas_call | solution.py:104
  113.3 2.9 %collective-permute-start = (f32[1,1024]{1,0:T(1,128)S(1)}, f32[1,1024]{1,0:T(1,128)S(1)}, u32[]{:S(2)}, u32[]{:S(2)}) collective-permute-start(f32[1,1024]{1,0:T(1,128)S(1)} %get-tuple-element.8), channel_id=1, source_target_pairs={{0,1},{1,0},{2,3},{3,2},{4,5},{5,4},{6,7},{7,6},{8,9},{9,8},{10,11... | collective-permute-start | bytes 12296 | tf_op jit(solution)/shard_map/ppermute | solution.py:290
  116.2 1.6 collective-permute-done
  117.8 2.1 collective-permute-start.1
  119.9 1.6 collective-permute-done.1
  121.6 5.6 %shard_map.50 = f32[128,128]{1,0:T(8,128)S(1)} custom-call(bf16[16384,1024]{1,0:T(8,128)(2,1)S(1)} %get-tuple-element.6.num_ref, f32[1,1024]{1,0:T(1,128)S(1)} %get-tuple-element.13.w_ref), custom_call_target="tpu_custom_call" | custom-call | tf_op jit(solution)/shard_map/pallas_call | solution.py:168
  127.2 0.1 collective-permute-start.2
  127.2 1.2 collective-permute-done.2
  128.5 1.7 collective-permute-start.3
  130.2 2.6 %collective-permute-done.3 = f32[128,128]{1,0:T(8,128)S(1)} collective-permute-done((f32[128,128]{1,0:T(8,128)S(1)}, f32[128,128]{1,0:T(8,128)S(1)}, u32[]{:S(2)}, u32[]{:S(2)}) %collective-permute-start.3) | collective-permute-done | bytes 65568 | tf_op jit(solution)/shard_map/ppermute | solution.py:290
  132.8 3.0 %collective-permute-start.4 = (f32[128,128]{1,0:T(8,128)S(1)}, f32[128,128]{1,0:T(8,128)S(1)}, u32[]{:S(2)}, u32[]{:S(2)}) collective-permute-start(f32[128,128]{1,0:T(8,128)S(1)} %add.47), channel_id=1, source_target_pairs={{0,16},{4,20},{8,24},{12,28},{16,0},{20,4},{24,8},{28,12},{1,17},{... | collective-permute-start | bytes 196616 | tf_op jit(solution)/shard_map/ppermute | solution.py:290
  135.8 2.6 %collective-permute-done.4 = f32[128,128]{1,0:T(8,128)S(1)} collective-permute-done((f32[128,128]{1,0:T(8,128)S(1)}, f32[128,128]{1,0:T(8,128)S(1)}, u32[]{:S(2)}, u32[]{:S(2)}) %collective-permute-start.4) | collective-permute-done | bytes 65568 | tf_op jit(solution)/shard_map/ppermute | solution.py:290
  138.5 5.0 %shard_map.51 = f32[1,1024]{1,0:T(1,128)S(1)} custom-call(bf16[16384,1024]{1,0:T(8,128)(2,1)S(1)} %get-tuple-element.6.num_ref, f32[1,1024]{1,0:T(1,128)S(1)} %get-tuple-element.13.w_ref, f32[128,128]{1,0:T(8,128)S(1)} %multiply_divide_fusion.1.cs_ref), custom_call_target="tpu_custom_call" | custom-call | tf_op jit(solution)/shard_map/pallas_call | solution.py:216
  143.4 1.7 collective-permute-start.5
  145.1 2.0 collective-permute-done.5
  147.1 1.6 collective-permute-start.6
  148.8 2.0 collective-permute-done.6
  150.7 5.6 %shard_map.52 = f32[128,128]{1,0:T(8,128)S(1)} custom-call(bf16[16384,1024]{1,0:T(8,128)(2,1)S(1)} %get-tuple-element.6.num_ref, f32[1,1024]{1,0:T(1,128)S(1)} %divide_multiply_fusion.w_ref), custom_call_target="tpu_custom_call" | custom-call | tf_op jit(solution)/shard_map/pallas_call | solution.py:168
  156.3 0.1 collective-permute-start.7
  156.4 1.2 collective-permute-done.7
  157.7 1.6 collective-permute-start.8
  159.2 2.8 %collective-permute-done.8 = f32[128,128]{1,0:T(8,128)S(1)} collective-permute-done((f32[128,128]{1,0:T(8,128)S(1)}, f32[128,128]{1,0:T(8,128)S(1)}, u32[]{:S(2)}, u32[]{:S(2)}) %collective-permute-start.8) | collective-permute-done | bytes 65568 | tf_op jit(solution)/shard_map/ppermute | solution.py:290
  162.0 2.9 %collective-permute-start.9 = (f32[128,128]{1,0:T(8,128)S(1)}, f32[128,128]{1,0:T(8,128)S(1)}, u32[]{:S(2)}, u32[]{:S(2)}) collective-permute-start(f32[128,128]{1,0:T(8,128)S(1)} %add.52), channel_id=1, source_target_pairs={{0,16},{4,20},{8,24},{12,28},{16,0},{20,4},{24,8},{28,12},{1,17},{... | collective-permute-start | bytes 196616 | tf_op jit(solution)/shard_map/ppermute | solution.py:290
  164.9 2.6 %collective-permute-done.9 = f32[128,128]{1,0:T(8,128)S(1)} collective-permute-done((f32[128,128]{1,0:T(8,128)S(1)}, f32[128,128]{1,0:T(8,128)S(1)}, u32[]{:S(2)}, u32[]{:S(2)}) %collective-permute-start.9) | collective-permute-done | bytes 65568 | tf_op jit(solution)/shard_map/ppermute | solution.py:290
  167.6 5.0 %shard_map.53 = f32[1,1024]{1,0:T(1,128)S(1)} custom-call(bf16[16384,1024]{1,0:T(8,128)(2,1)S(1)} %get-tuple-element.6.num_ref, f32[1,1024]{1,0:T(1,128)S(1)} %get-tuple-element.13.w_ref, f32[128,128]{1,0:T(8,128)S(1)} %get-tuple-element.12.cs_ref), custom_call_target="tpu_custom_call" | custom-call | tf_op jit(solution)/shard_map/pallas_call | solution.py:216
  172.5 1.8 collective-permute-start.10
  174.3 1.9 collective-permute-done.10
  176.2 1.7 collective-permute-start.11
  177.9 1.9 collective-permute-done.11
  179.8 0.6 fusion.2
  180.5 0.1 collective-permute-start.12
  180.5 0.7 copy.5
  181.3 0.4 collective-permute-done.12
  181.7 1.6 collective-permute-start.13
  183.3 2.2 collective-permute-done.13
  185.4 2.8 %collective-permute-start.14 = (f32[1,4096]{1,0:T(1,128)S(1)}, f32[1,4096]{1,0:T(1,128)S(1)}, u32[]{:S(2)}, u32[]{:S(2)}) collective-permute-start(f32[1,4096]{1,0:T(1,128)S(1)} %broadcast_select_fusion.1), channel_id=1, source_target_pairs={{0,16},{4,20},{8,24},{12,28},{16,0},{20,4},{24,8},{28,12},{1,17},{... | collective-permute-start | bytes 49160 | tf_op jit(solution)/shard_map/ppermute | solution.py:290
  188.2 1.9 collective-permute-done.14
  190.2 0.0 all-gather.2.cloned.1.call-done.e_ref
  190.2 43.6 %shard_map.54 = bf16[2048,512]{1,0:T(8,128)(2,1)} custom-call(s32[1]{0:T(128)} %bitcast.place_ref, bf16[16384,512]{1,0:T(8,128)(2,1)} %p_ref.3, bf16[8192,512]{1,0:T(8,128)(2,1)} %all-gather.2.cloned.1.call-done.e_ref, f32[1,8192]{1,0:T(1,128)S(1)} %broadcast_select_fusion.v_ref, f32[128,128]{1,0:T(8,128)S(1)} %get-tuple-element.12.cs_ref), custom_call_target="tpu_custom_call" | custom-call | tf_op jit(solution)/shard_map/pallas_call | solution.py:266
  (17 shorter events, 0.3 us)
Async XLA Ops:
  7.2 183.0 %all-gather.2.cloned.1.call-start = ((), (), s32[]{:S(2)}) async-start(), calls=%async_computation | async-start | bytes 9437184 | tf_op jit(solution)/shard_map/all_gather | solution.py:332
  113.3 4.5 %collective-permute-start = (f32[1,1024]{1,0:T(1,128)S(1)}, f32[1,1024]{1,0:T(1,128)S(1)}, u32[]{:S(2)}, u32[]{:S(2)}) collective-permute-start(f32[1,1024]{1,0:T(1,128)S(1)} %get-tuple-element.8), channel_id=1, source_target_pairs={{0,1},{1,0},{2,3},{3,2},{4,5},{5,4},{6,7},{7,6},{8,9},{9,8},{10,11... | collective-permute-start | bytes 12296 | tf_op jit(solution)/shard_map/ppermute | solution.py:290
  117.8 3.7 %collective-permute-start.1 = (f32[1,1024]{1,0:T(1,128)S(1)}, f32[1,1024]{1,0:T(1,128)S(1)}, u32[]{:S(2)}, u32[]{:S(2)}) collective-permute-start(f32[1,1024]{1,0:T(1,128)S(1)} %multiply_add_fusion.1), channel_id=1, source_target_pairs={{0,2},{1,3},{2,0},{3,1},{4,6},{5,7},{6,4},{7,5},{8,10},{9,11},{10,... | collective-permute-start | bytes 12296 | tf_op jit(solution)/shard_map/ppermute | solution.py:290
  127.2 1.3 collective-permute-start.2
  128.5 4.3 %collective-permute-start.3 = (f32[128,128]{1,0:T(8,128)S(1)}, f32[128,128]{1,0:T(8,128)S(1)}, u32[]{:S(2)}, u32[]{:S(2)}) collective-permute-start(f32[128,128]{1,0:T(8,128)S(1)} %add.46), channel_id=1, source_target_pairs={{0,8},{4,12},{8,0},{12,4},{16,24},{20,28},{24,16},{28,20},{1,9},{5... | collective-permute-start | bytes 196616 | tf_op jit(solution)/shard_map/ppermute | solution.py:290
  132.8 5.6 %collective-permute-start.4 = (f32[128,128]{1,0:T(8,128)S(1)}, f32[128,128]{1,0:T(8,128)S(1)}, u32[]{:S(2)}, u32[]{:S(2)}) collective-permute-start(f32[128,128]{1,0:T(8,128)S(1)} %add.47), channel_id=1, source_target_pairs={{0,16},{4,20},{8,24},{12,28},{16,0},{20,4},{24,8},{28,12},{1,17},{... | collective-permute-start | bytes 196616 | tf_op jit(solution)/shard_map/ppermute | solution.py:290
  143.4 3.7 %collective-permute-start.5 = (f32[1,1024]{1,0:T(1,128)S(1)}, f32[1,1024]{1,0:T(1,128)S(1)}, u32[]{:S(2)}, u32[]{:S(2)}) collective-permute-start(f32[1,1024]{1,0:T(1,128)S(1)} %shard_map.51), channel_id=1, source_target_pairs={{0,1},{1,0},{2,3},{3,2},{4,5},{5,4},{6,7},{7,6},{8,9},{9,8},{10,11... | collective-permute-start | bytes 12296 | tf_op jit(solution)/shard_map/ppermute | solution.py:290
  147.1 3.6 %collective-permute-start.6 = (f32[1,1024]{1,0:T(1,128)S(1)}, f32[1,1024]{1,0:T(1,128)S(1)}, u32[]{:S(2)}, u32[]{:S(2)}) collective-permute-start(f32[1,1024]{1,0:T(1,128)S(1)} %add.49), channel_id=1, source_target_pairs={{0,2},{1,3},{2,0},{3,1},{4,6},{5,7},{6,4},{7,5},{8,10},{9,11},{10,... | collective-permute-start | bytes 12296 | tf_op jit(solution)/shard_map/ppermute | solution.py:290
  156.3 1.3 collective-permute-start.7
  157.7 4.3 %collective-permute-start.8 = (f32[128,128]{1,0:T(8,128)S(1)}, f32[128,128]{1,0:T(8,128)S(1)}, u32[]{:S(2)}, u32[]{:S(2)}) collective-permute-start(f32[128,128]{1,0:T(8,128)S(1)} %add.51), channel_id=1, source_target_pairs={{0,8},{4,12},{8,0},{12,4},{16,24},{20,28},{24,16},{28,20},{1,9},{5... | collective-permute-start | bytes 196616 | tf_op jit(solution)/shard_map/ppermute | solution.py:290
  162.0 5.5 %collective-permute-start.9 = (f32[128,128]{1,0:T(8,128)S(1)}, f32[128,128]{1,0:T(8,128)S(1)}, u32[]{:S(2)}, u32[]{:S(2)}) collective-permute-start(f32[128,128]{1,0:T(8,128)S(1)} %add.52), channel_id=1, source_target_pairs={{0,16},{4,20},{8,24},{12,28},{16,0},{20,4},{24,8},{28,12},{1,17},{... | collective-permute-start | bytes 196616 | tf_op jit(solution)/shard_map/ppermute | solution.py:290
  172.5 3.7 %collective-permute-start.10 = (f32[1,1024]{1,0:T(1,128)S(1)}, f32[1,1024]{1,0:T(1,128)S(1)}, u32[]{:S(2)}, u32[]{:S(2)}) collective-permute-start(f32[1,1024]{1,0:T(1,128)S(1)} %shard_map.53), channel_id=1, source_target_pairs={{0,1},{1,0},{2,3},{3,2},{4,5},{5,4},{6,7},{7,6},{8,9},{9,8},{10,11... | collective-permute-start | bytes 12296 | tf_op jit(solution)/shard_map/ppermute | solution.py:290
  176.2 3.6 %collective-permute-start.11 = (f32[1,1024]{1,0:T(1,128)S(1)}, f32[1,1024]{1,0:T(1,128)S(1)}, u32[]{:S(2)}, u32[]{:S(2)}) collective-permute-start(f32[1,1024]{1,0:T(1,128)S(1)} %add.54), channel_id=1, source_target_pairs={{0,2},{1,3},{2,0},{3,1},{4,6},{5,7},{6,4},{7,5},{8,10},{9,11},{10,... | collective-permute-start | bytes 12296 | tf_op jit(solution)/shard_map/ppermute | solution.py:290
  180.5 1.2 collective-permute-start.12
  181.7 3.7 %collective-permute-start.13 = (f32[1,2048]{1,0:T(1,128)S(1)}, f32[1,2048]{1,0:T(1,128)S(1)}, u32[]{:S(2)}, u32[]{:S(2)}) collective-permute-start(f32[1,2048]{1,0:T(1,128)S(1)} %broadcast_select_fusion.2), channel_id=1, source_target_pairs={{0,8},{4,12},{8,0},{12,4},{16,24},{20,28},{24,16},{28,20},{1,9},{5... | collective-permute-start | bytes 24584 | tf_op jit(solution)/shard_map/ppermute | solution.py:290
  185.4 4.7 %collective-permute-start.14 = (f32[1,4096]{1,0:T(1,128)S(1)}, f32[1,4096]{1,0:T(1,128)S(1)}, u32[]{:S(2)}, u32[]{:S(2)}) collective-permute-start(f32[1,4096]{1,0:T(1,128)S(1)} %broadcast_select_fusion.1), channel_id=1, source_target_pairs={{0,16},{4,20},{8,24},{12,28},{16,0},{20,4},{24,8},{28,12},{1,17},{... | collective-permute-start | bytes 49160 | tf_op jit(solution)/shard_map/ppermute | solution.py:290
Sparse Core Ops, SparseCore 0:
  9.6 84.7 all-gather.1

commit v3 on v2

--- a/solution.py
+++ b/solution.py
@@ -18,6 +18,8 @@
 COLUMN_GROUP = 32
 ROW_GROUP = 16
 ROW_TAKEN = 10
+OWN_FIRST = 128
+UPDATE_ROWS = 256
 F32 = jnp.float32
 BF16 = jnp.bfloat16
 
@@ -46,7 +48,7 @@
     return pl.ds(pl.multiple_of(index * size, size), size)
 
 
-def stats_kernel(gain, e_ref, p_ref, p_any, num_ref, shift_ref, lse_ref, total, p_buf):
+def stats_kernel(gain, place_ref, e_ref, p_ref, p_any, num_ref, shift_ref, lse_ref, own_ref, total, p_buf):
     step = pl.program_id(0)
     docs = e_ref.shape[0]
     tiles = [slice(d, d + DOC_TILE) for d in range(0, docs, DOC_TILE)]
@@ -66,6 +68,15 @@
         total[pl.ds(block, 1), :] = jnp.concatenate(sums, axis=1)
 
     fill(p_ref, step)
+    own = own_ref.shape[0]
+    count, per = max(own // BLOCK, 1), max(BLOCK // own, 1)
+    for j in range(count):
+
+        @pl.when(step == place_ref[0] * count // per + j)
+        def _():
+            offset = pl.multiple_of((place_ref[0] % per) * own, 16) if per > 1 else 0
+            size = min(own, BLOCK)
+            own_ref[j * size : (j + 1) * size, :] = p_ref[pl.ds(offset, size), :]
 
     @pl.when(step == pl.num_programs(0) - 1)
     def _():
@@ -97,30 +108,34 @@
         lse_ref[...] = shift + jnp.log2(found)
 
 
-def stats(e, p, gain):
+def stats(place, own, e, p, gain):
     docs, width = e.shape
     protos = p.shape[0]
     blocks = protos // BLOCK
     return pl.pallas_call(
         functools.partial(stats_kernel, gain),
-        grid=(blocks,),
-        in_specs=[
-            pl.BlockSpec((docs, width), lambda i: (0, 0)),
-            pl.BlockSpec((BLOCK, width), lambda i: (i, 0)),
-            pl.BlockSpec(memory_space=pl.ANY),
-        ],
-        out_specs=[whole(), whole(), whole()],
+        grid_spec=pltpu.PrefetchScalarGridSpec(
+            num_scalar_prefetch=1,
+            grid=(blocks,),
+            in_specs=[
+                pl.BlockSpec((docs, width), lambda i, place: (0, 0)),
+                pl.BlockSpec((BLOCK, width), lambda i, place: (i, 0)),
+                pl.BlockSpec(memory_space=pl.ANY),
+            ],
+            out_specs=[whole()] * 4,
+            scratch_shapes=[
+                pltpu.VMEM((blocks, docs), F32),
+                pltpu.VMEM((BLOCK, width), BF16),
+            ],
+        ),
         out_shape=[
             pltpu.VMEM((protos, docs), BF16),
             pltpu.VMEM((1, docs), F32),
             pltpu.VMEM((1, docs), F32),
-        ],
-        scratch_shapes=[
-            pltpu.VMEM((blocks, docs), F32),
-            pltpu.VMEM((BLOCK, width), BF16),
+            pltpu.VMEM((own, width), BF16),
         ],
         compiler_params=params(),
-    )(e, p, p)
+    )(place, e, p, p)
 
 
 def split(x):
@@ -131,7 +146,8 @@
     return [part.astype(F32) for part in (high, mid, low)]
 
 
-def columns_kernel(num_ref, w_ref, out_ref, turned):
+def columns_kernel(num_ref, w_ref, num_out, out_ref, turned):
+    del num_out
     docs = num_ref.shape[1]
     taken = turned.shape[0]
     w = w_ref[...]
@@ -168,14 +184,16 @@
     return pl.pallas_call(
         columns_kernel,
         in_specs=[whole()] * 2,
-        out_specs=whole(),
-        out_shape=pltpu.VMEM((CHUNK, chunk_lanes(protos)), F32),
+        out_specs=[whole()] * 2,
+        out_shape=[pltpu.VMEM(num.shape, BF16), pltpu.VMEM((CHUNK, chunk_lanes(protos)), F32)],
+        input_output_aliases={0: 0},
         scratch_shapes=[pltpu.VMEM((docs // 2, CHUNK), BF16)],
         compiler_params=params(),
     )(num, in_vmem(w))
 
 
-def rows_kernel(num_ref, w_ref, cs_ref, out_ref, parts):
+def rows_kernel(num_ref, w_ref, cs_ref, num_out, out_ref, parts):
+    del num_out
     docs = num_ref.shape[1]
     turned = cs_ref[...]
     for j, part in enumerate(split(turned.T)):
@@ -216,73 +234,107 @@
     return pl.pallas_call(
         rows_kernel,
         in_specs=[whole()] * 3,
-        out_specs=whole(),
-        out_shape=pltpu.VMEM((1, docs), F32),
+        out_specs=[whole()] * 2,
+        out_shape=[pltpu.VMEM(num.shape, BF16), pltpu.VMEM((1, docs), F32)],
+        input_output_aliases={0: 0},
         scratch_shapes=[pltpu.VMEM((3, cs.shape[1], CHUNK), F32)],
         compiler_params=params(),
     )(num, in_vmem(w), in_vmem(cs))
 
 
-UPDATE_DOCS = 512
-UPDATE_SUB = 256
-
-
-def update_kernel(gain, place_ref, p_ref, e_ref, v_ref, cs_ref, out_ref, scores, acc):
-    step = pl.program_id(0)
+def share_kernel(gain, rank_ref, e_ref, p_ref, x_ref, held_ref, num_ref, shift_ref, x_out, held_out):
+    del rank_ref, held_ref, held_out
+
+    @pl.when(pl.program_id(0) == 0)
+    def _():
+        x_out[...] = x_ref[...]
+
     own = p_ref.shape[0]
-    parts = own // UPDATE_SUB
-
-    @pl.when(step == 0)
+    first = transposed_dot(p_ref[:OWN_FIRST, :], e_ref[...])
+    shift = jnp.max(first, axis=0, keepdims=True)
+    num = jnp.exp2((transposed_dot(p_ref[...], e_ref[...]) - shift) * gain)
+    num_ref[...] = num.astype(BF16)
+    shift_ref[...] = shift * gain
+    found = jnp.sum(num, axis=0, keepdims=True)
+    fits = jnp.min(jnp.where(found < LARGE, 1.0, 0.0))
+
+    @pl.when(fits < 0.5)
     def _():
-        acc[...] = jnp.zeros_like(acc)
-
-    def score(k):
-        scores[k % 2] = transposed_dot(
-            p_ref[k * UPDATE_SUB : (k + 1) * UPDATE_SUB, :], e_ref[...]
-        )
-
-    score(0)
-    for k in range(parts):
-        if k + 1 < parts:
-            score(k + 1)
-        share = jnp.exp2(scores[k % 2] * gain + v_ref[...]).astype(BF16)
-        place = slice(k * UPDATE_SUB, (k + 1) * UPDATE_SUB)
-        acc[place, :] += jnp.dot(share, e_ref[...], preferred_element_type=F32)
-
-    @pl.when(step == pl.num_programs(0) - 1)
-    def _():
-        lane = lax.broadcasted_iota(jnp.int32, cs_ref.shape, 1)
-        chunks = own // CHUNK
-        for k in range(chunks):
-            here = jnp.where(lane == place_ref[0] * chunks + k, cs_ref[...], 0.0)
-            place = slice(k * CHUNK, (k + 1) * CHUNK)
-            summed = acc[place, :] * jnp.sum(here, axis=1, keepdims=True)
-            square = jnp.mean(summed * summed, axis=1, keepdims=True)
-            out_ref[place, :] = (summed * lax.rsqrt(square + 1e-06)).astype(BF16)
-
-
-def update(place, p, e_all, v_all, cs, own, gain):
-    docs, width = e_all.shape
+        scores = transposed_dot(p_ref[...], e_ref[...])
+        peak = jnp.max(scores, axis=0, keepdims=True)
+        num_ref[...] = jnp.exp2((scores - peak) * gain).astype(BF16)
+        shift_ref[...] = peak * gain
+
+
+def share(rank, docs, e, p_own, x, held, gain):
+    own, width = p_own.shape
+    tiles = docs // DOC_TILE
     return pl.pallas_call(
-        functools.partial(update_kernel, gain),
+        functools.partial(share_kernel, gain),
         grid_spec=pltpu.PrefetchScalarGridSpec(
             num_scalar_prefetch=1,
-            grid=(docs // UPDATE_DOCS,),
+            grid=(tiles,),
             in_specs=[
-                pl.BlockSpec((own, width), lambda i, place: (place[0], 0)),
-                pl.BlockSpec((UPDATE_DOCS, width), lambda i, place: (i, 0)),
-                pl.BlockSpec((1, UPDATE_DOCS), lambda i, place: (0, i)),
-                pl.BlockSpec(cs.shape, lambda i, place: (0, 0)),
+                pl.BlockSpec((DOC_TILE, width), lambda i, rank: (rank[0] * tiles + i, 0)),
+                whole(),
+                whole(),
+                whole(),
             ],
-            out_specs=pl.BlockSpec((own, width), lambda i, place: (0, 0)),
-            scratch_shapes=[
-                pltpu.VMEM((2, UPDATE_SUB, UPDATE_DOCS), F32),
-                pltpu.VMEM((own, width), F32),
+            out_specs=[
+                pl.BlockSpec((own, DOC_TILE), lambda i, rank: (0, i)),
+                pl.BlockSpec((1, DOC_TILE), lambda i, rank: (0, i)),
+                whole(),
+                whole(),
             ],
+        ),
+        out_shape=[
+            pltpu.HBM((own, docs), BF16),
+            pltpu.VMEM((1, docs), F32),
+            pltpu.VMEM(x.shape, F32),
+            pltpu.VMEM(held.shape, held.dtype),
+        ],
+        input_output_aliases={4: 3},
+        compiler_params=params(),
+    )(rank, e, in_vmem(p_own), in_vmem(x), in_vmem(held))
+
+
+def update_kernel(ranks, place_ref, e_ref, v_ref, cs_ref, *refs):
+    nums, shifts, out_ref = refs[:ranks], refs[ranks : 2 * ranks], refs[2 * ranks]
+    rows, docs = nums[0].shape
+    summed = jnp.zeros(out_ref.shape, F32)
+    for k in range(ranks):
+        weight = jnp.exp2(shifts[k][...] + v_ref[:, k * docs : (k + 1) * docs])
+        scaled = (nums[k][...].astype(F32) * weight).astype(BF16)
+        held = e_ref[rows_of(jnp.bitwise_xor(place_ref[0], k), docs), :]
+        summed += jnp.dot(scaled, held, preferred_element_type=F32)
+    lane = lax.broadcasted_iota(jnp.int32, cs_ref.shape, 1)
+    chunks = rows // CHUNK
+    first = (place_ref[0] * pl.num_programs(0) + pl.program_id(0)) * chunks
+    for k in range(chunks):
+        here = jnp.where(lane == first + k, cs_ref[...], 0.0)
+        part = summed[k * CHUNK : (k + 1) * CHUNK] * jnp.sum(here, axis=1, keepdims=True)
+        square = jnp.mean(part * part, axis=1, keepdims=True)
+        out_ref[k * CHUNK : (k + 1) * CHUNK, :] = (part * lax.rsqrt(square + 1e-06)).astype(BF16)
+
+
+def update(place, e_all, v, cs, nums, shifts):
+    ranks = len(nums)
+    own, docs = nums[0].shape
+    width = e_all.shape[1]
+    rows = min(UPDATE_ROWS, own)
+    return pl.pallas_call(
+        functools.partial(update_kernel, ranks),
+        grid_spec=pltpu.PrefetchScalarGridSpec(
+            num_scalar_prefetch=1,
+            grid=(own // rows,),
+            in_specs=[whole()] * 3
+            + [pl.BlockSpec((rows, docs), lambda i, place: (i, 0))] * ranks
+            + [whole()] * ranks,
+            out_specs=pl.BlockSpec((rows, width), lambda i, place: (i, 0)),
         ),
         out_shape=jax.ShapeDtypeStruct((own, width), BF16),
         compiler_params=params(),
-    )(place, in_hbm(p), in_hbm(e_all), v_all, cs)
+    )(place, in_vmem(e_all), in_vmem(v), in_vmem(cs), *[in_hbm(num) for num in nums], *shifts)
 
 
 def swap(x, axis, bit):
@@ -297,21 +349,21 @@
         bit *= 2
 
 
-def reduce_over(x, axis, combine):
-    for bit in bits(axis):
-        x = combine(x, swap(x, axis, bit))
-    return x
-
-
-def gather_over(x, axis):
+def reduce_over(x, axis, combine, jobs={}):
     for bit in bits(axis):
         other = swap(x, axis, bit)
-        upper = (lax.axis_index(axis) & bit) != 0
-        x = jnp.where(
-            upper,
-            jnp.concatenate([other, x], axis=1),
-            jnp.concatenate([x, other], axis=1),
-        )
+        for job in jobs.get(bit, ()):
+            x = job(x)
+        x = combine(x, other)
+    return x
+
+
+def gather_over(x, axis, jobs={}):
+    for bit in bits(axis):
+        other = swap(x, axis, bit)
+        for job in jobs.get(bit, ()):
+            x = job(x)
+        x = jnp.concatenate([x, other], axis=1)
     return x
 
 
@@ -329,21 +381,60 @@
     own = protos // doc_ranks
     gain = 4.0 / math.sqrt(width) / math.log(2.0)
 
+    place = lax.axis_index("docs").astype(jnp.int32)
+
     e_all = lax.all_gather(embeddings, "docs", tiled=True)
-    num, shift, lse = stats(embeddings, in_hbm(prototypes), gain)
-    num = in_vmem(num)
+    partner = swap(embeddings, "docs", 1)
+    state = [None, None]
+    nums, shifts = [None] * doc_ranks, [None] * doc_ranks
+
+    def job_of(k, kept=True):
+        def job(x):
+            source, rank = (embeddings, partner, e_all)[min(k, 2)], place ^ k if k > 1 else 0 * place
+            source = in_hbm(source) if k != 1 else source
+            held = state[0] if kept else jnp.zeros((8, CHUNK), F32)
+            nums[k], shifts[k], x, held = share(
+                rank.reshape(1), docs, source, state[1], x, held, gain
+            )
+            if kept:
+                state[0] = held
+            return x
+
+        return job
+
+    doc_bits, proto_bits = list(bits("docs")), list(bits("protos"))
+    early = {bit: [] for bit in doc_bits}
+    column_jobs = {doc_bits[-1]: []}
+    row_jobs = {bit: [] for bit in proto_bits}
+    gather_jobs = {bit: [] for bit in doc_bits}
+    for k in range(2):
+        early[doc_bits[1 + k % (len(doc_bits) - 1)]].append(job_of(k))
+    late = list(row_jobs.values())
+    late += [gather_jobs[bit] for bit in doc_bits[1:]]
+    rest = list(range(2, doc_ranks))
+    for i, slot in enumerate(late):
+        slot.extend(job_of(k, False) for k in rest[i :: len(late)])
+
+    num, shift, lse, own_table = stats(
+        place.reshape(1), own, in_hbm(embeddings), in_hbm(prototypes), gain
+    )
+    state[1] = own_table
+    state[0] = num
     lse = reduce_over(lse, "protos", log_add)
     w = jnp.exp2(shift - lse)
     weight = w
     for sweep_index in range(SWEEPS):
-        col_total = reduce_over(columns(num, weight), "docs", jnp.add)
+        last = sweep_index == SWEEPS - 1
+        beside = column_jobs if last else (early if sweep_index == 0 else {})
+        state[0], col_local = columns(in_vmem(state[0]), weight)
+        col_total = reduce_over(col_local, "docs", jnp.add, beside)
         cs = 1.0 / (total_protos * col_total)
-        row_sum = reduce_over(row_sums(num, w, cs), "protos", jnp.add)
+        state[0], row_local = row_sums(in_vmem(state[0]), w, cs)
+        row_sum = reduce_over(row_local, "protos", jnp.add, row_jobs if last else {})
         r = 1.0 / (total_docs * row_sum)
         weight = w * r
-    v_all = gather_over(jnp.log2(r * total_docs) - lse, "docs")
-    place = lax.axis_index("docs").reshape(1).astype(jnp.int32)
-    new_prototypes = update(place, prototypes, e_all, v_all, cs, own, gain)
+    v = gather_over(jnp.log2(r * total_docs) - lse, "docs", gather_jobs)
+    new_prototypes = update(place.reshape(1), e_all, v, cs, nums, shifts)
     column_potential = jnp.log(total_docs * cs.T.reshape(-1)[:protos])
     row_potential = jnp.log(r).reshape(-1)
     return (new_prototypes, column_potential, row_potential)

time: 242 us -> 269 us (1.11); the launches traced: 241 us -> 264 us
  Pallas kernels: 170 us -> 206 us
  waiting for transfers between devices: 29.2 us -> 16.1 us
  local copies, waits for them, and re-layouts: 0.73 us -> 5.09 us
  starting transfers between devices: 25.6 us -> 21.4 us
    pallas_call x6 -> x14, Pallas kernels: 170 us -> 206 us  [the longest x1 106 us: stats(): pl.pallas_call(functools.partial(stats_kernel, gain), grid_spec=pltpu.Pre...]
    ppermute x15 -> x16, waiting for transfers between devices: 28.5 us -> 15.4 us  [swap(): return lax.ppermute(x, axis, [(i, i ^ bit) for i in range(size)])]
    unnamed x0 -> x5, local copies, waits for them, and re-layouts: none -> 4.35 us
    ppermute x15 -> x16, starting transfers between devices: 25.6 us -> 21.3 us  [swap(): return lax.ppermute(x, axis, [(i, i ^ bit) for i in range(size)])]
  transfers between devices with their start and end apart: 16 -> 17, of which waited for: 15 -> 9; matrix products, arithmetic and copies ran while one was open for 1% -> 0% of each run, Pallas kernels for 53% -> 69%
where the time goes in v3:
time: 269 us; the launch traced here: 264 us
  Pallas kernels  206 us (77%)
  starting transfers between devices  21.4 us (8%)
  waiting for transfers between devices  16.1 us (6%)
  between operations  14.2 us (5%)
  local copies, waits for them, and re-layouts  5.09 us (2%)
    pallas_call x1, Pallas kernels, stats(): pl.pallas_call(functools.partial(stats_kernel, gain), grid_spec=pltpu.Pre...  106 us
    pallas_call x8, Pallas kernels, share(): pl.pallas_call(functools.partial(share_kernel, gain), grid_spec=pltpu.Pre...  56 us
    pallas_call x1, Pallas kernels, update(): pl.pallas_call(functools.partial(update_kernel, ranks), grid_spec=pltpu.P...  23.3 us
    ppermute x16, starting transfers between devices, swap(): return lax.ppermute(x, axis, [(i, i ^ bit) for i in range(size)])  21.3 us
    ppermute x16, waiting for transfers between devices, swap(): return lax.ppermute(x, axis, [(i, i ^ bit) for i in range(size)])  15.4 us
    pallas_call x2, Pallas kernels, columns(): pl.pallas_call(columns_kernel, in_specs=[whole()] * 2, out_specs=[whole()...  11.2 us
    pallas_call x2, Pallas kernels, row_sums(): pl.pallas_call(rows_kernel, in_specs=[whole()] * 3, out_specs=[whole()] *...  10.1 us
  transfers between devices with their start and end apart: 17, of which 9 were waited for; matrix products, arithmetic and copies ran while one was open for 0% of the time, Pallas kernels for 69%

profile of v3, /device:TPU:0, one launch (start us, length us, event | category | flops | bytes accessed | tf_op | source)
XLA Modules:
  0.0 263.8 jit_solution(10267316668980319249)
XLA Ops:
  7.2 0.0 all-gather.2.cloned.1.call-start
  7.2 0.7 all-gather.2.cloned.1.call-update
  7.9 0.5 collective-permute-start
  8.4 105.7 %shard_map.49 = (bf16[16384,1024]{1,0:T(8,128)(2,1)S(1)}, f32[1,1024]{1,0:T(1,128)S(1)}, f32[1,1024]{1,0:T(1,128)S(1)}, bf16[2048,512]{1,0:T(8,128)(2,1)S(1)}) custom-call(s32[1]{0:T(128)} %bitcast.place_ref, bf16[1024,512]{1,0:T(8,128)(2,1)} %e_ref.3, bf16[16384,512]{1,0:T(8,128)(2,1)} %p_any.1, bf16[16384,512]{1,0:T(8,128)(2,1)} %p_any.1), custom_call_target="tpu_custom_call" | custom-call | tf_op jit(solution)/shard_map/pallas_call | solution.py:115
  114.1 2.6 collective-permute-start.1
  116.7 1.6 collective-permute-done.1
  118.3 2.1 collective-permute-start.2
  120.4 1.6 collective-permute-done.2
  122.0 5.6 %shard_map.50 = (bf16[16384,1024]{1,0:T(8,128)(2,1)S(1)}, f32[128,128]{1,0:T(8,128)S(1)}) custom-call(bf16[16384,1024]{1,0:T(8,128)(2,1)S(1)} %get-tuple-element.41.num_ref, f32[1,1024]{1,0:T(1,128)S(1)} %get-tuple-element.81.w_ref), custom_call_target="tpu_custom_call", output_to_operand_aliasing={{0}: (0, {})} | custom-call | tf_op jit(solution)/shard_map/pallas_call | solution.py:184
  127.6 0.1 collective-permute-start.3
  127.7 1.2 collective-permute-done.3
  128.9 2.2 collective-permute-start.4
  131.1 7.3 %shard_map.51 = (bf16[2048,1024]{1,0:T(8,128)(2,1)}, f32[1,1024]{1,0:T(1,128)S(1)}, f32[128,128]{1,0:T(8,128)S(1)}, bf16[16384,1024]{1,0:T(8,128)(2,1)S(1)}) custom-call(s32[1]{0:T(128)} %constant.9.clone.1.rank_ref, bf16[1024,512]{1,0:T(8,128)(2,1)} %e_ref.3, bf16[2048,512]{1,0:T(8,128)(2,1)S(1)} %get-tuple-element.40.p_ref, ...), custom_call_target="tpu_custom_call", output_to_operand_aliasing={{3}: (4, {})} | custom-call | tf_op jit(solution)/shard_map/pallas_call | solution.py:272
  138.4 0.0 collective-permute-done.4
  138.4 1.6 collective-permute-start.5
  140.0 0.0 collective-permute-done.e_ref
  140.0 0.0 copy-start.1
  140.0 1.0 copy-done.1
  141.0 6.2 %shard_map.52 = (bf16[2048,1024]{1,0:T(8,128)(2,1)}, f32[1,1024]{1,0:T(1,128)S(1)}, f32[128,128]{1,0:T(8,128)S(1)}, bf16[16384,1024]{1,0:T(8,128)(2,1)S(1)}) custom-call(s32[1]{0:T(128)} %constant.9.clone.1.rank_ref, bf16[1024,512]{1,0:T(8,128)(2,1)} %copy-done.1, bf16[2048,512]{1,0:T(8,128)(2,1)S(1)} %get-tuple-element.40.p_ref, ...), custom_call_target="tpu_custom_call", output_to_operand_aliasing={{3}: (4, {})} | custom-call | tf_op jit(solution)/shard_map/pallas_call | solution.py:272
  147.2 0.0 collective-permute-done.5
  147.2 5.0 %shard_map.53 = (bf16[16384,1024]{1,0:T(8,128)(2,1)S(1)}, f32[1,1024]{1,0:T(1,128)S(1)}) custom-call(bf16[16384,1024]{1,0:T(8,128)(2,1)S(1)} %get-tuple-element.48.num_ref, f32[1,1024]{1,0:T(1,128)S(1)} %get-tuple-element.81.w_ref, f32[128,128]{1,0:T(8,128)S(1)} %multiply_divide_fusion.1.cs_ref), custom_call_target="tpu_custom_call", output_to_operand_aliasing={{0}: (0, {})} | custom-call | tf_op jit(solution)/shard_map/pallas_call | solution.py:234
  152.2 2.7 %collective-permute-start.6 = (f32[1,1024]{1,0:T(1,128)S(1)}, f32[1,1024]{1,0:T(1,128)S(1)}, u32[]{:S(2)}, u32[]{:S(2)}) collective-permute-start(f32[1,1024]{1,0:T(1,128)S(1)} %get-tuple-element.51), channel_id=1, source_target_pairs={{0,1},{1,0},{2,3},{3,2},{4,5},{5,4},{6,7},{7,6},{8,9},{9,8},{10,11... | collective-permute-start | bytes 12296 | tf_op jit(solution)/shard_map/ppermute | solution.py:342
  154.9 1.6 collective-permute-done.6
  156.4 1.6 collective-permute-start.7
  158.0 2.0 collective-permute-done.7
  160.1 5.6 %shard_map.54 = (bf16[16384,1024]{1,0:T(8,128)(2,1)S(1)}, f32[128,128]{1,0:T(8,128)S(1)}) custom-call(bf16[16384,1024]{1,0:T(8,128)(2,1)S(1)} %get-tuple-element.50.num_ref, f32[1,1024]{1,0:T(1,128)S(1)} %divide_multiply_fusion.w_ref), custom_call_target="tpu_custom_call", output_to_operand_aliasing={{0}: (0, {})} | custom-call | tf_op jit(solution)/shard_map/pallas_call | solution.py:184
  165.7 0.1 collective-permute-start.8
  165.7 1.2 collective-permute-done.8
  167.0 2.1 collective-permute-start.9
  169.1 2.4 collective-permute-done.9
  171.6 2.7 %collective-permute-start.10 = (f32[128,128]{1,0:T(8,128)S(1)}, f32[128,128]{1,0:T(8,128)S(1)}, u32[]{:S(2)}, u32[]{:S(2)}) collective-permute-start(f32[128,128]{1,0:T(8,128)S(1)} %add.52), channel_id=1, source_target_pairs={{0,16},{4,20},{8,24},{12,28},{16,0},{20,4},{24,8},{28,12},{1,17},{... | collective-permute-start | bytes 196616 | tf_op jit(solution)/shard_map/ppermute | solution.py:342
  174.3 2.6 collective-permute-done.10
  176.9 5.1 %shard_map.55 = (bf16[16384,1024]{1,0:T(8,128)(2,1)S(1)}, f32[1,1024]{1,0:T(1,128)S(1)}) custom-call(bf16[16384,1024]{1,0:T(8,128)(2,1)S(1)} %get-tuple-element.52.num_ref, f32[1,1024]{1,0:T(1,128)S(1)} %get-tuple-element.81.w_ref, f32[128,128]{1,0:T(8,128)S(1)} %get-tuple-element.80.cs_ref), custom_call_target="tpu_custom_call", output_to_operand_aliasing={{0}: (0, {})} | custom-call | tf_op jit(solution)/shard_map/pallas_call | solution.py:234
  182.0 2.1 collective-permute-start.11
  184.1 0.0 all-gather.2.cloned.1.call-done.e_ref
  184.1 8.3 %shard_map.56 = (bf16[2048,1024]{1,0:T(8,128)(2,1)}, f32[1,1024]{1,0:T(1,128)S(1)}, f32[1,1024]{1,0:T(1,128)S(1)}, f32[8,128]{1,0:T(8,128)S(1)}) custom-call(s32[1]{0:T(128)} %bitcast.6.rank_ref, bf16[8192,512]{1,0:T(8,128)(2,1)} %all-gather.2.cloned.1.call-done.e_ref, ...), custom_call_target="tpu_custom_call", output_to_operand_aliasing={{3}: (4, {})} | custom-call | tf_op jit(solution)/shard_map/pallas_call | solution.py:272
  192.5 7.3 %shard_map.57 = (bf16[2048,1024]{1,0:T(8,128)(2,1)}, f32[1,1024]{1,0:T(1,128)S(1)}, f32[1,1024]{1,0:T(1,128)S(1)}, f32[8,128]{1,0:T(8,128)S(1)}) custom-call(s32[1]{0:T(128)} %bitcast.5.rank_ref, bf16[8192,512]{1,0:T(8,128)(2,1)} %all-gather.2.cloned.1.call-done.e_ref, ...), custom_call_target="tpu_custom_call", output_to_operand_aliasing={{3}: (4, {})} | custom-call | tf_op jit(solution)/shard_map/pallas_call | solution.py:272
  199.7 0.0 collective-permute-done.11
  199.7 0.1 collective-permute-start.12
  199.8 8.4 %shard_map.58 = (bf16[2048,1024]{1,0:T(8,128)(2,1)}, f32[1,1024]{1,0:T(1,128)S(1)}, f32[1,1024]{1,0:T(1,128)S(1)}, f32[8,128]{1,0:T(8,128)S(1)}) custom-call(s32[1]{0:T(128)} %bitcast.4.rank_ref, bf16[8192,512]{1,0:T(8,128)(2,1)} %all-gather.2.cloned.1.call-done.e_ref, ...), custom_call_target="tpu_custom_call", output_to_operand_aliasing={{3}: (4, {})} | custom-call | tf_op jit(solution)/shard_map/pallas_call | solution.py:272
  208.2 6.2 %shard_map.59 = (bf16[2048,1024]{1,0:T(8,128)(2,1)}, f32[1,1024]{1,0:T(1,128)S(1)}, f32[1,1024]{1,0:T(1,128)S(1)}, f32[8,128]{1,0:T(8,128)S(1)}) custom-call(s32[1]{0:T(128)} %bitcast.3.rank_ref, bf16[8192,512]{1,0:T(8,128)(2,1)} %all-gather.2.cloned.1.call-done.e_ref, ...), custom_call_target="tpu_custom_call", output_to_operand_aliasing={{3}: (4, {})} | custom-call | tf_op jit(solution)/shard_map/pallas_call | solution.py:272
  214.4 0.0 collective-permute-done.12
  214.4 0.6 fusion.2
  215.1 0.1 collective-permute-start.13
  215.1 1.2 collective-permute-done.13
  216.3 0.1 collective-permute-start.14
  216.4 6.2 %shard_map.60 = (bf16[2048,1024]{1,0:T(8,128)(2,1)}, f32[1,1024]{1,0:T(1,128)S(1)}, f32[1,2048]{1,0:T(1,128)S(1)}, f32[8,128]{1,0:T(8,128)S(1)}) custom-call(s32[1]{0:T(128)} %bitcast.2.rank_ref, bf16[8192,512]{1,0:T(8,128)(2,1)} %all-gather.2.cloned.1.call-done.e_ref, ...), custom_call_target="tpu_custom_call", output_to_operand_aliasing={{3}: (4, {})} | custom-call | tf_op jit(solution)/shard_map/pallas_call | solution.py:272
  222.6 0.0 collective-permute-done.14
  222.6 0.8 collective-permute-start.15
  223.4 0.7 copy.17
  224.1 6.2 %shard_map.61 = (bf16[2048,1024]{1,0:T(8,128)(2,1)}, f32[1,1024]{1,0:T(1,128)S(1)}, f32[1,4096]{1,0:T(1,128)S(1)}, f32[8,128]{1,0:T(8,128)S(1)}) custom-call(s32[1]{0:T(128)} %bitcast.1.rank_ref, bf16[8192,512]{1,0:T(8,128)(2,1)} %all-gather.2.cloned.1.call-done.e_ref, ...), custom_call_target="tpu_custom_call", output_to_operand_aliasing={{3}: (4, {})} | custom-call | tf_op jit(solution)/shard_map/pallas_call | solution.py:272
  230.3 0.0 collective-permute-done.15
  230.3 0.0 copy-start
  230.3 3.4 %copy-done = bf16[8192,512]{1,0:T(8,128)(2,1)S(1)} copy-done((bf16[8192,512]{1,0:T(8,128)(2,1)S(1)}, bf16[8192,512]{1,0:T(8,128)(2,1)}, u32[]{:S(2)}) %copy-start) | copy-done | bytes 8388632
  233.7 23.3 %shard_map.62 = bf16[2048,512]{1,0:T(8,128)(2,1)} custom-call(s32[1]{0:T(128)} %bitcast.place_ref, bf16[8192,512]{1,0:T(8,128)(2,1)S(1)} %copy-done, f32[1,8192]{1,0:T(1,128)S(1)} %pad_maximum_fusion.v_ref, f32[128,128]{1,0:T(8,128)S(1)} %get-tuple-element.80.cs_ref, bf16[2048,1024]{1,0:T(8,128)(2,1)} %get-tuple-element.61.refs_0_, ...), custom_call_target="tpu_custom_call" | custom-call | tf_op jit(solution)/shard_map/pallas_call | solution.py:325
  (22 shorter events, 0.3 us)
Async XLA Ops:
  7.2 177.0 %all-gather.2.cloned.1.call-start = ((), (), s32[]{:S(2)}) async-start(), calls=%async_computation | async-start | bytes 9437184 | tf_op jit(solution)/shard_map/all_gather | solution.py:386
  7.9 132.1 %collective-permute-start = (bf16[1024,512]{1,0:T(8,128)(2,1)}, bf16[1024,512]{1,0:T(8,128)(2,1)S(1)}, u32[]{:S(2)}, u32[]{:S(2)}) collective-permute-start(bf16[1024,512]{1,0:T(8,128)(2,1)} %e_ref.3), channel_id=1, source_target_pairs={{0,4},{4,0},{8,12},{12,8},{16,20},{20,16},{24,28},{28,24},{1,5},{5... | collective-permute-start | bytes 3145736 | tf_op jit(solution)/shard_map/ppermute | solution.py:342
  114.1 4.2 %collective-permute-start.1 = (f32[1,1024]{1,0:T(1,128)S(1)}, f32[1,1024]{1,0:T(1,128)S(1)}, u32[]{:S(2)}, u32[]{:S(2)}) collective-permute-start(f32[1,1024]{1,0:T(1,128)S(1)} %get-tuple-element.43), channel_id=1, source_target_pairs={{0,1},{1,0},{2,3},{3,2},{4,5},{5,4},{6,7},{7,6},{8,9},{9,8},{10,11... | collective-permute-start | bytes 12296 | tf_op jit(solution)/shard_map/ppermute | solution.py:342
  118.3 3.7 %collective-permute-start.2 = (f32[1,1024]{1,0:T(1,128)S(1)}, f32[1,1024]{1,0:T(1,128)S(1)}, u32[]{:S(2)}, u32[]{:S(2)}) collective-permute-start(f32[1,1024]{1,0:T(1,128)S(1)} %multiply_add_fusion.1), channel_id=1, source_target_pairs={{0,2},{1,3},{2,0},{3,1},{4,6},{5,7},{6,4},{7,5},{8,10},{9,11},{10,... | collective-permute-start | bytes 12296 | tf_op jit(solution)/shard_map/ppermute | solution.py:342
  127.6 1.3 collective-permute-start.3
  128.9 9.4 %collective-permute-start.4 = (f32[128,128]{1,0:T(8,128)S(1)}, f32[128,128]{1,0:T(8,128)S(1)}, u32[]{:S(2)}, u32[]{:S(2)}) collective-permute-start(f32[128,128]{1,0:T(8,128)S(1)} %add.46.x_ref), channel_id=1, source_target_pairs={{0,8},{4,12},{8,0},{12,4},{16,24},{20,28},{24,16},{28,20},{1,9},{5... | collective-permute-start | bytes 196616 | tf_op jit(solution)/shard_map/ppermute | solution.py:342
  138.4 8.8 %collective-permute-start.5 = (f32[128,128]{1,0:T(8,128)S(1)}, f32[128,128]{1,0:T(8,128)S(1)}, u32[]{:S(2)}, u32[]{:S(2)}) collective-permute-start(f32[128,128]{1,0:T(8,128)S(1)} %add.47.x_ref), channel_id=1, source_target_pairs={{0,16},{4,20},{8,24},{12,28},{16,0},{20,4},{24,8},{28,12},{1,17},{... | collective-permute-start | bytes 196616 | tf_op jit(solution)/shard_map/ppermute | solution.py:342
  140.0 1.0 copy-start.1
  152.2 4.3 %collective-permute-start.6 = (f32[1,1024]{1,0:T(1,128)S(1)}, f32[1,1024]{1,0:T(1,128)S(1)}, u32[]{:S(2)}, u32[]{:S(2)}) collective-permute-start(f32[1,1024]{1,0:T(1,128)S(1)} %get-tuple-element.51), channel_id=1, source_target_pairs={{0,1},{1,0},{2,3},{3,2},{4,5},{5,4},{6,7},{7,6},{8,9},{9,8},{10,11... | collective-permute-start | bytes 12296 | tf_op jit(solution)/shard_map/ppermute | solution.py:342
  156.4 3.6 %collective-permute-start.7 = (f32[1,1024]{1,0:T(1,128)S(1)}, f32[1,1024]{1,0:T(1,128)S(1)}, u32[]{:S(2)}, u32[]{:S(2)}) collective-permute-start(f32[1,1024]{1,0:T(1,128)S(1)} %add.49), channel_id=1, source_target_pairs={{0,2},{1,3},{2,0},{3,1},{4,6},{5,7},{6,4},{7,5},{8,10},{9,11},{10,... | collective-permute-start | bytes 12296 | tf_op jit(solution)/shard_map/ppermute | solution.py:342
  165.7 1.3 collective-permute-start.8
  167.0 4.6 %collective-permute-start.9 = (f32[128,128]{1,0:T(8,128)S(1)}, f32[128,128]{1,0:T(8,128)S(1)}, u32[]{:S(2)}, u32[]{:S(2)}) collective-permute-start(f32[128,128]{1,0:T(8,128)S(1)} %add.51), channel_id=1, source_target_pairs={{0,8},{4,12},{8,0},{12,4},{16,24},{20,28},{24,16},{28,20},{1,9},{5... | collective-permute-start | bytes 196616 | tf_op jit(solution)/shard_map/ppermute | solution.py:342
  171.6 5.3 %collective-permute-start.10 = (f32[128,128]{1,0:T(8,128)S(1)}, f32[128,128]{1,0:T(8,128)S(1)}, u32[]{:S(2)}, u32[]{:S(2)}) collective-permute-start(f32[128,128]{1,0:T(8,128)S(1)} %add.52), channel_id=1, source_target_pairs={{0,16},{4,20},{8,24},{12,28},{16,0},{20,4},{24,8},{28,12},{1,17},{... | collective-permute-start | bytes 196616 | tf_op jit(solution)/shard_map/ppermute | solution.py:342
  182.0 17.7 %collective-permute-start.11 = (f32[1,1024]{1,0:T(1,128)S(1)}, f32[1,1024]{1,0:T(1,128)S(1)}, u32[]{:S(2)}, u32[]{:S(2)}) collective-permute-start(f32[1,1024]{1,0:T(1,128)S(1)} %get-tuple-element.54.x_ref), channel_id=1, source_target_pairs={{0,1},{1,0},{2,3},{3,2},{4,5},{5,4},{6,7},{7,6},{8,9},{9,8},{10,11... | collective-permute-start | bytes 12296 | tf_op jit(solution)/shard_map/ppermute | solution.py:342
  199.7 14.7 %collective-permute-start.12 = (f32[1,1024]{1,0:T(1,128)S(1)}, f32[1,1024]{1,0:T(1,128)S(1)}, u32[]{:S(2)}, u32[]{:S(2)}) collective-permute-start(f32[1,1024]{1,0:T(1,128)S(1)} %add.54.x_ref), channel_id=1, source_target_pairs={{0,2},{1,3},{2,0},{3,1},{4,6},{5,7},{6,4},{7,5},{8,10},{9,11},{10,... | collective-permute-start | bytes 12296 | tf_op jit(solution)/shard_map/ppermute | solution.py:342
  215.1 1.2 collective-permute-start.13
  216.3 6.3 %collective-permute-start.14 = (f32[1,2048]{1,0:T(1,128)S(1)}, f32[1,2048]{1,0:T(1,128)S(1)}, u32[]{:S(2)}, u32[]{:S(2)}) collective-permute-start(f32[1,2048]{1,0:T(1,128)S(1)} %pad_maximum_fusion.1.x_ref), channel_id=1, source_target_pairs={{0,8},{4,12},{8,0},{12,4},{16,24},{20,28},{24,16},{28,20},{1,9},{5... | collective-permute-start | bytes 24584 | tf_op jit(solution)/shard_map/ppermute | solution.py:342
  222.6 7.7 %collective-permute-start.15 = (f32[1,4096]{1,0:T(1,128)S(1)}, f32[1,4096]{1,0:T(1,128)S(1)}, u32[]{:S(2)}, u32[]{:S(2)}) collective-permute-start(f32[1,4096]{1,0:T(1,128)S(1)} %constant_dynamic-update-slice_fusion.x_ref), channel_id=1, source_target_pairs={{0,16},{4,20},{8,24},{12,28},{16,0},{20,4},{24,8},{28,12},{1,17},{... | collective-permute-start | bytes 49160 | tf_op jit(solution)/shard_map/ppermute | solution.py:342
  230.3 3.4 %copy-start = (bf16[8192,512]{1,0:T(8,128)(2,1)S(1)}, bf16[8192,512]{1,0:T(8,128)(2,1)}, u32[]{:S(2)}) copy-start(bf16[8192,512]{1,0:T(8,128)(2,1)} %all-gather.2.cloned.1.call-done.e_ref) | copy-start | bytes 25165828
Sparse Core Ops, SparseCore 0:
  9.6 84.7 all-gather.1

commit v4 on v3

--- a/solution.py
+++ b/solution.py
@@ -19,7 +19,8 @@
 ROW_GROUP = 16
 ROW_TAKEN = 10
 OWN_FIRST = 128
-UPDATE_ROWS = 256
+UPDATE_ROWS = 512
+HELD = 2
 F32 = jnp.float32
 BF16 = jnp.bfloat16
 
@@ -242,14 +243,13 @@
     )(num, in_vmem(w), in_vmem(cs))
 
 
-def share_kernel(gain, rank_ref, e_ref, p_ref, x_ref, held_ref, num_ref, shift_ref, x_out, held_out):
-    del rank_ref, held_ref, held_out
+def share_kernel(gain, e_ref, p_ref, x_ref, held_ref, num_ref, shift_ref, x_out, held_out):
+    del held_ref, held_out
 
     @pl.when(pl.program_id(0) == 0)
     def _():
         x_out[...] = x_ref[...]
 
-    own = p_ref.shape[0]
     first = transposed_dot(p_ref[:OWN_FIRST, :], e_ref[...])
     shift = jnp.max(first, axis=0, keepdims=True)
     num = jnp.exp2((transposed_dot(p_ref[...], e_ref[...]) - shift) * gain)
@@ -266,75 +266,121 @@
         shift_ref[...] = peak * gain
 
 
-def share(rank, docs, e, p_own, x, held, gain):
-    own, width = p_own.shape
-    tiles = docs // DOC_TILE
+def share(e, p_own, x, held, gain):
+    docs, width = e.shape
+    own = p_own.shape[0]
     return pl.pallas_call(
         functools.partial(share_kernel, gain),
-        grid_spec=pltpu.PrefetchScalarGridSpec(
-            num_scalar_prefetch=1,
-            grid=(tiles,),
-            in_specs=[
-                pl.BlockSpec((DOC_TILE, width), lambda i, rank: (rank[0] * tiles + i, 0)),
-                whole(),
-                whole(),
-                whole(),
-            ],
-            out_specs=[
-                pl.BlockSpec((own, DOC_TILE), lambda i, rank: (0, i)),
-                pl.BlockSpec((1, DOC_TILE), lambda i, rank: (0, i)),
-                whole(),
-                whole(),
-            ],
-        ),
+        grid=(docs // DOC_TILE,),
+        in_specs=[pl.BlockSpec((DOC_TILE, width), lambda i: (i, 0))] + [whole()] * 3,
+        out_specs=[
+            pl.BlockSpec((own, DOC_TILE), lambda i: (0, i)),
+            pl.BlockSpec((1, DOC_TILE), lambda i: (0, i)),
+            whole(),
+            whole(),
+        ],
         out_shape=[
             pltpu.HBM((own, docs), BF16),
             pltpu.VMEM((1, docs), F32),
             pltpu.VMEM(x.shape, F32),
             pltpu.VMEM(held.shape, held.dtype),
         ],
-        input_output_aliases={4: 3},
+        input_output_aliases={3: 3},
         compiler_params=params(),
-    )(rank, e, in_vmem(p_own), in_vmem(x), in_vmem(held))
-
-
-def update_kernel(ranks, place_ref, e_ref, v_ref, cs_ref, *refs):
-    nums, shifts, out_ref = refs[:ranks], refs[ranks : 2 * ranks], refs[2 * ranks]
-    rows, docs = nums[0].shape
-    summed = jnp.zeros(out_ref.shape, F32)
-    for k in range(ranks):
-        weight = jnp.exp2(shifts[k][...] + v_ref[:, k * docs : (k + 1) * docs])
-        scaled = (nums[k][...].astype(F32) * weight).astype(BF16)
-        held = e_ref[rows_of(jnp.bitwise_xor(place_ref[0], k), docs), :]
-        summed += jnp.dot(scaled, held, preferred_element_type=F32)
-    lane = lax.broadcasted_iota(jnp.int32, cs_ref.shape, 1)
-    chunks = rows // CHUNK
-    first = (place_ref[0] * pl.num_programs(0) + pl.program_id(0)) * chunks
-    for k in range(chunks):
-        here = jnp.where(lane == first + k, cs_ref[...], 0.0)
-        part = summed[k * CHUNK : (k + 1) * CHUNK] * jnp.sum(here, axis=1, keepdims=True)
-        square = jnp.mean(part * part, axis=1, keepdims=True)
-        out_ref[k * CHUNK : (k + 1) * CHUNK, :] = (part * lax.rsqrt(square + 1e-06)).astype(BF16)
-
-
-def update(place, e_all, v, cs, nums, shifts):
-    ranks = len(nums)
-    own, docs = nums[0].shape
-    width = e_all.shape[1]
-    rows = min(UPDATE_ROWS, own)
+    )(e, in_vmem(p_own), in_vmem(x), in_vmem(held))
+
+
+def update_kernel(gain, place_ref, e_ref, v_ref, p_ref, cs_ref, *refs):
+    nums, shifts = refs[:HELD], refs[HELD : 2 * HELD]
+    out_ref, scores, acc, held, arrived = refs[2 * HELD :]
+    step = pl.program_id(0)
+    fresh = pl.num_programs(0) - HELD
+    own = p_ref.shape[0]
+    size = scores.shape[1]
+    places = [slice(d, d + size) for d in range(0, own, size)]
+
+    def add(place, part):
+        acc[place, :] += jnp.dot(part.astype(BF16), e_ref[...], preferred_element_type=F32)
+
+    @pl.when(step == 0)
+    def _():
+        acc[...] = jnp.zeros_like(acc)
+        for k in range(HELD):
+            pltpu.make_async_copy(nums[k], held.at[k], arrived.at[k]).start()
+
+    for k in range(HELD):
+
+        @pl.when(step == fresh + k)
+        def _():
+            pltpu.make_async_copy(nums[k], held.at[k], arrived.at[k]).wait()
+            weight = jnp.exp2(shifts[k][...] + v_ref[...])
+            for place in places:
+                add(place, held[k, place, :].astype(F32) * weight)
+
+    @pl.when(step < fresh)
+    def _():
+        def score(j):
+            scores[j % 2] = transposed_dot(p_ref[places[j], :], e_ref[...])
+
+        score(0)
+        for j in range(len(places)):
+            if j + 1 < len(places):
+                score(j + 1)
+            add(places[j], jnp.exp2(scores[j % 2] * gain + v_ref[...]))
+
+    @pl.when(step == pl.num_programs(0) - 1)
+    def _():
+        lane = lax.broadcasted_iota(jnp.int32, cs_ref.shape, 1)
+        chunks = own // CHUNK
+        for k in range(chunks):
+            here = jnp.where(lane == place_ref[0] * chunks + k, cs_ref[...], 0.0)
+            place = slice(k * CHUNK, (k + 1) * CHUNK)
+            summed = acc[place, :] * jnp.sum(here, axis=1, keepdims=True)
+            square = jnp.mean(summed * summed, axis=1, keepdims=True)
+            out_ref[place, :] = (summed * lax.rsqrt(square + 1e-06)).astype(BF16)
+
+
+def update(place, docs, e_all, v, p_own, cs, nums, shifts, gain):
+    own, width = p_own.shape
+    size = min(UPDATE_ROWS, own)
+    ranks = e_all.shape[0] // docs
+
+    def turn(i):
+        return lax.rem(i + HELD, ranks)
+
     return pl.pallas_call(
-        functools.partial(update_kernel, ranks),
+        functools.partial(update_kernel, gain),
         grid_spec=pltpu.PrefetchScalarGridSpec(
             num_scalar_prefetch=1,
-            grid=(own // rows,),
-            in_specs=[whole()] * 3
-            + [pl.BlockSpec((rows, docs), lambda i, place: (i, 0))] * ranks
-            + [whole()] * ranks,
-            out_specs=pl.BlockSpec((rows, width), lambda i, place: (i, 0)),
+            grid=(ranks,),
+            in_specs=[
+                pl.BlockSpec(
+                    (docs, width), lambda i, place: (jnp.bitwise_xor(place[0], turn(i)), 0)
+                ),
+                pl.BlockSpec((1, docs), lambda i, place: (0, turn(i))),
+            ]
+            + [whole()] * 2
+            + [pl.BlockSpec(memory_space=pl.ANY)] * HELD
+            + [whole()] * HELD,
+            out_specs=pl.BlockSpec((own, width), lambda i, place: (0, 0)),
+            scratch_shapes=[
+                pltpu.VMEM((2, size, docs), F32),
+                pltpu.VMEM((own, width), F32),
+                pltpu.VMEM((HELD, own, docs), BF16),
+                pltpu.SemaphoreType.DMA((HELD,)),
+            ],
         ),
         out_shape=jax.ShapeDtypeStruct((own, width), BF16),
         compiler_params=params(),
-    )(place, in_vmem(e_all), in_vmem(v), in_vmem(cs), *[in_hbm(num) for num in nums], *shifts)
+    )(
+        place,
+        in_hbm(e_all),
+        v,
+        in_vmem(p_own),
+        in_vmem(cs),
+        *[in_hbm(num) for num in nums],
+        *[in_vmem(shift) for shift in shifts],
+    )
 
 
 def swap(x, axis, bit):
@@ -385,58 +431,42 @@
 
     e_all = lax.all_gather(embeddings, "docs", tiled=True)
     partner = swap(embeddings, "docs", 1)
-    state = [None, None]
-    nums, shifts = [None] * doc_ranks, [None] * doc_ranks
-
-    def job_of(k, kept=True):
+    state = {}
+    nums, shifts = [None] * HELD, [None] * HELD
+
+    def share_job(k):
         def job(x):
-            source, rank = (embeddings, partner, e_all)[min(k, 2)], place ^ k if k > 1 else 0 * place
-            source = in_hbm(source) if k != 1 else source
-            held = state[0] if kept else jnp.zeros((8, CHUNK), F32)
-            nums[k], shifts[k], x, held = share(
-                rank.reshape(1), docs, source, state[1], x, held, gain
-            )
-            if kept:
-                state[0] = held
+            e = in_hbm((embeddings, partner)[k])
+            nums[k], shifts[k], x, state["num"] = share(e, state["own"], x, state["num"], gain)
             return x
 
         return job
 
-    doc_bits, proto_bits = list(bits("docs")), list(bits("protos"))
-    early = {bit: [] for bit in doc_bits}
-    column_jobs = {doc_bits[-1]: []}
-    row_jobs = {bit: [] for bit in proto_bits}
-    gather_jobs = {bit: [] for bit in doc_bits}
-    for k in range(2):
-        early[doc_bits[1 + k % (len(doc_bits) - 1)]].append(job_of(k))
-    late = list(row_jobs.values())
-    late += [gather_jobs[bit] for bit in doc_bits[1:]]
-    rest = list(range(2, doc_ranks))
-    for i, slot in enumerate(late):
-        slot.extend(job_of(k, False) for k in rest[i :: len(late)])
+    doc_bits = list(bits("docs"))
+    early = {doc_bits[1]: [share_job(0)], doc_bits[2]: [share_job(1)]}
 
     num, shift, lse, own_table = stats(
         place.reshape(1), own, in_hbm(embeddings), in_hbm(prototypes), gain
     )
-    state[1] = own_table
-    state[0] = num
+    state["own"], state["num"] = own_table, num
     lse = reduce_over(lse, "protos", log_add)
     w = jnp.exp2(shift - lse)
     weight = w
     for sweep_index in range(SWEEPS):
-        last = sweep_index == SWEEPS - 1
-        beside = column_jobs if last else (early if sweep_index == 0 else {})
-        state[0], col_local = columns(in_vmem(state[0]), weight)
+        beside = early if sweep_index == 0 else {}
+        state["num"], col_local = columns(in_vmem(state["num"]), weight)
         col_total = reduce_over(col_local, "docs", jnp.add, beside)
         cs = 1.0 / (total_protos * col_total)
-        state[0], row_local = row_sums(in_vmem(state[0]), w, cs)
-        row_sum = reduce_over(row_local, "protos", jnp.add, row_jobs if last else {})
+        state["num"], row_local = row_sums(in_vmem(state["num"]), w, cs)
+        row_sum = reduce_over(row_local, "protos", jnp.add)
         r = 1.0 / (total_docs * row_sum)
         weight = w * r
-    v = gather_over(jnp.log2(r * total_docs) - lse, "docs", gather_jobs)
-    new_prototypes = update(place.reshape(1), e_all, v, cs, nums, shifts)
+    v = gather_over(jnp.log2(r * total_docs) - lse, "docs")
+    new_prototypes = update(
+        place.reshape(1), docs, e_all, v, state["own"], cs, nums, shifts, gain
+    )
     column_potential = jnp.log(total_docs * cs.T.reshape(-1)[:protos])
-    row_potential = jnp.log(r).reshape(-1)
+    row_potential = jnp.log(lax.optimization_barrier(r)).reshape(-1)
     return (new_prototypes, column_potential, row_potential)
 
 

time: 269 us -> 245 us (0.911); the launches traced: 264 us -> 244 us
  Pallas kernels: 206 us -> 176 us
  waiting for transfers between devices: 16.1 us -> 27.3 us
  local copies, waits for them, and re-layouts: 5.09 us -> 2.3 us
    pallas_call x9 -> x3, Pallas kernels: 79.3 us -> 49 us  [the longest x1 36.6 us: update(): pl.pallas_call(functools.partial(update_kernel, gain), grid_spec=pltpu.Pr...]
    ppermute x16, waiting for transfers between devices: 15.4 us -> 26.6 us  [swap(): return lax.ppermute(x, axis, [(i, i ^ bit) for i in range(size)])]
    unnamed x5 -> x2, local copies, waits for them, and re-layouts: 4.35 us -> 0.97 us
  transfers between devices with their start and end apart: 17 -> 17, of which waited for: 9 -> 13; matrix products, arithmetic and copies ran while one was open for 0% -> 1% of each run, Pallas kernels for 69% -> 57%
where the time goes in v4:
time: 245 us; the launch traced here: 244 us
  Pallas kernels  176 us (72%)
  waiting for transfers between devices  27.3 us (11%)
  starting transfers between devices  23.7 us (10%)
  between operations  14.2 us (6%)
    pallas_call x1, Pallas kernels, stats(): pl.pallas_call(functools.partial(stats_kernel, gain), grid_spec=pltpu.Pre...  106 us
    pallas_call x1, Pallas kernels, update(): pl.pallas_call(functools.partial(update_kernel, gain), grid_spec=pltpu.Pr...  36.6 us
    ppermute x16, waiting for transfers between devices, swap(): return lax.ppermute(x, axis, [(i, i ^ bit) for i in range(size)])  26.6 us
    ppermute x16, starting transfers between devices, swap(): return lax.ppermute(x, axis, [(i, i ^ bit) for i in range(size)])  23.7 us
    pallas_call x2, Pallas kernels, share(): pl.pallas_call(functools.partial(share_kernel, gain), grid=(docs // DOC_T...  12.4 us
    pallas_call x2, Pallas kernels, columns(): pl.pallas_call(columns_kernel, in_specs=[whole()] * 2, out_specs=[whole()...  11.2 us
    pallas_call x2, Pallas kernels, row_sums(): pl.pallas_call(rows_kernel, in_specs=[whole()] * 3, out_specs=[whole()] *...  10.1 us
  transfers between devices with their start and end apart: 17, of which 13 were waited for; matrix products, arithmetic and copies ran while one was open for 1% of the time, Pallas kernels for 57%

profile of v4, /device:TPU:0, one launch (start us, length us, event | category | flops | bytes accessed | tf_op | source)
XLA Modules:
  0.0 243.7 jit_solution(3540021175351453027)
XLA Ops:
  7.2 0.0 all-gather.2.cloned.1.call-start
  7.2 0.7 all-gather.2.cloned.1.call-update
  7.9 0.5 collective-permute-start
  8.4 105.7 %shard_map.49 = (bf16[16384,1024]{1,0:T(8,128)(2,1)S(1)}, f32[1,1024]{1,0:T(1,128)S(1)}, f32[1,1024]{1,0:T(1,128)S(1)}, bf16[2048,512]{1,0:T(8,128)(2,1)S(1)}) custom-call(s32[1]{0:T(128)} %bitcast.place_ref, bf16[1024,512]{1,0:T(8,128)(2,1)} %e_ref.3, bf16[16384,512]{1,0:T(8,128)(2,1)} %p_any.1, bf16[16384,512]{1,0:T(8,128)(2,1)} %p_any.1), custom_call_target="tpu_custom_call" | custom-call | tf_op jit(solution)/shard_map/pallas_call | solution.py:116
  114.1 2.6 %collective-permute-start.1 = (f32[1,1024]{1,0:T(1,128)S(1)}, f32[1,1024]{1,0:T(1,128)S(1)}, u32[]{:S(2)}, u32[]{:S(2)}) collective-permute-start(f32[1,1024]{1,0:T(1,128)S(1)} %get-tuple-element.25), channel_id=1, source_target_pairs={{0,1},{1,0},{2,3},{3,2},{4,5},{5,4},{6,7},{7,6},{8,9},{9,8},{10,11... | collective-permute-start | bytes 12296 | tf_op jit(solution)/shard_map/ppermute | solution.py:388
  116.7 1.6 collective-permute-done.1
  118.3 2.1 collective-permute-start.2
  120.4 1.6 collective-permute-done.2
  122.0 5.6 %shard_map.50 = (bf16[16384,1024]{1,0:T(8,128)(2,1)S(1)}, f32[128,128]{1,0:T(8,128)S(1)}) custom-call(bf16[16384,1024]{1,0:T(8,128)(2,1)S(1)} %get-tuple-element.23.num_ref, f32[1,1024]{1,0:T(1,128)S(1)} %get-tuple-element.45.w_ref), custom_call_target="tpu_custom_call", output_to_operand_aliasing={{0}: (0, {})} | custom-call | tf_op jit(solution)/shard_map/pallas_call | solution.py:185
  127.6 0.1 collective-permute-start.3
  127.7 1.2 collective-permute-done.3
  128.9 2.1 collective-permute-start.4
  131.1 6.2 %shard_map.51 = (bf16[2048,1024]{1,0:T(8,128)(2,1)}, f32[1,1024]{1,0:T(1,128)S(1)}, f32[128,128]{1,0:T(8,128)S(1)}, bf16[16384,1024]{1,0:T(8,128)(2,1)S(1)}) custom-call(bf16[1024,512]{1,0:T(8,128)(2,1)} %e_ref.3, bf16[2048,512]{1,0:T(8,128)(2,1)S(1)} %get-tuple-element.22.p_ref, f32[128,128]{1,0:T(8,128)S(1)} %add.46.x_ref, ...), custom_call_target="tpu_custom_call", output_to_operand_aliasing={{3}: (3, {})} | custom-call | tf_op jit(solution)/shard_map/pallas_call | solution.py:272
  137.3 0.0 collective-permute-done.4
  137.3 3.4 %collective-permute-start.5 = (f32[128,128]{1,0:T(8,128)S(1)}, f32[128,128]{1,0:T(8,128)S(1)}, u32[]{:S(2)}, u32[]{:S(2)}) collective-permute-start(f32[128,128]{1,0:T(8,128)S(1)} %add.47.x_ref), channel_id=1, source_target_pairs={{0,16},{4,20},{8,24},{12,28},{16,0},{20,4},{24,8},{28,12},{1,17},{... | collective-permute-start | bytes 196616 | tf_op jit(solution)/shard_map/ppermute | solution.py:388
  140.7 0.0 collective-permute-done.e_ref
  140.7 0.0 copy-start
  140.7 1.0 copy-done
  141.7 6.2 %shard_map.52 = (bf16[2048,1024]{1,0:T(8,128)(2,1)}, f32[1,1024]{1,0:T(1,128)S(1)}, f32[128,128]{1,0:T(8,128)S(1)}, bf16[16384,1024]{1,0:T(8,128)(2,1)S(1)}) custom-call(bf16[1024,512]{1,0:T(8,128)(2,1)} %copy-done, bf16[2048,512]{1,0:T(8,128)(2,1)S(1)} %get-tuple-element.22.p_ref, f32[128,128]{1,0:T(8,128)S(1)} %add.47.x_ref, ...), custom_call_target="tpu_custom_call", output_to_operand_aliasing={{3}: (3, {})} | custom-call | tf_op jit(solution)/shard_map/pallas_call | solution.py:272
  147.9 0.0 collective-permute-done.5
  147.9 5.0 %shard_map.53 = (bf16[16384,1024]{1,0:T(8,128)(2,1)S(1)}, f32[1,1024]{1,0:T(1,128)S(1)}) custom-call(bf16[16384,1024]{1,0:T(8,128)(2,1)S(1)} %get-tuple-element.30.num_ref, f32[1,1024]{1,0:T(1,128)S(1)} %get-tuple-element.45.w_ref, f32[128,128]{1,0:T(8,128)S(1)} %multiply_divide_fusion.1.cs_ref), custom_call_target="tpu_custom_call", output_to_operand_aliasing={{0}: (0, {})} | custom-call | tf_op jit(solution)/shard_map/pallas_call | solution.py:235
  152.9 3.1 %collective-permute-start.6 = (f32[1,1024]{1,0:T(1,128)S(1)}, f32[1,1024]{1,0:T(1,128)S(1)}, u32[]{:S(2)}, u32[]{:S(2)}) collective-permute-start(f32[1,1024]{1,0:T(1,128)S(1)} %get-tuple-element.33), channel_id=1, source_target_pairs={{0,1},{1,0},{2,3},{3,2},{4,5},{5,4},{6,7},{7,6},{8,9},{9,8},{10,11... | collective-permute-start | bytes 12296 | tf_op jit(solution)/shard_map/ppermute | solution.py:388
  155.9 1.6 collective-permute-done.6
  157.5 2.1 collective-permute-start.7
  159.6 1.6 collective-permute-done.7
  161.2 5.6 %shard_map.54 = (bf16[16384,1024]{1,0:T(8,128)(2,1)S(1)}, f32[128,128]{1,0:T(8,128)S(1)}) custom-call(bf16[16384,1024]{1,0:T(8,128)(2,1)S(1)} %get-tuple-element.32.num_ref, f32[1,1024]{1,0:T(1,128)S(1)} %divide_multiply_fusion.w_ref), custom_call_target="tpu_custom_call", output_to_operand_aliasing={{0}: (0, {})} | custom-call | tf_op jit(solution)/shard_map/pallas_call | solution.py:185
  166.8 0.1 collective-permute-start.8
  166.8 1.2 collective-permute-done.8
  168.1 0.1 collective-permute-start.9
  168.2 4.3 %collective-permute-done.9 = f32[128,128]{1,0:T(8,128)S(1)} collective-permute-done((f32[128,128]{1,0:T(8,128)S(1)}, f32[128,128]{1,0:T(8,128)S(1)}, u32[]{:S(2)}, u32[]{:S(2)}) %collective-permute-start.9) | collective-permute-done | bytes 65568 | tf_op jit(solution)/shard_map/ppermute | solution.py:388
  172.4 1.8 collective-permute-start.10
  174.3 3.7 %collective-permute-done.10 = f32[128,128]{1,0:T(8,128)S(1)} collective-permute-done((f32[128,128]{1,0:T(8,128)S(1)}, f32[128,128]{1,0:T(8,128)S(1)}, u32[]{:S(2)}, u32[]{:S(2)}) %collective-permute-start.10) | collective-permute-done | bytes 65568 | tf_op jit(solution)/shard_map/ppermute | solution.py:388
  178.0 5.1 %shard_map.55 = (bf16[16384,1024]{1,0:T(8,128)(2,1)S(1)}, f32[1,1024]{1,0:T(1,128)S(1)}) custom-call(bf16[16384,1024]{1,0:T(8,128)(2,1)S(1)} %get-tuple-element.34.num_ref, f32[1,1024]{1,0:T(1,128)S(1)} %get-tuple-element.45.w_ref, f32[128,128]{1,0:T(8,128)S(1)} %get-tuple-element.42.cs_ref), custom_call_target="tpu_custom_call", output_to_operand_aliasing={{0}: (0, {})} | custom-call | tf_op jit(solution)/shard_map/pallas_call | solution.py:235
  183.2 2.0 collective-permute-start.11
  185.2 1.6 collective-permute-done.11
  186.8 2.0 collective-permute-start.12
  188.9 1.6 collective-permute-done.12
  190.5 0.1 collective-permute-start.13
  190.6 1.2 collective-permute-done.13
  191.7 0.1 collective-permute-start.14
  191.8 3.6 %collective-permute-done.14 = f32[1,2048]{1,0:T(1,128)S(1)} collective-permute-done((f32[1,2048]{1,0:T(1,128)S(1)}, f32[1,2048]{1,0:T(1,128)S(1)}, u32[]{:S(2)}, u32[]{:S(2)}) %collective-permute-start.14) | collective-permute-done | bytes 8224 | tf_op jit(solution)/shard_map/ppermute | solution.py:388
  195.5 1.5 collective-permute-start.15
  197.0 0.7 copy.11
  197.7 0.6 log.15
  198.3 1.8 collective-permute-done.15
  200.2 0.0 all-gather.2.cloned.1.call-done.e_ref
  200.2 36.6 %shard_map.56 = bf16[2048,512]{1,0:T(8,128)(2,1)} custom-call(s32[1]{0:T(128)} %bitcast.place_ref, bf16[8192,512]{1,0:T(8,128)(2,1)} %all-gather.2.cloned.1.call-done.e_ref, f32[1,8192]{1,0:T(1,128)S(1)} %pad_maximum_fusion.v_ref, bf16[2048,512]{1,0:T(8,128)(2,1)S(1)} %get-tuple-element.22.p_ref, f32[128,128]{1,0:T(8,128)S(1)} %get-tuple-element.42.cs_ref, ...), custom_call_target="tpu_custom_call" | custom-call | tf_op jit(solution)/shard_map/pallas_call | solution.py:351
  (15 shorter events, 0.3 us)
Async XLA Ops:
  7.2 193.1 %all-gather.2.cloned.1.call-start = ((), (), s32[]{:S(2)}) async-start(), calls=%async_computation | async-start | bytes 9437184 | tf_op jit(solution)/shard_map/all_gather | solution.py:432
  7.9 132.8 %collective-permute-start = (bf16[1024,512]{1,0:T(8,128)(2,1)}, bf16[1024,512]{1,0:T(8,128)(2,1)S(1)}, u32[]{:S(2)}, u32[]{:S(2)}) collective-permute-start(bf16[1024,512]{1,0:T(8,128)(2,1)} %e_ref.3), channel_id=1, source_target_pairs={{0,4},{4,0},{8,12},{12,8},{16,20},{20,16},{24,28},{28,24},{1,5},{5... | collective-permute-start | bytes 3145736 | tf_op jit(solution)/shard_map/ppermute | solution.py:388
  114.1 4.2 %collective-permute-start.1 = (f32[1,1024]{1,0:T(1,128)S(1)}, f32[1,1024]{1,0:T(1,128)S(1)}, u32[]{:S(2)}, u32[]{:S(2)}) collective-permute-start(f32[1,1024]{1,0:T(1,128)S(1)} %get-tuple-element.25), channel_id=1, source_target_pairs={{0,1},{1,0},{2,3},{3,2},{4,5},{5,4},{6,7},{7,6},{8,9},{9,8},{10,11... | collective-permute-start | bytes 12296 | tf_op jit(solution)/shard_map/ppermute | solution.py:388
  118.3 3.7 %collective-permute-start.2 = (f32[1,1024]{1,0:T(1,128)S(1)}, f32[1,1024]{1,0:T(1,128)S(1)}, u32[]{:S(2)}, u32[]{:S(2)}) collective-permute-start(f32[1,1024]{1,0:T(1,128)S(1)} %multiply_add_fusion.1), channel_id=1, source_target_pairs={{0,2},{1,3},{2,0},{3,1},{4,6},{5,7},{6,4},{7,5},{8,10},{9,11},{10,... | collective-permute-start | bytes 12296 | tf_op jit(solution)/shard_map/ppermute | solution.py:388
  127.6 1.3 collective-permute-start.3
  128.9 8.3 %collective-permute-start.4 = (f32[128,128]{1,0:T(8,128)S(1)}, f32[128,128]{1,0:T(8,128)S(1)}, u32[]{:S(2)}, u32[]{:S(2)}) collective-permute-start(f32[128,128]{1,0:T(8,128)S(1)} %add.46.x_ref), channel_id=1, source_target_pairs={{0,8},{4,12},{8,0},{12,4},{16,24},{20,28},{24,16},{28,20},{1,9},{5... | collective-permute-start | bytes 196616 | tf_op jit(solution)/shard_map/ppermute | solution.py:388
  137.3 10.6 %collective-permute-start.5 = (f32[128,128]{1,0:T(8,128)S(1)}, f32[128,128]{1,0:T(8,128)S(1)}, u32[]{:S(2)}, u32[]{:S(2)}) collective-permute-start(f32[128,128]{1,0:T(8,128)S(1)} %add.47.x_ref), channel_id=1, source_target_pairs={{0,16},{4,20},{8,24},{12,28},{16,0},{20,4},{24,8},{28,12},{1,17},{... | collective-permute-start | bytes 196616 | tf_op jit(solution)/shard_map/ppermute | solution.py:388
  140.7 1.0 copy-start
  152.9 4.6 %collective-permute-start.6 = (f32[1,1024]{1,0:T(1,128)S(1)}, f32[1,1024]{1,0:T(1,128)S(1)}, u32[]{:S(2)}, u32[]{:S(2)}) collective-permute-start(f32[1,1024]{1,0:T(1,128)S(1)} %get-tuple-element.33), channel_id=1, source_target_pairs={{0,1},{1,0},{2,3},{3,2},{4,5},{5,4},{6,7},{7,6},{8,9},{9,8},{10,11... | collective-permute-start | bytes 12296 | tf_op jit(solution)/shard_map/ppermute | solution.py:388
  157.5 3.7 %collective-permute-start.7 = (f32[1,1024]{1,0:T(1,128)S(1)}, f32[1,1024]{1,0:T(1,128)S(1)}, u32[]{:S(2)}, u32[]{:S(2)}) collective-permute-start(f32[1,1024]{1,0:T(1,128)S(1)} %add.49), channel_id=1, source_target_pairs={{0,2},{1,3},{2,0},{3,1},{4,6},{5,7},{6,4},{7,5},{8,10},{9,11},{10,... | collective-permute-start | bytes 12296 | tf_op jit(solution)/shard_map/ppermute | solution.py:388
  166.8 1.3 collective-permute-start.8
  168.1 4.3 %collective-permute-start.9 = (f32[128,128]{1,0:T(8,128)S(1)}, f32[128,128]{1,0:T(8,128)S(1)}, u32[]{:S(2)}, u32[]{:S(2)}) collective-permute-start(f32[128,128]{1,0:T(8,128)S(1)} %add.51), channel_id=1, source_target_pairs={{0,8},{4,12},{8,0},{12,4},{16,24},{20,28},{24,16},{28,20},{1,9},{5... | collective-permute-start | bytes 196616 | tf_op jit(solution)/shard_map/ppermute | solution.py:388
  172.4 5.5 %collective-permute-start.10 = (f32[128,128]{1,0:T(8,128)S(1)}, f32[128,128]{1,0:T(8,128)S(1)}, u32[]{:S(2)}, u32[]{:S(2)}) collective-permute-start(f32[128,128]{1,0:T(8,128)S(1)} %add.52), channel_id=1, source_target_pairs={{0,16},{4,20},{8,24},{12,28},{16,0},{20,4},{24,8},{28,12},{1,17},{... | collective-permute-start | bytes 196616 | tf_op jit(solution)/shard_map/ppermute | solution.py:388
  183.2 3.7 %collective-permute-start.11 = (f32[1,1024]{1,0:T(1,128)S(1)}, f32[1,1024]{1,0:T(1,128)S(1)}, u32[]{:S(2)}, u32[]{:S(2)}) collective-permute-start(f32[1,1024]{1,0:T(1,128)S(1)} %get-tuple-element.36), channel_id=1, source_target_pairs={{0,1},{1,0},{2,3},{3,2},{4,5},{5,4},{6,7},{7,6},{8,9},{9,8},{10,11... | collective-permute-start | bytes 12296 | tf_op jit(solution)/shard_map/ppermute | solution.py:388
  186.8 3.6 %collective-permute-start.12 = (f32[1,1024]{1,0:T(1,128)S(1)}, f32[1,1024]{1,0:T(1,128)S(1)}, u32[]{:S(2)}, u32[]{:S(2)}) collective-permute-start(f32[1,1024]{1,0:T(1,128)S(1)} %add.54), channel_id=1, source_target_pairs={{0,2},{1,3},{2,0},{3,1},{4,6},{5,7},{6,4},{7,5},{8,10},{9,11},{10,... | collective-permute-start | bytes 12296 | tf_op jit(solution)/shard_map/ppermute | solution.py:388
  190.5 1.2 collective-permute-start.13
  191.7 3.7 %collective-permute-start.14 = (f32[1,2048]{1,0:T(1,128)S(1)}, f32[1,2048]{1,0:T(1,128)S(1)}, u32[]{:S(2)}, u32[]{:S(2)}) collective-permute-start(f32[1,2048]{1,0:T(1,128)S(1)} %pad_maximum_fusion.2), channel_id=1, source_target_pairs={{0,8},{4,12},{8,0},{12,4},{16,24},{20,28},{24,16},{28,20},{1,9},{5... | collective-permute-start | bytes 24584 | tf_op jit(solution)/shard_map/ppermute | solution.py:388
  195.5 4.7 %collective-permute-start.15 = (f32[1,4096]{1,0:T(1,128)S(1)}, f32[1,4096]{1,0:T(1,128)S(1)}, u32[]{:S(2)}, u32[]{:S(2)}) collective-permute-start(f32[1,4096]{1,0:T(1,128)S(1)} %pad_maximum_fusion.1), channel_id=1, source_target_pairs={{0,16},{4,20},{8,24},{12,28},{16,0},{20,4},{24,8},{28,12},{1,17},{... | collective-permute-start | bytes 49160 | tf_op jit(solution)/shard_map/ppermute | solution.py:388
Sparse Core Ops, SparseCore 0:
  9.6 84.7 all-gather.1

commit v5 on v4

--- a/solution.py
+++ b/solution.py
@@ -147,14 +147,19 @@
     return [part.astype(F32) for part in (high, mid, low)]
 
 
-def columns_kernel(num_ref, w_ref, num_out, out_ref, turned):
+def halves(place_ref):
+    core = lax.rem(place_ref[0], 2)
+    return rows_of(core, CHUNK // 2), rows_of(1 - core, CHUNK // 2)
+
+
+def columns_kernel(num_ref, w_ref, place_ref, num_out, mine_ref, other_ref, turned, sums):
     del num_out
     docs = num_ref.shape[1]
     taken = turned.shape[0]
     w = w_ref[...]
     rows = split(w[:, :taken]) + [jnp.zeros((CHUNK - 3, taken), F32)]
     turned[...] = jnp.concatenate(rows, axis=0).T.astype(BF16)
-    lane = lax.broadcasted_iota(jnp.int32, out_ref.shape, 1)
+    lane = lax.broadcasted_iota(jnp.int32, sums.shape, 1)
 
     def body(group, found):
         base = pl.multiple_of(group * COLUMN_GROUP * CHUNK, CHUNK)
@@ -173,29 +178,43 @@
         return found
 
     groups = num_ref.shape[0] // (COLUMN_GROUP * CHUNK)
-    out_ref[...] = lax.fori_loop(0, groups, body, jnp.ones(out_ref.shape, F32))
+    sums[...] = lax.fori_loop(0, groups, body, jnp.ones(sums.shape, F32))
+    mine, other = halves(place_ref)
+    mine_ref[...] = sums[mine, :]
+    other_ref[...] = sums[other, :]
 
 
 def chunk_lanes(protos):
     return -(-protos // (CHUNK * CHUNK)) * CHUNK
 
 
-def columns(num, w):
+def columns(num, w, place):
     protos, docs = num.shape
+    lanes = chunk_lanes(protos)
     return pl.pallas_call(
         columns_kernel,
-        in_specs=[whole()] * 2,
-        out_specs=[whole()] * 2,
-        out_shape=[pltpu.VMEM(num.shape, BF16), pltpu.VMEM((CHUNK, chunk_lanes(protos)), F32)],
+        in_specs=[whole()] * 2 + [pl.BlockSpec(memory_space=pltpu.SMEM)],
+        out_specs=[whole()] * 3,
+        out_shape=[pltpu.VMEM(num.shape, BF16)] + [pltpu.VMEM((CHUNK // 2, lanes), F32)] * 2,
         input_output_aliases={0: 0},
-        scratch_shapes=[pltpu.VMEM((docs // 2, CHUNK), BF16)],
+        scratch_shapes=[pltpu.VMEM((docs // 2, CHUNK), BF16), pltpu.VMEM((CHUNK, lanes), F32)],
         compiler_params=params(),
-    )(num, in_vmem(w))
-
-
-def rows_kernel(num_ref, w_ref, cs_ref, num_out, out_ref, parts):
+    )(num, in_vmem(w), place)
+
+
+def rows_kernel(total, num_ref, w_ref, mine_ref, other_ref, place_ref, num_out, out_ref, cs_ref, *refs):
     del num_out
+    parts = refs[-1]
+    copy = None
+    if len(refs) > 1:
+        taken, done = refs[0], refs[1]
+        own = taken.shape[0]
+        copy = pltpu.make_async_copy(num_ref.at[rows_of(place_ref[0], own)], taken, done)
+        copy.start()
     docs = num_ref.shape[1]
+    mine, other = halves(place_ref)
+    cs_ref[mine, :] = 1.0 / (total * mine_ref[...])
+    cs_ref[other, :] = 1.0 / (total * other_ref[...])
     turned = cs_ref[...]
     for j, part in enumerate(split(turned.T)):
         parts[j] = part
@@ -228,19 +247,27 @@
     zero = jnp.zeros((8, docs), F32)
     added, product = lax.fori_loop(0, groups, body, (zero, zero))
     out_ref[...] = w_ref[...] * jnp.sum(added + product, axis=0, keepdims=True)
-
-
-def row_sums(num, w, cs):
+    if copy is not None:
+        copy.wait()
+
+
+def row_sums(num, w, mine, other, place, total, own):
     docs = num.shape[1]
+    lanes = mine.shape[1]
     return pl.pallas_call(
-        rows_kernel,
-        in_specs=[whole()] * 3,
-        out_specs=[whole()] * 2,
-        out_shape=[pltpu.VMEM(num.shape, BF16), pltpu.VMEM((1, docs), F32)],
+        functools.partial(rows_kernel, total),
+        in_specs=[whole()] * 4 + [pl.BlockSpec(memory_space=pltpu.SMEM)],
+        out_specs=[whole()] * 3 + [pl.BlockSpec(memory_space=pl.ANY)] * (own > 0),
+        out_shape=[
+            pltpu.VMEM(num.shape, BF16),
+            pltpu.VMEM((1, docs), F32),
+            pltpu.VMEM((CHUNK, lanes), F32),
+        ]
+        + [pltpu.HBM((own, docs), BF16)] * (own > 0),
         input_output_aliases={0: 0},
-        scratch_shapes=[pltpu.VMEM((3, cs.shape[1], CHUNK), F32)],
+        scratch_shapes=[pltpu.SemaphoreType.DMA] * (own > 0) + [pltpu.VMEM((3, lanes, CHUNK), F32)],
         compiler_params=params(),
-    )(num, in_vmem(w), in_vmem(cs))
+    )(num, in_vmem(w), in_vmem(mine), in_vmem(other), place)
 
 
 def share_kernel(gain, e_ref, p_ref, x_ref, held_ref, num_ref, shift_ref, x_out, held_out):
@@ -395,22 +422,26 @@
         bit *= 2
 
 
-def reduce_over(x, axis, combine, jobs={}):
+def reduce_over(x, axis, combine):
     for bit in bits(axis):
-        other = swap(x, axis, bit)
+        x = combine(x, swap(x, axis, bit))
+    return x
+
+
+def gather_over(x, axis):
+    for bit in bits(axis):
+        x = jnp.concatenate([x, swap(x, axis, bit)], axis=1)
+    return x
+
+
+def sum_over_docs(mine, other, jobs={}):
+    mine = mine + swap(other, "docs", 1)
+    for bit in list(bits("docs"))[1:]:
+        arrived = swap(mine, "docs", bit)
         for job in jobs.get(bit, ()):
-            x = job(x)
-        x = combine(x, other)
-    return x
-
-
-def gather_over(x, axis, jobs={}):
-    for bit in bits(axis):
-        other = swap(x, axis, bit)
-        for job in jobs.get(bit, ()):
-            x = job(x)
-        x = jnp.concatenate([x, other], axis=1)
-    return x
+            mine = job(mine)
+        mine = mine + arrived
+    return mine, swap(mine, "docs", 1)
 
 
 def log_add(a, b):
@@ -436,14 +467,14 @@
 
     def share_job(k):
         def job(x):
-            e = in_hbm((embeddings, partner)[k])
+            e = in_hbm(partner)
             nums[k], shifts[k], x, state["num"] = share(e, state["own"], x, state["num"], gain)
             return x
 
         return job
 
     doc_bits = list(bits("docs"))
-    early = {doc_bits[1]: [share_job(0)], doc_bits[2]: [share_job(1)]}
+    early = {doc_bits[1]: [share_job(1)]}
 
     num, shift, lse, own_table = stats(
         place.reshape(1), own, in_hbm(embeddings), in_hbm(prototypes), gain
@@ -454,10 +485,19 @@
     weight = w
     for sweep_index in range(SWEEPS):
         beside = early if sweep_index == 0 else {}
-        state["num"], col_local = columns(in_vmem(state["num"]), weight)
-        col_total = reduce_over(col_local, "docs", jnp.add, beside)
-        cs = 1.0 / (total_protos * col_total)
-        state["num"], row_local = row_sums(in_vmem(state["num"]), w, cs)
+        state["num"], *parts = columns(in_vmem(state["num"]), weight, place.reshape(1))
+        mine, other = sum_over_docs(*parts, beside)
+        state["num"], row_local, cs, *taken = row_sums(
+            in_vmem(state["num"]),
+            w,
+            mine,
+            other,
+            place.reshape(1),
+            float(total_protos),
+            0 if sweep_index else own,
+        )
+        if taken:
+            nums[0], shifts[0] = taken[0], shift
         row_sum = reduce_over(row_local, "protos", jnp.add)
         r = 1.0 / (total_docs * row_sum)
         weight = w * r

time: 245 us -> 242 us (0.988)
  Pallas kernels: 176 us -> 170 us
    pallas_call x2 -> x1, Pallas kernels: 12.4 us -> 6.17 us  [share(): pl.pallas_call(functools.partial(share_kernel, gain), grid=(docs // DOC_T...]
    ppermute x16 -> x18, waiting for transfers between devices: 26.6 us -> 27.9 us  [swap(): return lax.ppermute(x, axis, [(i, i ^ bit) for i in range(size)])]
    ppermute x16 -> x18, starting transfers between devices: 23.7 us -> 24.8 us  [swap(): return lax.ppermute(x, axis, [(i, i ^ bit) for i in range(size)])]
  transfers between devices with their start and end apart: 17 -> 19, of which waited for: 13 -> 16; matrix products, arithmetic and copies ran while one was open for 1% -> 1% of each run, Pallas kernels for 57% -> 56%
where the time goes in v5:
time: 242 us; the launch traced here: 240 us
  Pallas kernels  170 us (70%)
  waiting for transfers between devices  28.6 us (12%)
  starting transfers between devices  24.8 us (10%)
  between operations  14.2 us (6%)
    pallas_call x1, Pallas kernels, stats(): pl.pallas_call(functools.partial(stats_kernel, gain), grid_spec=pltpu.Pre...  106 us
    pallas_call x1, Pallas kernels, update(): pl.pallas_call(functools.partial(update_kernel, gain), grid_spec=pltpu.Pr...  36.8 us
    ppermute x18, waiting for transfers between devices, swap(): return lax.ppermute(x, axis, [(i, i ^ bit) for i in range(size)])  27.9 us
    ppermute x18, starting transfers between devices, swap(): return lax.ppermute(x, axis, [(i, i ^ bit) for i in range(size)])  24.8 us
    pallas_call x2, Pallas kernels, columns(): pl.pallas_call(columns_kernel, in_specs=[whole()] * 2 + [pl.BlockSpec(mem...  11.2 us
    pallas_call x2, Pallas kernels, row_sums(): pl.pallas_call(functools.partial(rows_kernel, total), in_specs=[whole()]...  10.6 us
    pallas_call x1, Pallas kernels, share(): pl.pallas_call(functools.partial(share_kernel, gain), grid=(docs // DOC_T...  6.17 us
  transfers between devices with their start and end apart: 19, of which 16 were waited for; matrix products, arithmetic and copies ran while one was open for 1% of the time, Pallas kernels for 56%

profile of v5, /device:TPU:0, one launch (start us, length us, event | category | flops | bytes accessed | tf_op | source)
XLA Modules:
  0.0 240.5 jit_solution(4188036778296017191)
XLA Ops:
  7.2 0.0 all-gather.2.cloned.1.call-start
  7.2 0.7 all-gather.2.cloned.1.call-update
  7.9 0.5 collective-permute-start
  8.4 105.6 %shard_map.49 = (bf16[16384,1024]{1,0:T(8,128)(2,1)S(1)}, f32[1,1024]{1,0:T(1,128)S(1)}, f32[1,1024]{1,0:T(1,128)S(1)}, bf16[2048,512]{1,0:T(8,128)(2,1)S(1)}) custom-call(s32[1]{0:T(128)} %bitcast.place_ref, bf16[1024,512]{1,0:T(8,128)(2,1)} %e_ref.1, bf16[16384,512]{1,0:T(8,128)(2,1)} %p_any.1, bf16[16384,512]{1,0:T(8,128)(2,1)} %p_any.1), custom_call_target="tpu_custom_call" | custom-call | tf_op jit(solution)/shard_map/pallas_call | solution.py:116
  114.1 2.6 %collective-permute-start.1 = (f32[1,1024]{1,0:T(1,128)S(1)}, f32[1,1024]{1,0:T(1,128)S(1)}, u32[]{:S(2)}, u32[]{:S(2)}) collective-permute-start(f32[1,1024]{1,0:T(1,128)S(1)} %get-tuple-element.25), channel_id=1, source_target_pairs={{0,1},{1,0},{2,3},{3,2},{4,5},{5,4},{6,7},{7,6},{8,9},{9,8},{10,11... | collective-permute-start | bytes 12296 | tf_op jit(solution)/shard_map/ppermute | solution.py:415
  116.7 1.6 collective-permute-done.1
  118.3 2.1 collective-permute-start.2
  120.4 1.6 collective-permute-done.2
  122.0 5.6 %shard_map.50 = (bf16[16384,1024]{1,0:T(8,128)(2,1)S(1)}, f32[64,128]{1,0:T(8,128)S(1)}, f32[64,128]{1,0:T(8,128)S(1)}) custom-call(bf16[16384,1024]{1,0:T(8,128)(2,1)S(1)} %get-tuple-element.23.num_ref, f32[1,1024]{1,0:T(1,128)S(1)} %get-tuple-element.43.w_ref, s32[1]{0:T(128)} %bitcast.place_ref), custom_call_target="tpu_custom_call", output_to_operand_aliasing={{0}: (0, {})} | custom-call | tf_op jit(solution)/shard_map/pallas_call | solution.py:194
  127.6 0.1 collective-permute-start.3
  127.7 1.2 collective-permute-done.3
  128.9 2.1 collective-permute-start.4
  131.0 0.0 collective-permute-done.e_ref
  131.0 0.0 copy-start
  131.0 1.0 copy-done
  131.9 6.2 %shard_map.51 = (bf16[2048,1024]{1,0:T(8,128)(2,1)}, f32[1,1024]{1,0:T(1,128)S(1)}, f32[64,128]{1,0:T(8,128)S(1)}, bf16[16384,1024]{1,0:T(8,128)(2,1)S(1)}) custom-call(bf16[1024,512]{1,0:T(8,128)(2,1)} %copy-done, bf16[2048,512]{1,0:T(8,128)(2,1)S(1)} %get-tuple-element.22.p_ref, f32[64,128]{1,0:T(8,128)S(1)} %add.46.x_ref, ...), custom_call_target="tpu_custom_call", output_to_operand_aliasing={{3}: (3, {})} | custom-call | tf_op jit(solution)/shard_map/pallas_call | solution.py:299
  138.1 0.0 collective-permute-done.4
  138.1 2.8 %collective-permute-start.5 = (f32[64,128]{1,0:T(8,128)S(1)}, f32[64,128]{1,0:T(8,128)S(1)}, u32[]{:S(2)}, u32[]{:S(2)}) collective-permute-start(f32[64,128]{1,0:T(8,128)S(1)} %add.47), channel_id=1, source_target_pairs={{0,16},{4,20},{8,24},{12,28},{16,0},{20,4},{24,8},{28,12},{1,17},{... | collective-permute-start | bytes 98312 | tf_op jit(solution)/shard_map/ppermute | solution.py:415
  140.9 2.1 collective-permute-done.5
  143.0 0.0 collective-permute-start.6
  143.0 1.2 collective-permute-done.6.other_ref
  144.2 5.6 %shard_map.52 = (bf16[16384,1024]{1,0:T(8,128)(2,1)S(1)}, f32[1,1024]{1,0:T(1,128)S(1)}, f32[128,128]{1,0:T(8,128)}, bf16[2048,1024]{1,0:T(8,128)(2,1)}) custom-call(bf16[16384,1024]{1,0:T(8,128)(2,1)S(1)} %get-tuple-element.29.num_ref, f32[1,1024]{1,0:T(1,128)S(1)} %get-tuple-element.43.w_ref, ...), custom_call_target="tpu_custom_call", output_to_operand_aliasing={{0}: (0, {})} | custom-call | tf_op jit(solution)/shard_map/pallas_call | solution.py:257
  149.9 1.9 collective-permute-start.7
  151.7 1.8 collective-permute-done.7
  153.5 2.7 %collective-permute-start.8 = (f32[1,1024]{1,0:T(1,128)S(1)}, f32[1,1024]{1,0:T(1,128)S(1)}, u32[]{:S(2)}, u32[]{:S(2)}) collective-permute-start(f32[1,1024]{1,0:T(1,128)S(1)} %add.49), channel_id=1, source_target_pairs={{0,2},{1,3},{2,0},{3,1},{4,6},{5,7},{6,4},{7,5},{8,10},{9,11},{10,... | collective-permute-start | bytes 12296 | tf_op jit(solution)/shard_map/ppermute | solution.py:415
  156.2 1.6 collective-permute-done.8
  157.8 5.6 %shard_map.53 = (bf16[16384,1024]{1,0:T(8,128)(2,1)S(1)}, f32[64,128]{1,0:T(8,128)S(1)}, f32[64,128]{1,0:T(8,128)S(1)}) custom-call(bf16[16384,1024]{1,0:T(8,128)(2,1)S(1)} %get-tuple-element.31.num_ref, f32[1,1024]{1,0:T(1,128)S(1)} %divide_multiply_fusion.w_ref, s32[1]{0:T(128)} %bitcast.place_ref), custom_call_target="tpu_custom_call", output_to_operand_aliasing={{0}: (0, {})} | custom-call | tf_op jit(solution)/shard_map/pallas_call | solution.py:194
  163.4 0.1 collective-permute-start.9
  163.5 1.2 collective-permute-done.9
  164.7 0.4 collective-permute-start.10
  165.0 3.6 %collective-permute-done.10 = f32[64,128]{1,0:T(8,128)S(1)} collective-permute-done((f32[64,128]{1,0:T(8,128)S(1)}, f32[64,128]{1,0:T(8,128)S(1)}, u32[]{:S(2)}, u32[]{:S(2)}) %collective-permute-start.10) | collective-permute-done | bytes 32800 | tf_op jit(solution)/shard_map/ppermute | solution.py:415
  168.6 2.7 %collective-permute-start.11 = (f32[64,128]{1,0:T(8,128)S(1)}, f32[64,128]{1,0:T(8,128)S(1)}, u32[]{:S(2)}, u32[]{:S(2)}) collective-permute-start(f32[64,128]{1,0:T(8,128)S(1)} %add.52), channel_id=1, source_target_pairs={{0,16},{4,20},{8,24},{12,28},{16,0},{20,4},{24,8},{28,12},{1,17},{... | collective-permute-start | bytes 98312 | tf_op jit(solution)/shard_map/ppermute | solution.py:415
  171.3 2.2 collective-permute-done.11
  173.6 0.0 collective-permute-start.12
  173.6 1.2 collective-permute-done.12.other_ref
  174.8 5.0 %shard_map.54 = (bf16[16384,1024]{1,0:T(8,128)(2,1)S(1)}, f32[1,1024]{1,0:T(1,128)S(1)}, f32[128,128]{1,0:T(8,128)S(1)}) custom-call(bf16[16384,1024]{1,0:T(8,128)(2,1)S(1)} %get-tuple-element.33.num_ref, f32[1,1024]{1,0:T(1,128)S(1)} %get-tuple-element.43.w_ref, f32[64,128]{1,0:T(8,128)S(1)} %add.53.mine_ref, ...), custom_call_target="tpu_custom_call", output_to_operand_aliasing={{0}: (0, {})} | custom-call | tf_op jit(solution)/shard_map/pallas_call | solution.py:257
  179.7 2.1 collective-permute-start.13
  181.8 1.6 collective-permute-done.13
  183.4 1.9 collective-permute-start.14
  185.3 1.7 collective-permute-done.14
  187.1 0.1 collective-permute-start.15
  187.1 1.2 collective-permute-done.15
  188.3 0.3 collective-permute-start.16
  188.6 3.4 %collective-permute-done.16 = f32[1,2048]{1,0:T(1,128)S(1)} collective-permute-done((f32[1,2048]{1,0:T(1,128)S(1)}, f32[1,2048]{1,0:T(1,128)S(1)}, u32[]{:S(2)}, u32[]{:S(2)}) %collective-permute-start.16) | collective-permute-done | bytes 8224 | tf_op jit(solution)/shard_map/ppermute | solution.py:415
  192.0 2.6 %collective-permute-start.17 = (f32[1,4096]{1,0:T(1,128)S(1)}, f32[1,4096]{1,0:T(1,128)S(1)}, u32[]{:S(2)}, u32[]{:S(2)}) collective-permute-start(f32[1,4096]{1,0:T(1,128)S(1)} %pad_maximum_fusion.1), channel_id=1, source_target_pairs={{0,16},{4,20},{8,24},{12,28},{16,0},{20,4},{24,8},{28,12},{1,17},{... | collective-permute-start | bytes 49160 | tf_op jit(solution)/shard_map/ppermute | solution.py:415
  194.7 0.7 copy.10
  195.4 0.6 log.15
  196.0 0.7 collective-permute-done.17
  196.8 0.0 all-gather.2.cloned.1.call-done.e_ref
  196.8 36.8 %shard_map.55 = bf16[2048,512]{1,0:T(8,128)(2,1)} custom-call(s32[1]{0:T(128)} %bitcast.place_ref, bf16[8192,512]{1,0:T(8,128)(2,1)} %all-gather.2.cloned.1.call-done.e_ref, f32[1,8192]{1,0:T(1,128)S(1)} %pad_maximum_fusion.v_ref, bf16[2048,512]{1,0:T(8,128)(2,1)S(1)} %get-tuple-element.22.p_ref, f32[128,128]{1,0:T(8,128)S(1)} %get-tuple-element.37.cs_ref, ...), custom_call_target="tpu_custom_call" | custom-call | tf_op jit(solution)/shard_map/pallas_call | solution.py:378
  (16 shorter events, 0.2 us)
Async XLA Ops:
  7.2 189.6 %all-gather.2.cloned.1.call-start = ((), (), s32[]{:S(2)}) async-start(), calls=%async_computation | async-start | bytes 9437184 | tf_op jit(solution)/shard_map/all_gather | solution.py:463
  7.9 123.1 %collective-permute-start = (bf16[1024,512]{1,0:T(8,128)(2,1)}, bf16[1024,512]{1,0:T(8,128)(2,1)S(1)}, u32[]{:S(2)}, u32[]{:S(2)}) collective-permute-start(bf16[1024,512]{1,0:T(8,128)(2,1)} %e_ref.1), channel_id=1, source_target_pairs={{0,4},{4,0},{8,12},{12,8},{16,20},{20,16},{24,28},{28,24},{1,5},{5... | collective-permute-start | bytes 3145736 | tf_op jit(solution)/shard_map/ppermute | solution.py:415
  114.1 4.2 %collective-permute-start.1 = (f32[1,1024]{1,0:T(1,128)S(1)}, f32[1,1024]{1,0:T(1,128)S(1)}, u32[]{:S(2)}, u32[]{:S(2)}) collective-permute-start(f32[1,1024]{1,0:T(1,128)S(1)} %get-tuple-element.25), channel_id=1, source_target_pairs={{0,1},{1,0},{2,3},{3,2},{4,5},{5,4},{6,7},{7,6},{8,9},{9,8},{10,11... | collective-permute-start | bytes 12296 | tf_op jit(solution)/shard_map/ppermute | solution.py:415
  118.3 3.7 %collective-permute-start.2 = (f32[1,1024]{1,0:T(1,128)S(1)}, f32[1,1024]{1,0:T(1,128)S(1)}, u32[]{:S(2)}, u32[]{:S(2)}) collective-permute-start(f32[1,1024]{1,0:T(1,128)S(1)} %multiply_add_fusion.1), channel_id=1, source_target_pairs={{0,2},{1,3},{2,0},{3,1},{4,6},{5,7},{6,4},{7,5},{8,10},{9,11},{10,... | collective-permute-start | bytes 12296 | tf_op jit(solution)/shard_map/ppermute | solution.py:415
  127.6 1.3 collective-permute-start.3
  128.9 9.2 %collective-permute-start.4 = (f32[64,128]{1,0:T(8,128)S(1)}, f32[64,128]{1,0:T(8,128)S(1)}, u32[]{:S(2)}, u32[]{:S(2)}) collective-permute-start(f32[64,128]{1,0:T(8,128)S(1)} %add.46.x_ref), channel_id=1, source_target_pairs={{0,8},{4,12},{8,0},{12,4},{16,24},{20,28},{24,16},{28,20},{1,9},{5... | collective-permute-start | bytes 98312 | tf_op jit(solution)/shard_map/ppermute | solution.py:415
  131.0 1.0 copy-start
  138.1 4.9 %collective-permute-start.5 = (f32[64,128]{1,0:T(8,128)S(1)}, f32[64,128]{1,0:T(8,128)S(1)}, u32[]{:S(2)}, u32[]{:S(2)}) collective-permute-start(f32[64,128]{1,0:T(8,128)S(1)} %add.47), channel_id=1, source_target_pairs={{0,16},{4,20},{8,24},{12,28},{16,0},{20,4},{24,8},{28,12},{1,17},{... | collective-permute-start | bytes 98312 | tf_op jit(solution)/shard_map/ppermute | solution.py:415
  143.0 1.2 collective-permute-start.6
  149.9 3.7 %collective-permute-start.7 = (f32[1,1024]{1,0:T(1,128)S(1)}, f32[1,1024]{1,0:T(1,128)S(1)}, u32[]{:S(2)}, u32[]{:S(2)}) collective-permute-start(f32[1,1024]{1,0:T(1,128)S(1)} %get-tuple-element.32), channel_id=1, source_target_pairs={{0,1},{1,0},{2,3},{3,2},{4,5},{5,4},{6,7},{7,6},{8,9},{9,8},{10,11... | collective-permute-start | bytes 12296 | tf_op jit(solution)/shard_map/ppermute | solution.py:415
  153.5 4.3 %collective-permute-start.8 = (f32[1,1024]{1,0:T(1,128)S(1)}, f32[1,1024]{1,0:T(1,128)S(1)}, u32[]{:S(2)}, u32[]{:S(2)}) collective-permute-start(f32[1,1024]{1,0:T(1,128)S(1)} %add.49), channel_id=1, source_target_pairs={{0,2},{1,3},{2,0},{3,1},{4,6},{5,7},{6,4},{7,5},{8,10},{9,11},{10,... | collective-permute-start | bytes 12296 | tf_op jit(solution)/shard_map/ppermute | solution.py:415
  163.4 1.3 collective-permute-start.9
  164.7 3.9 %collective-permute-start.10 = (f32[64,128]{1,0:T(8,128)S(1)}, f32[64,128]{1,0:T(8,128)S(1)}, u32[]{:S(2)}, u32[]{:S(2)}) collective-permute-start(f32[64,128]{1,0:T(8,128)S(1)} %add.51), channel_id=1, source_target_pairs={{0,8},{4,12},{8,0},{12,4},{16,24},{20,28},{24,16},{28,20},{1,9},{5... | collective-permute-start | bytes 98312 | tf_op jit(solution)/shard_map/ppermute | solution.py:415
  168.6 5.0 %collective-permute-start.11 = (f32[64,128]{1,0:T(8,128)S(1)}, f32[64,128]{1,0:T(8,128)S(1)}, u32[]{:S(2)}, u32[]{:S(2)}) collective-permute-start(f32[64,128]{1,0:T(8,128)S(1)} %add.52), channel_id=1, source_target_pairs={{0,16},{4,20},{8,24},{12,28},{16,0},{20,4},{24,8},{28,12},{1,17},{... | collective-permute-start | bytes 98312 | tf_op jit(solution)/shard_map/ppermute | solution.py:415
  173.6 1.2 collective-permute-start.12
  179.7 3.7 %collective-permute-start.13 = (f32[1,1024]{1,0:T(1,128)S(1)}, f32[1,1024]{1,0:T(1,128)S(1)}, u32[]{:S(2)}, u32[]{:S(2)}) collective-permute-start(f32[1,1024]{1,0:T(1,128)S(1)} %get-tuple-element.36), channel_id=1, source_target_pairs={{0,1},{1,0},{2,3},{3,2},{4,5},{5,4},{6,7},{7,6},{8,9},{9,8},{10,11... | collective-permute-start | bytes 12296 | tf_op jit(solution)/shard_map/ppermute | solution.py:415
  183.4 3.6 %collective-permute-start.14 = (f32[1,1024]{1,0:T(1,128)S(1)}, f32[1,1024]{1,0:T(1,128)S(1)}, u32[]{:S(2)}, u32[]{:S(2)}) collective-permute-start(f32[1,1024]{1,0:T(1,128)S(1)} %add.54), channel_id=1, source_target_pairs={{0,2},{1,3},{2,0},{3,1},{4,6},{5,7},{6,4},{7,5},{8,10},{9,11},{10,... | collective-permute-start | bytes 12296 | tf_op jit(solution)/shard_map/ppermute | solution.py:415
  187.1 1.2 collective-permute-start.15
  188.3 3.7 %collective-permute-start.16 = (f32[1,2048]{1,0:T(1,128)S(1)}, f32[1,2048]{1,0:T(1,128)S(1)}, u32[]{:S(2)}, u32[]{:S(2)}) collective-permute-start(f32[1,2048]{1,0:T(1,128)S(1)} %pad_maximum_fusion.2), channel_id=1, source_target_pairs={{0,8},{4,12},{8,0},{12,4},{16,24},{20,28},{24,16},{28,20},{1,9},{5... | collective-permute-start | bytes 24584 | tf_op jit(solution)/shard_map/ppermute | solution.py:415
  192.0 4.7 %collective-permute-start.17 = (f32[1,4096]{1,0:T(1,128)S(1)}, f32[1,4096]{1,0:T(1,128)S(1)}, u32[]{:S(2)}, u32[]{:S(2)}) collective-permute-start(f32[1,4096]{1,0:T(1,128)S(1)} %pad_maximum_fusion.1), channel_id=1, source_target_pairs={{0,16},{4,20},{8,24},{12,28},{16,0},{20,4},{24,8},{28,12},{1,17},{... | collective-permute-start | bytes 49160 | tf_op jit(solution)/shard_map/ppermute | solution.py:415
Sparse Core Ops, SparseCore 0:
  9.6 84.7 all-gather.1

commit v6 on v5

--- a/solution.py
+++ b/solution.py
@@ -317,14 +317,47 @@
     )(e, in_vmem(p_own), in_vmem(x), in_vmem(held))
 
 
-def update_kernel(gain, place_ref, e_ref, v_ref, p_ref, cs_ref, *refs):
-    nums, shifts = refs[:HELD], refs[HELD : 2 * HELD]
-    out_ref, scores, acc, held, arrived = refs[2 * HELD :]
+def apply_kernel(x_ref, *refs):
+    nums, shifts, tables = refs[:HELD], refs[HELD : 2 * HELD], refs[2 * HELD : 3 * HELD]
+    out_ref, x_out = refs[3 * HELD :]
+    docs = nums[0].shape[1]
+
+    @pl.when(pl.program_id(0) == 0)
+    def _():
+        x_out[...] = x_ref[...]
+
+    part = jnp.zeros(out_ref.shape, F32)
+    for k in range(HELD):
+        weight = jnp.exp2(shifts[k][...] + x_ref[:, k * docs : (k + 1) * docs])
+        scaled = (nums[k][...].astype(F32) * weight).astype(BF16)
+        part += jnp.dot(scaled, tables[k][...], preferred_element_type=F32)
+    out_ref[...] = part
+
+
+def apply(nums, shifts, tables, x):
+    own, docs = nums[0].shape
+    width = tables[0].shape[1]
+    rows = min(UPDATE_ROWS, own)
+    return pl.pallas_call(
+        apply_kernel,
+        grid=(own // rows,),
+        in_specs=[whole()]
+        + [pl.BlockSpec((rows, docs), lambda i: (i, 0))] * HELD
+        + [whole()] * HELD
+        + [pl.BlockSpec((docs, width), lambda i: (0, 0))] * HELD,
+        out_specs=[pl.BlockSpec((rows, width), lambda i: (i, 0)), whole()],
+        out_shape=[pltpu.HBM((own, width), F32), pltpu.VMEM(x.shape, F32)],
+        compiler_params=params(),
+    )(in_vmem(x), *nums, *[in_vmem(shift) for shift in shifts], *tables)
+
+
+def update_kernel(gain, place_ref, e_ref, v_ref, p_ref, cs_ref, before_ref, *refs):
+    out_ref, scores, acc, before, arrived = refs
     step = pl.program_id(0)
-    fresh = pl.num_programs(0) - HELD
     own = p_ref.shape[0]
     size = scores.shape[1]
     places = [slice(d, d + size) for d in range(0, own, size)]
+    copy = pltpu.make_async_copy(before_ref, before, arrived)
 
     def add(place, part):
         acc[place, :] += jnp.dot(part.astype(BF16), e_ref[...], preferred_element_type=F32)
@@ -332,69 +365,54 @@
     @pl.when(step == 0)
     def _():
         acc[...] = jnp.zeros_like(acc)
-        for k in range(HELD):
-            pltpu.make_async_copy(nums[k], held.at[k], arrived.at[k]).start()
-
-    for k in range(HELD):
-
-        @pl.when(step == fresh + k)
-        def _():
-            pltpu.make_async_copy(nums[k], held.at[k], arrived.at[k]).wait()
-            weight = jnp.exp2(shifts[k][...] + v_ref[...])
-            for place in places:
-                add(place, held[k, place, :].astype(F32) * weight)
-
-    @pl.when(step < fresh)
-    def _():
-        def score(j):
-            scores[j % 2] = transposed_dot(p_ref[places[j], :], e_ref[...])
-
-        score(0)
-        for j in range(len(places)):
-            if j + 1 < len(places):
-                score(j + 1)
-            add(places[j], jnp.exp2(scores[j % 2] * gain + v_ref[...]))
+        copy.start()
+
+    def score(j):
+        scores[j % 2] = transposed_dot(p_ref[places[j], :], e_ref[...])
+
+    score(0)
+    for j in range(len(places)):
+        if j + 1 < len(places):
+            score(j + 1)
+        add(places[j], jnp.exp2(scores[j % 2] * gain + v_ref[...]))
 
     @pl.when(step == pl.num_programs(0) - 1)
     def _():
+        copy.wait()
         lane = lax.broadcasted_iota(jnp.int32, cs_ref.shape, 1)
         chunks = own // CHUNK
         for k in range(chunks):
             here = jnp.where(lane == place_ref[0] * chunks + k, cs_ref[...], 0.0)
             place = slice(k * CHUNK, (k + 1) * CHUNK)
-            summed = acc[place, :] * jnp.sum(here, axis=1, keepdims=True)
+            summed = (acc[place, :] + before[place, :]) * jnp.sum(here, axis=1, keepdims=True)
             square = jnp.mean(summed * summed, axis=1, keepdims=True)
             out_ref[place, :] = (summed * lax.rsqrt(square + 1e-06)).astype(BF16)
 
 
-def update(place, docs, e_all, v, p_own, cs, nums, shifts, gain):
+def update(place, docs, e_all, v, p_own, cs, before, gain):
     own, width = p_own.shape
     size = min(UPDATE_ROWS, own)
     ranks = e_all.shape[0] // docs
-
-    def turn(i):
-        return lax.rem(i + HELD, ranks)
 
     return pl.pallas_call(
         functools.partial(update_kernel, gain),
         grid_spec=pltpu.PrefetchScalarGridSpec(
             num_scalar_prefetch=1,
-            grid=(ranks,),
+            grid=(ranks - HELD,),
             in_specs=[
                 pl.BlockSpec(
-                    (docs, width), lambda i, place: (jnp.bitwise_xor(place[0], turn(i)), 0)
+                    (docs, width), lambda i, place: (jnp.bitwise_xor(place[0], i + HELD), 0)
                 ),
-                pl.BlockSpec((1, docs), lambda i, place: (0, turn(i))),
+                pl.BlockSpec((1, docs), lambda i, place: (0, i + HELD)),
             ]
             + [whole()] * 2
-            + [pl.BlockSpec(memory_space=pl.ANY)] * HELD
-            + [whole()] * HELD,
+            + [pl.BlockSpec(memory_space=pl.ANY)],
             out_specs=pl.BlockSpec((own, width), lambda i, place: (0, 0)),
             scratch_shapes=[
                 pltpu.VMEM((2, size, docs), F32),
                 pltpu.VMEM((own, width), F32),
-                pltpu.VMEM((HELD, own, docs), BF16),
-                pltpu.SemaphoreType.DMA((HELD,)),
+                pltpu.VMEM((own, width), F32),
+                pltpu.SemaphoreType.DMA,
             ],
         ),
         out_shape=jax.ShapeDtypeStruct((own, width), BF16),
@@ -405,8 +423,7 @@
         v,
         in_vmem(p_own),
         in_vmem(cs),
-        *[in_hbm(num) for num in nums],
-        *[in_vmem(shift) for shift in shifts],
+        in_hbm(before),
     )
 
 
@@ -428,9 +445,12 @@
     return x
 
 
-def gather_over(x, axis):
+def gather_over(x, axis, jobs={}):
     for bit in bits(axis):
-        x = jnp.concatenate([x, swap(x, axis, bit)], axis=1)
+        other = swap(x, axis, bit)
+        for job in jobs.get(bit, ()):
+            x = job(x)
+        x = jnp.concatenate([x, other], axis=1)
     return x
 
 
@@ -501,9 +521,15 @@
         row_sum = reduce_over(row_local, "protos", jnp.add)
         r = 1.0 / (total_docs * row_sum)
         weight = w * r
-    v = gather_over(jnp.log2(r * total_docs) - lse, "docs")
+
+    def apply_job(x):
+        tables = [in_hbm(embeddings), in_hbm(partner)]
+        state["part"], x = apply([in_hbm(num) for num in nums], shifts, tables, x)
+        return x
+
+    v = gather_over(jnp.log2(r * total_docs) - lse, "docs", {doc_bits[2]: [apply_job]})
     new_prototypes = update(
-        place.reshape(1), docs, e_all, v, state["own"], cs, nums, shifts, gain
+        place.reshape(1), docs, e_all, v, state["own"], cs, state["part"], gain
     )
     column_potential = jnp.log(total_docs * cs.T.reshape(-1)[:protos])
     row_potential = jnp.log(lax.optimization_barrier(r)).reshape(-1)

time: 242 us -> 247 us (1.021)
  Pallas kernels: 170 us -> 174 us
  waiting for transfers between devices: 28.6 us -> 31.2 us
    pallas_call x0 -> x1, Pallas kernels: none -> 9.07 us  [apply(): pl.pallas_call(apply_kernel, grid=(own // rows,), in_specs=[whole()] + [p...]
    pallas_call x1, Pallas kernels: 36.8 us -> 31.8 us  [update(): pl.pallas_call(functools.partial(update_kernel, gain), grid_spec=pltpu.Pr...]
    ppermute x18, waiting for transfers between devices: 27.9 us -> 30.5 us  [swap(): return lax.ppermute(x, axis, [(i, i ^ bit) for i in range(size)])]
  transfers between devices with their start and end apart: 19 -> 19, of which waited for: 16 -> 15; matrix products, arithmetic and copies ran while one was open for 1% -> 1% of each run, Pallas kernels for 56% -> 58%
where the time goes in v6:
time: 247 us; the launch traced here: 245 us
  Pallas kernels  174 us (70%)
  waiting for transfers between devices  31.2 us (13%)
  starting transfers between devices  23 us (9%)
  between operations  14.2 us (6%)
    pallas_call x1, Pallas kernels, stats(): pl.pallas_call(functools.partial(stats_kernel, gain), grid_spec=pltpu.Pre...  106 us
    pallas_call x1, Pallas kernels, update(): pl.pallas_call(functools.partial(update_kernel, gain), grid_spec=pltpu.Pr...  31.8 us
    ppermute x18, waiting for transfers between devices, swap(): return lax.ppermute(x, axis, [(i, i ^ bit) for i in range(size)])  30.5 us
    ppermute x18, starting transfers between devices, swap(): return lax.ppermute(x, axis, [(i, i ^ bit) for i in range(size)])  23 us
    pallas_call x2, Pallas kernels, columns(): pl.pallas_call(columns_kernel, in_specs=[whole()] * 2 + [pl.BlockSpec(mem...  11.2 us
    pallas_call x2, Pallas kernels, row_sums(): pl.pallas_call(functools.partial(rows_kernel, total), in_specs=[whole()]...  10.6 us
    pallas_call x1, Pallas kernels, apply(): pl.pallas_call(apply_kernel, grid=(own // rows,), in_specs=[whole()] + [p...  9.07 us
    pallas_call x1, Pallas kernels, share(): pl.pallas_call(functools.partial(share_kernel, gain), grid=(docs // DOC_T...  6.19 us
  transfers between devices with their start and end apart: 19, of which 15 were waited for; matrix products, arithmetic and copies ran while one was open for 1% of the time, Pallas kernels for 58%

profile of v6, /device:TPU:0, one launch (start us, length us, event | category | flops | bytes accessed | tf_op | source)
XLA Modules:
  0.0 245.4 jit_solution(11576889909615730452)
XLA Ops:
  7.2 0.0 all-gather.2.cloned.1.call-start
  7.2 0.7 all-gather.2.cloned.1.call-update
  7.9 0.5 collective-permute-start
  8.4 105.6 %shard_map.49 = (bf16[16384,1024]{1,0:T(8,128)(2,1)S(1)}, f32[1,1024]{1,0:T(1,128)S(1)}, f32[1,1024]{1,0:T(1,128)S(1)}, bf16[2048,512]{1,0:T(8,128)(2,1)S(1)}) custom-call(s32[1]{0:T(128)} %bitcast.place_ref, bf16[1024,512]{1,0:T(8,128)(2,1)} %refs_4_.1, bf16[16384,512]{1,0:T(8,128)(2,1)} %p_any.1, bf16[16384,512]{1,0:T(8,128)(2,1)} %p_any.1), custom_call_target="tpu_custom_call" | custom-call | tf_op jit(solution)/shard_map/pallas_call | solution.py:116
  114.1 2.6 %collective-permute-start.1 = (f32[1,1024]{1,0:T(1,128)S(1)}, f32[1,1024]{1,0:T(1,128)S(1)}, u32[]{:S(2)}, u32[]{:S(2)}) collective-permute-start(f32[1,1024]{1,0:T(1,128)S(1)} %get-tuple-element.27), channel_id=1, source_target_pairs={{0,1},{1,0},{2,3},{3,2},{4,5},{5,4},{6,7},{7,6},{8,9},{9,8},{10,11... | collective-permute-start | bytes 12296 | tf_op jit(solution)/shard_map/ppermute | solution.py:432
  116.7 1.6 collective-permute-done.1
  118.3 2.1 collective-permute-start.2
  120.4 1.6 collective-permute-done.2
  122.0 5.6 %shard_map.50 = (bf16[16384,1024]{1,0:T(8,128)(2,1)S(1)}, f32[64,128]{1,0:T(8,128)S(1)}, f32[64,128]{1,0:T(8,128)S(1)}) custom-call(bf16[16384,1024]{1,0:T(8,128)(2,1)S(1)} %get-tuple-element.25.num_ref, f32[1,1024]{1,0:T(1,128)S(1)} %get-tuple-element.47.w_ref, s32[1]{0:T(128)} %bitcast.place_ref), custom_call_target="tpu_custom_call", output_to_operand_aliasing={{0}: (0, {})} | custom-call | tf_op jit(solution)/shard_map/pallas_call | solution.py:194
  127.6 0.1 collective-permute-start.3
  127.7 1.2 collective-permute-done.3
  128.9 2.1 collective-permute-start.4
  131.0 0.0 collective-permute-done.e_ref.refs_5_
  131.0 0.0 copy-start
  131.0 1.0 copy-done
  131.9 6.2 %shard_map.51 = (bf16[2048,1024]{1,0:T(8,128)(2,1)}, f32[1,1024]{1,0:T(1,128)S(1)}, f32[64,128]{1,0:T(8,128)S(1)}, bf16[16384,1024]{1,0:T(8,128)(2,1)S(1)}) custom-call(bf16[1024,512]{1,0:T(8,128)(2,1)} %copy-done, bf16[2048,512]{1,0:T(8,128)(2,1)S(1)} %get-tuple-element.24.p_ref, f32[64,128]{1,0:T(8,128)S(1)} %add.46.x_ref, ...), custom_call_target="tpu_custom_call", output_to_operand_aliasing={{3}: (3, {})} | custom-call | tf_op jit(solution)/shard_map/pallas_call | solution.py:299
  138.1 0.0 collective-permute-done.4
  138.2 5.0 %collective-permute-start.5 = (f32[64,128]{1,0:T(8,128)S(1)}, f32[64,128]{1,0:T(8,128)S(1)}, u32[]{:S(2)}, u32[]{:S(2)}) collective-permute-start(f32[64,128]{1,0:T(8,128)S(1)} %add.47), channel_id=1, source_target_pairs={{0,16},{4,20},{8,24},{12,28},{16,0},{20,4},{24,8},{28,12},{1,17},{... | collective-permute-start | bytes 98312 | tf_op jit(solution)/shard_map/ppermute | solution.py:432
  143.1 1.9 collective-permute-done.5
  145.0 0.0 collective-permute-start.6
  145.0 1.2 collective-permute-done.6.other_ref
  146.2 5.6 %shard_map.52 = (bf16[16384,1024]{1,0:T(8,128)(2,1)S(1)}, f32[1,1024]{1,0:T(1,128)S(1)}, f32[128,128]{1,0:T(8,128)}, bf16[2048,1024]{1,0:T(8,128)(2,1)}) custom-call(bf16[16384,1024]{1,0:T(8,128)(2,1)S(1)} %get-tuple-element.31.num_ref, f32[1,1024]{1,0:T(1,128)S(1)} %get-tuple-element.47.w_ref, ...), custom_call_target="tpu_custom_call", output_to_operand_aliasing={{0}: (0, {})} | custom-call | tf_op jit(solution)/shard_map/pallas_call | solution.py:257
  151.8 0.1 collective-permute-start.7
  151.9 3.6 %collective-permute-done.7 = f32[1,1024]{1,0:T(1,128)S(1)} collective-permute-done((f32[1,1024]{1,0:T(1,128)S(1)}, f32[1,1024]{1,0:T(1,128)S(1)}, u32[]{:S(2)}, u32[]{:S(2)}) %collective-permute-start.7) | collective-permute-done | bytes 4128 | tf_op jit(solution)/shard_map/ppermute | solution.py:432
  155.5 1.7 collective-permute-start.8
  157.2 1.9 collective-permute-done.8
  159.2 5.6 %shard_map.53 = (bf16[16384,1024]{1,0:T(8,128)(2,1)S(1)}, f32[64,128]{1,0:T(8,128)S(1)}, f32[64,128]{1,0:T(8,128)S(1)}) custom-call(bf16[16384,1024]{1,0:T(8,128)(2,1)S(1)} %get-tuple-element.33.num_ref, f32[1,1024]{1,0:T(1,128)S(1)} %divide_multiply_fusion.w_ref, s32[1]{0:T(128)} %bitcast.place_ref), custom_call_target="tpu_custom_call", output_to_operand_aliasing={{0}: (0, {})} | custom-call | tf_op jit(solution)/shard_map/pallas_call | solution.py:194
  164.8 0.1 collective-permute-start.9
  164.8 1.2 collective-permute-done.9
  166.0 0.0 collective-permute-start.10
  166.0 3.9 %collective-permute-done.10 = f32[64,128]{1,0:T(8,128)S(1)} collective-permute-done((f32[64,128]{1,0:T(8,128)S(1)}, f32[64,128]{1,0:T(8,128)S(1)}, u32[]{:S(2)}, u32[]{:S(2)}) %collective-permute-start.10) | collective-permute-done | bytes 32800 | tf_op jit(solution)/shard_map/ppermute | solution.py:432
  170.0 2.9 %collective-permute-start.11 = (f32[64,128]{1,0:T(8,128)S(1)}, f32[64,128]{1,0:T(8,128)S(1)}, u32[]{:S(2)}, u32[]{:S(2)}) collective-permute-start(f32[64,128]{1,0:T(8,128)S(1)} %add.52), channel_id=1, source_target_pairs={{0,16},{4,20},{8,24},{12,28},{16,0},{20,4},{24,8},{28,12},{1,17},{... | collective-permute-start | bytes 98312 | tf_op jit(solution)/shard_map/ppermute | solution.py:432
  172.9 1.9 collective-permute-done.11
  174.8 0.0 collective-permute-start.12
  174.8 1.2 collective-permute-done.12.other_ref
  176.0 5.0 %shard_map.54 = (bf16[16384,1024]{1,0:T(8,128)(2,1)S(1)}, f32[1,1024]{1,0:T(1,128)S(1)}, f32[128,128]{1,0:T(8,128)S(1)}) custom-call(bf16[16384,1024]{1,0:T(8,128)(2,1)S(1)} %get-tuple-element.35.num_ref, f32[1,1024]{1,0:T(1,128)S(1)} %get-tuple-element.47.w_ref, f32[64,128]{1,0:T(8,128)S(1)} %add.53.mine_ref, ...), custom_call_target="tpu_custom_call", output_to_operand_aliasing={{0}: (0, {})} | custom-call | tf_op jit(solution)/shard_map/pallas_call | solution.py:257
  181.0 1.1 collective-permute-start.13
  182.0 2.6 %collective-permute-done.13 = f32[1,1024]{1,0:T(1,128)S(1)} collective-permute-done((f32[1,1024]{1,0:T(1,128)S(1)}, f32[1,1024]{1,0:T(1,128)S(1)}, u32[]{:S(2)}, u32[]{:S(2)}) %collective-permute-start.13) | collective-permute-done | bytes 4128 | tf_op jit(solution)/shard_map/ppermute | solution.py:432
  184.6 1.7 collective-permute-start.14
  186.3 1.9 collective-permute-done.14
  188.3 0.1 collective-permute-start.15
  188.4 1.2 collective-permute-done.15
  189.5 0.1 collective-permute-start.16
  189.6 3.6 %collective-permute-done.16 = f32[1,2048]{1,0:T(1,128)S(1)} collective-permute-done((f32[1,2048]{1,0:T(1,128)S(1)}, f32[1,2048]{1,0:T(1,128)S(1)}, u32[]{:S(2)}, u32[]{:S(2)}) %collective-permute-start.16) | collective-permute-done | bytes 8224 | tf_op jit(solution)/shard_map/ppermute | solution.py:432
  193.3 3.0 %collective-permute-start.17 = (f32[1,4096]{1,0:T(1,128)S(1)}, f32[1,4096]{1,0:T(1,128)S(1)}, u32[]{:S(2)}, u32[]{:S(2)}) collective-permute-start(f32[1,4096]{1,0:T(1,128)S(1)} %pad_maximum_fusion.1.x_ref), channel_id=1, source_target_pairs={{0,16},{4,20},{8,24},{12,28},{16,0},{20,4},{24,8},{28,12},{1,17},{... | collective-permute-start | bytes 49160 | tf_op jit(solution)/shard_map/ppermute | solution.py:432
  196.3 0.7 copy.10
  197.0 0.6 log.15
  197.6 9.1 %shard_map.55 = (f32[2048,512]{1,0:T(8,128)}, f32[1,4096]{1,0:T(1,128)S(1)}) custom-call(f32[1,4096]{1,0:T(1,128)S(1)} %pad_maximum_fusion.1.x_ref, bf16[2048,1024]{1,0:T(8,128)(2,1)} %get-tuple-element.39.refs_0_, bf16[2048,1024]{1,0:T(8,128)(2,1)} %get-tuple-element.40.refs_1_, f32[1,1024]{1,0:T(1,128)S(1)} %get-tuple-element.26.refs_2_, ...), custom_call_target="tpu_custom_call" | custom-call | tf_op jit(solution)/shard_map/pallas_call | solution.py:341
  206.7 0.0 collective-permute-done.17
  206.7 0.0 all-gather.2.cloned.1.call-done.e_ref
  206.7 31.8 %shard_map.56 = bf16[2048,512]{1,0:T(8,128)(2,1)} custom-call(s32[1]{0:T(128)} %bitcast.place_ref, bf16[8192,512]{1,0:T(8,128)(2,1)} %all-gather.2.cloned.1.call-done.e_ref, f32[1,8192]{1,0:T(1,128)S(1)} %pad_maximum_fusion.v_ref, bf16[2048,512]{1,0:T(8,128)(2,1)S(1)} %get-tuple-element.24.p_ref, f32[128,128]{1,0:T(8,128)S(1)} %get-tuple-element.43.cs_ref, ...), custom_call_target="tpu_custom_call" | custom-call | tf_op jit(solution)/shard_map/pallas_call | solution.py:397
  (16 shorter events, 0.2 us)
Async XLA Ops:
  7.2 199.6 %all-gather.2.cloned.1.call-start = ((), (), s32[]{:S(2)}) async-start(), calls=%async_computation | async-start | bytes 9437184 | tf_op jit(solution)/shard_map/all_gather | solution.py:483
  7.9 123.1 %collective-permute-start = (bf16[1024,512]{1,0:T(8,128)(2,1)}, bf16[1024,512]{1,0:T(8,128)(2,1)S(1)}, u32[]{:S(2)}, u32[]{:S(2)}) collective-permute-start(bf16[1024,512]{1,0:T(8,128)(2,1)} %refs_4_.1), channel_id=1, source_target_pairs={{0,4},{4,0},{8,12},{12,8},{16,20},{20,16},{24,28},{28,24},{1,5},{5... | collective-permute-start | bytes 3145736 | tf_op jit(solution)/shard_map/ppermute | solution.py:432
  114.1 4.2 %collective-permute-start.1 = (f32[1,1024]{1,0:T(1,128)S(1)}, f32[1,1024]{1,0:T(1,128)S(1)}, u32[]{:S(2)}, u32[]{:S(2)}) collective-permute-start(f32[1,1024]{1,0:T(1,128)S(1)} %get-tuple-element.27), channel_id=1, source_target_pairs={{0,1},{1,0},{2,3},{3,2},{4,5},{5,4},{6,7},{7,6},{8,9},{9,8},{10,11... | collective-permute-start | bytes 12296 | tf_op jit(solution)/shard_map/ppermute | solution.py:432
  118.3 3.7 %collective-permute-start.2 = (f32[1,1024]{1,0:T(1,128)S(1)}, f32[1,1024]{1,0:T(1,128)S(1)}, u32[]{:S(2)}, u32[]{:S(2)}) collective-permute-start(f32[1,1024]{1,0:T(1,128)S(1)} %multiply_add_fusion.1), channel_id=1, source_target_pairs={{0,2},{1,3},{2,0},{3,1},{4,6},{5,7},{6,4},{7,5},{8,10},{9,11},{10,... | collective-permute-start | bytes 12296 | tf_op jit(solution)/shard_map/ppermute | solution.py:432
  127.6 1.3 collective-permute-start.3
  128.9 9.3 %collective-permute-start.4 = (f32[64,128]{1,0:T(8,128)S(1)}, f32[64,128]{1,0:T(8,128)S(1)}, u32[]{:S(2)}, u32[]{:S(2)}) collective-permute-start(f32[64,128]{1,0:T(8,128)S(1)} %add.46.x_ref), channel_id=1, source_target_pairs={{0,8},{4,12},{8,0},{12,4},{16,24},{20,28},{24,16},{28,20},{1,9},{5... | collective-permute-start | bytes 98312 | tf_op jit(solution)/shard_map/ppermute | solution.py:432
  131.0 1.0 copy-start
  138.2 6.8 %collective-permute-start.5 = (f32[64,128]{1,0:T(8,128)S(1)}, f32[64,128]{1,0:T(8,128)S(1)}, u32[]{:S(2)}, u32[]{:S(2)}) collective-permute-start(f32[64,128]{1,0:T(8,128)S(1)} %add.47), channel_id=1, source_target_pairs={{0,16},{4,20},{8,24},{12,28},{16,0},{20,4},{24,8},{28,12},{1,17},{... | collective-permute-start | bytes 98312 | tf_op jit(solution)/shard_map/ppermute | solution.py:432
  145.0 1.2 collective-permute-start.6
  151.8 3.7 %collective-permute-start.7 = (f32[1,1024]{1,0:T(1,128)S(1)}, f32[1,1024]{1,0:T(1,128)S(1)}, u32[]{:S(2)}, u32[]{:S(2)}) collective-permute-start(f32[1,1024]{1,0:T(1,128)S(1)} %get-tuple-element.34), channel_id=1, source_target_pairs={{0,1},{1,0},{2,3},{3,2},{4,5},{5,4},{6,7},{7,6},{8,9},{9,8},{10,11... | collective-permute-start | bytes 12296 | tf_op jit(solution)/shard_map/ppermute | solution.py:432
  155.5 3.6 %collective-permute-start.8 = (f32[1,1024]{1,0:T(1,128)S(1)}, f32[1,1024]{1,0:T(1,128)S(1)}, u32[]{:S(2)}, u32[]{:S(2)}) collective-permute-start(f32[1,1024]{1,0:T(1,128)S(1)} %add.49), channel_id=1, source_target_pairs={{0,2},{1,3},{2,0},{3,1},{4,6},{5,7},{6,4},{7,5},{8,10},{9,11},{10,... | collective-permute-start | bytes 12296 | tf_op jit(solution)/shard_map/ppermute | solution.py:432
  164.8 1.3 collective-permute-start.9
  166.0 3.9 %collective-permute-start.10 = (f32[64,128]{1,0:T(8,128)S(1)}, f32[64,128]{1,0:T(8,128)S(1)}, u32[]{:S(2)}, u32[]{:S(2)}) collective-permute-start(f32[64,128]{1,0:T(8,128)S(1)} %add.51), channel_id=1, source_target_pairs={{0,8},{4,12},{8,0},{12,4},{16,24},{20,28},{24,16},{28,20},{1,9},{5... | collective-permute-start | bytes 98312 | tf_op jit(solution)/shard_map/ppermute | solution.py:432
  170.0 4.8 %collective-permute-start.11 = (f32[64,128]{1,0:T(8,128)S(1)}, f32[64,128]{1,0:T(8,128)S(1)}, u32[]{:S(2)}, u32[]{:S(2)}) collective-permute-start(f32[64,128]{1,0:T(8,128)S(1)} %add.52), channel_id=1, source_target_pairs={{0,16},{4,20},{8,24},{12,28},{16,0},{20,4},{24,8},{28,12},{1,17},{... | collective-permute-start | bytes 98312 | tf_op jit(solution)/shard_map/ppermute | solution.py:432
  174.8 1.2 collective-permute-start.12
  181.0 3.7 %collective-permute-start.13 = (f32[1,1024]{1,0:T(1,128)S(1)}, f32[1,1024]{1,0:T(1,128)S(1)}, u32[]{:S(2)}, u32[]{:S(2)}) collective-permute-start(f32[1,1024]{1,0:T(1,128)S(1)} %get-tuple-element.38), channel_id=1, source_target_pairs={{0,1},{1,0},{2,3},{3,2},{4,5},{5,4},{6,7},{7,6},{8,9},{9,8},{10,11... | collective-permute-start | bytes 12296 | tf_op jit(solution)/shard_map/ppermute | solution.py:432
  184.6 3.6 %collective-permute-start.14 = (f32[1,1024]{1,0:T(1,128)S(1)}, f32[1,1024]{1,0:T(1,128)S(1)}, u32[]{:S(2)}, u32[]{:S(2)}) collective-permute-start(f32[1,1024]{1,0:T(1,128)S(1)} %add.54), channel_id=1, source_target_pairs={{0,2},{1,3},{2,0},{3,1},{4,6},{5,7},{6,4},{7,5},{8,10},{9,11},{10,... | collective-permute-start | bytes 12296 | tf_op jit(solution)/shard_map/ppermute | solution.py:432
  188.3 1.2 collective-permute-start.15
  189.5 3.7 %collective-permute-start.16 = (f32[1,2048]{1,0:T(1,128)S(1)}, f32[1,2048]{1,0:T(1,128)S(1)}, u32[]{:S(2)}, u32[]{:S(2)}) collective-permute-start(f32[1,2048]{1,0:T(1,128)S(1)} %pad_maximum_fusion.2), channel_id=1, source_target_pairs={{0,8},{4,12},{8,0},{12,4},{16,24},{20,28},{24,16},{28,20},{1,9},{5... | collective-permute-start | bytes 24584 | tf_op jit(solution)/shard_map/ppermute | solution.py:432
  193.3 13.4 %collective-permute-start.17 = (f32[1,4096]{1,0:T(1,128)S(1)}, f32[1,4096]{1,0:T(1,128)S(1)}, u32[]{:S(2)}, u32[]{:S(2)}) collective-permute-start(f32[1,4096]{1,0:T(1,128)S(1)} %pad_maximum_fusion.1.x_ref), channel_id=1, source_target_pairs={{0,16},{4,20},{8,24},{12,28},{16,0},{20,4},{24,8},{28,12},{1,17},{... | collective-permute-start | bytes 49160 | tf_op jit(solution)/shard_map/ppermute | solution.py:432
Sparse Core Ops, SparseCore 0:
  9.6 84.7 all-gather.1
